TPU v7x, 32 devices: a whole 2x2x4 slice. The times are simulated.
32 devices in a mesh: dp: 8 (over y, x, core), seq: 4 (over z).
Axes of the slice: x: 2, y: 2, z: 4, core: 2. Of those that a mesh axis runs over, the one named last changes fastest.
Arguments:
- inputs: bfloat16 [8, 1024, 2048], P('dp', 'seq'), may hold values from -6 to 6
- cotangent: bfloat16 [8, 1024, 2048], P('dp', 'seq'), may hold values from -6 to 6
- attn_params: float32 [2048, 8192], P(('dp', 'seq'))
- attn_first: float32 [2048, 8192], P(('dp', 'seq'))
- attn_second: float32 [2048, 8192], P(('dp', 'seq')), as said below
- mlp_params: float32 [2048, 16384], P(('dp', 'seq'))
- mlp_first: float32 [2048, 16384], P(('dp', 'seq'))
- mlp_second: float32 [2048, 16384], P(('dp', 'seq')), as said below
- small: float32 [2048, 13], P(('dp', 'seq'))
- small_first: float32 [2048, 13], P(('dp', 'seq'))
- small_second: float32 [2048, 13], P(('dp', 'seq')), as said below
Outputs:
- outputs: bfloat16 [8, 1024, 2048], P('dp', 'seq')
- input_grad: float32 [8, 1024, 2048], P('dp', 'seq')
- attn_grad: float32 [2048, 8192], P(('dp', 'seq'))
- attn_new: float32 [2048, 8192], P(('dp', 'seq'))
- attn_first_new: float32 [2048, 8192], P(('dp', 'seq'))
- attn_second_new: float32 [2048, 8192], P(('dp', 'seq'))
- mlp_grad: float32 [2048, 16384], P(('dp', 'seq'))
- mlp_new: float32 [2048, 16384], P(('dp', 'seq'))
- mlp_first_new: float32 [2048, 16384], P(('dp', 'seq'))
- mlp_second_new: float32 [2048, 16384], P(('dp', 'seq'))
- small_grad: float32 [2048, 13], P(('dp', 'seq'))
- small_new: float32 [2048, 13], P(('dp', 'seq'))
- small_first_new: float32 [2048, 13], P(('dp', 'seq'))
- small_second_new: float32 [2048, 13], P(('dp', 'seq'))
Inputs may be any that keep to these rules, and one draw needn't show every extreme that they name: `attn_second`: positive. `mlp_second`: positive. `small_second`: positive.
All inputs are finite; a program needn't handle non-finite values.
Results may differ from a plain program's by a relative error of at most 0.012.
Values may be sent and summed in bfloat16 or wider, within the bound.
No kernel may reach another device: no remote copies, remote signals or barrier semaphores. Data moves between devices by JAX's collectives and lax.ppermute only.
A program may use at most 896 MiB of HBM per device.

v0:
```python
from functools import partial

import jax
import jax.numpy as jnp
from jax import lax
from jax.sharding import PartitionSpec as P

HEADS = 8
STEP = 10


norm_eps = 1e-05
masked_value = -1e30
beta_first = 0.9
beta_second = 0.95
adam_eps = 1e-08
decay_rate = 0.01
rate_attention = 0.06
rate_mlp = 0.02
rate_vector = 0.2


def normalize(values):
    row_mean = jnp.mean(values, axis=-1, keepdims=True)
    centred = values - row_mean
    spread = jnp.mean(centred * centred, axis=-1, keepdims=True)
    scaling = lax.rsqrt(spread + norm_eps)
    return (centred * scaling, scaling)


def rotary_tables(positions, rot_dims):
    frequency = 10000.0 ** (-(jnp.arange(rot_dims // 2, dtype=jnp.float32) * 2.0) / rot_dims)
    angles = positions.astype(jnp.float32)[:, None] * frequency[None, :]
    angles = jnp.concatenate([angles, angles], axis=-1)
    return (jnp.cos(angles)[:, None, :], jnp.sin(angles)[:, None, :])


def rotate(values, cosine, sine, rot_dims):
    rotated_part = values[..., :rot_dims]
    first_half = rotated_part[..., : rot_dims // 2]
    second_half = rotated_part[..., rot_dims // 2 :]
    turned = jnp.concatenate([-second_half, first_half], axis=-1)
    return jnp.concatenate([rotated_part * cosine + turned * sine, values[..., rot_dims:]], axis=-1)


def contract(left_op, right_op, left_dim, right_dim):
    return lax.dot_general(
        left_op,
        right_op,
        (((left_dim,), (right_dim,)), ((), ())),
        preferred_element_type=jnp.float32,
    )


def adamw(master, gradient, first_old, second_old, step_rate):
    first_new = beta_first * first_old + (1.0 - beta_first) * gradient
    second_new = beta_second * second_old + (1.0 - beta_second) * gradient * gradient
    first_hat = first_new / (1.0 - beta_first**STEP)
    second_hat = second_new / (1.0 - beta_second**STEP)
    updated = master - step_rate * (
        first_hat / (jnp.sqrt(second_hat) + adam_eps) + decay_rate * master
    )
    return (gradient, updated, first_new, second_new)


def body(
    inputs,
    cotangent,
    attn_params,
    attn_first,
    attn_second,
    mlp_params,
    mlp_first,
    mlp_second,
    small,
    small_first,
    small_second,
):
    seq_count, span_len, model_width = inputs.shape
    token_count = seq_count * span_len
    ff_units = mlp_params.shape[1] // 2
    head_size = model_width // HEADS
    rot_dims = head_size // 4
    score_scale = head_size ** (-0.5)
    attn_low = attn_params.astype(jnp.bfloat16)
    mlp_low = mlp_params.astype(jnp.bfloat16)
    small_low = small.astype(jnp.bfloat16)
    attn_all, mlp_all, small_all = (
        lax.all_gather(attn_low, ("dp", "seq"), axis=0, tiled=True),
        lax.all_gather(mlp_low, ("dp", "seq"), axis=0, tiled=True),
        lax.all_gather(small_low, ("dp", "seq"), axis=0, tiled=True),
    )
    vectors = small_all.astype(jnp.float32)
    qkv_bias = vectors[:, 6:9].T.reshape(-1)
    up_bias = vectors[:, 9:13].T.reshape(-1)
    tokens = inputs.astype(jnp.float32).reshape(token_count, model_width)
    normed, scaling = normalize(tokens)
    attn_in = (normed * vectors[:, 0] + vectors[:, 1]).astype(jnp.bfloat16)
    mlp_in = (normed * vectors[:, 2] + vectors[:, 3]).astype(jnp.bfloat16)
    projected = (
        jnp.dot(attn_in, attn_all[:, : 3 * model_width], preferred_element_type=jnp.float32)
        + qkv_bias
    )
    shaped = projected.reshape(seq_count, span_len, 3, HEADS, head_size)
    positions = lax.axis_index("seq") * span_len + jnp.arange(span_len, dtype=jnp.int32)
    cosine, sine = rotary_tables(positions, rot_dims)
    queries = rotate(shaped[:, :, 0], cosine, sine, rot_dims).astype(jnp.bfloat16)
    keys_own = rotate(shaped[:, :, 1], cosine, sine, rot_dims).astype(jnp.bfloat16)
    values_own = shaped[:, :, 2].astype(jnp.bfloat16)
    keys_flat, values_flat = (
        lax.all_gather(
            keys_own.reshape(seq_count, span_len, model_width), "seq", axis=1, tiled=True
        ),
        lax.all_gather(
            values_own.reshape(seq_count, span_len, model_width), "seq", axis=1, tiled=True
        ),
    )
    seq_length = keys_flat.shape[1]
    keys_all = keys_flat.reshape(seq_count, seq_length, HEADS, head_size)
    values_all = values_flat.reshape(seq_count, seq_length, HEADS, head_size)
    causal = jnp.arange(seq_length, dtype=jnp.int32)[None, :] <= positions[:, None]

    def masked_scores():
        raw = (
            jnp.einsum("sqhd,skhd->shqk", queries, keys_all, preferred_element_type=jnp.float32)
            * score_scale
        )
        return jnp.where(causal[None, None], raw, masked_value)

    scores = masked_scores()
    row_max = jnp.max(scores, axis=-1, keepdims=True)
    exp_terms = jnp.exp(scores - row_max)
    row_sum = jnp.sum(exp_terms, axis=-1, keepdims=True)
    log_total = row_max + jnp.log(row_sum)
    probs = (exp_terms / row_sum).astype(jnp.bfloat16)
    mixed = jnp.einsum("shqk,skhd->sqhd", probs, values_all, preferred_element_type=jnp.float32)
    mixed_low = mixed.reshape(token_count, model_width).astype(jnp.bfloat16)
    attn_out = (
        jnp.dot(mixed_low, attn_all[:, 3 * model_width :], preferred_element_type=jnp.float32)
        + vectors[:, 4]
    )
    gate_pre = jnp.dot(mlp_in, mlp_all[:, :ff_units], preferred_element_type=jnp.float32) + up_bias
    activated = jax.nn.gelu(gate_pre, approximate=False).astype(jnp.bfloat16)
    mlp_out = contract(activated, mlp_all[:, ff_units:], 1, 1) + vectors[:, 5]
    outputs = (
        (tokens + attn_out + mlp_out).astype(jnp.bfloat16).reshape(seq_count, span_len, model_width)
    )
    attn_back, mlp_back, small_back = (
        lax.all_gather(attn_low, ("dp", "seq"), axis=0, tiled=True),
        lax.all_gather(mlp_low, ("dp", "seq"), axis=0, tiled=True),
        lax.all_gather(small_low, ("dp", "seq"), axis=0, tiled=True),
    )
    vectors_back = small_back.astype(jnp.float32)
    upstream = cotangent.reshape(token_count, model_width)
    upstream_wide = upstream.astype(jnp.float32)
    hidden_grad = jnp.dot(upstream, mlp_back[:, ff_units:], preferred_element_type=jnp.float32)
    gelu_value, gelu_pull = jax.vjp(partial(jax.nn.gelu, approximate=False), gate_pre)
    gate_grad = gelu_pull(hidden_grad)[0].astype(jnp.bfloat16)
    mlp_in_grad = contract(gate_grad, mlp_back[:, :ff_units], 1, 1)
    mlp_grad = lax.psum_scatter(
        jnp.concatenate(
            [contract(mlp_in, gate_grad, 0, 0), contract(upstream, activated, 0, 0)], axis=1
        ),
        ("dp", "seq"),
        scatter_dimension=0,
        tiled=True,
    )
    mixed_grad = contract(upstream, attn_back[:, 3 * model_width :], 1, 1).astype(jnp.bfloat16)
    mixed_grad = mixed_grad.reshape(seq_count, span_len, HEADS, head_size)
    probs_back = jnp.exp(masked_scores() - log_total)
    probs_grad = jnp.einsum(
        "sqhd,skhd->shqk", mixed_grad, values_all, preferred_element_type=jnp.float32
    )
    row_dot = jnp.sum(probs_back * probs_grad, axis=-1, keepdims=True)
    score_grad = (probs_back * (probs_grad - row_dot)).astype(jnp.bfloat16)
    query_grad = (
        jnp.einsum("shqk,skhd->sqhd", score_grad, keys_all, preferred_element_type=jnp.float32)
        * score_scale
    )
    key_terms = (
        jnp.einsum("shqk,sqhd->skhd", score_grad, queries, preferred_element_type=jnp.float32)
        * score_scale
    )
    value_terms = jnp.einsum(
        "shqk,sqhd->skhd",
        probs_back.astype(jnp.bfloat16),
        mixed_grad,
        preferred_element_type=jnp.float32,
    )
    key_grad, value_grad = (
        lax.psum_scatter(
            key_terms.reshape(seq_count, seq_length, model_width),
            "seq",
            scatter_dimension=1,
            tiled=True,
        ),
        lax.psum_scatter(
            value_terms.reshape(seq_count, seq_length, model_width),
            "seq",
            scatter_dimension=1,
            tiled=True,
        ),
    )
    query_pre = rotate(query_grad, cosine, -sine, rot_dims)
    key_pre = rotate(
        key_grad.reshape(seq_count, span_len, HEADS, head_size), cosine, -sine, rot_dims
    )
    value_pre = value_grad.reshape(seq_count, span_len, HEADS, head_size)
    projected_grad = (
        jnp.stack([query_pre, key_pre, value_pre], axis=2)
        .reshape(token_count, 3 * model_width)
        .astype(jnp.bfloat16)
    )
    attn_in_grad = contract(projected_grad, attn_back[:, : 3 * model_width], 1, 1)
    normed_grad = attn_in_grad * vectors_back[:, 0] + mlp_in_grad * vectors_back[:, 2]
    grad_mean = jnp.mean(normed_grad, axis=-1, keepdims=True)
    grad_proj = jnp.mean(normed_grad * normed, axis=-1, keepdims=True)
    input_grad = upstream_wide + scaling * (normed_grad - grad_mean - normed * grad_proj)
    input_grad = input_grad.reshape(seq_count, span_len, model_width)
    upstream_sum = jnp.sum(upstream_wide, axis=0)
    norm_columns = jnp.stack(
        [
            jnp.sum(attn_in_grad * normed, axis=0),
            jnp.sum(attn_in_grad, axis=0),
            jnp.sum(mlp_in_grad * normed, axis=0),
            jnp.sum(mlp_in_grad, axis=0),
            upstream_sum,
            upstream_sum,
        ],
        axis=1,
    )
    qkv_columns = jnp.sum(projected_grad.astype(jnp.float32), axis=0).reshape(3, model_width).T
    up_columns = (
        jnp.sum(gate_grad.astype(jnp.float32), axis=0)
        .reshape(ff_units // model_width, model_width)
        .T
    )
    small_term = jnp.concatenate([norm_columns, qkv_columns, up_columns], axis=1)
    attn_term = jnp.concatenate(
        [contract(attn_in, projected_grad, 0, 0), contract(mixed_low, upstream, 0, 0)], axis=1
    )
    attn_grad, small_grad = (
        lax.psum_scatter(attn_term, ("dp", "seq"), scatter_dimension=0, tiled=True),
        lax.psum_scatter(small_term, ("dp", "seq"), scatter_dimension=0, tiled=True),
    )
    attn_result = adamw(attn_params, attn_grad, attn_first, attn_second, rate_attention)
    mlp_result = adamw(mlp_params, mlp_grad, mlp_first, mlp_second, rate_mlp)
    small_result = adamw(small, small_grad, small_first, small_second, rate_vector)
    return (
        outputs,
        input_grad,
        attn_result[0],
        attn_result[1],
        attn_result[2],
        attn_result[3],
        mlp_result[0],
        mlp_result[1],
        mlp_result[2],
        mlp_result[3],
        small_result[0],
        small_result[1],
        small_result[2],
        small_result[3],
    )


def solution(mesh):
    placed = (
        P("dp", "seq", None),
        P("dp", "seq", None),
        P(("dp", "seq"), None),
        P(("dp", "seq"), None),
        P(("dp", "seq"), None),
        P(("dp", "seq"), None),
        P(("dp", "seq"), None),
        P(("dp", "seq"), None),
        P(("dp", "seq"), None),
        P(("dp", "seq"), None),
        P(("dp", "seq"), None),
    )
    return jax.shard_map(
        body,
        mesh=mesh,
        in_specs=placed,
        out_specs=(
            P("dp", "seq", None),
            P("dp", "seq", None),
            P(("dp", "seq"), None),
            P(("dp", "seq"), None),
            P(("dp", "seq"), None),
            P(("dp", "seq"), None),
            P(("dp", "seq"), None),
            P(("dp", "seq"), None),
            P(("dp", "seq"), None),
            P(("dp", "seq"), None),
            P(("dp", "seq"), None),
            P(("dp", "seq"), None),
            P(("dp", "seq"), None),
            P(("dp", "seq"), None),
        ),
        check_vma=False,
    )
```

profile of v0, /device:TPU:5, one launch (start us, length us, event | category | flops | bytes accessed | tf_op | source)
XLA Modules:
  0.0 5497.8 jit_solution(3993568660808250794)
XLA Ops:
  10.7 65.9 %all-gather = bf16[32,64,13]{1,2,0:T(8,128)(2,1)S(1)} all-gather(bf16[1,64,13]{1,2,0:T(8,128)(2,1)S(1)} %convert_bitcast_fusion.1), channel_id=1, replica_groups=mesh['dp'=8,'seq'=4] {'dp','seq'}, dimensions={0}, use_global_device_ids=true | all-gather | bytes 54912 | tf_op jit(solution)/shard_map/all_gather | solution.py:91
  81.9 127.4 %all-gather.6.cloned.1.call-done = bf16[2048,8192]{1,0:T(8,128)(2,1)} async-done(((bf16[64,8192]{1,0:T(8,128)(2,1)}), bf16[2048,8192]{1,0:T(8,128)(2,1)}) %all-gather.6.cloned.1.call-update) | async-done | bytes 33554448 | tf_op jit(solution)/shard_map/all_gather | solution.py:89
  209.3 12.1 fusion.23
  249.1 62.5 %all-gather.10.cloned.1.call-done = bf16[1,1024,2048]{1,2,0:T(8,128)(2,1)} async-done(((bf16[1,256,2048]{1,2,0:T(8,128)(2,1)}), bf16[1,1024,2048]{1,2,0:T(8,128)(2,1)}) %all-gather.10.cloned.1.call-update) | async-done | bytes 4194320 | tf_op jit(solution)/shard_map/all_gather | solution.py:111
  321.7 70.9 %all-gather.8.cloned.1.call-done = bf16[1,1024,2048]{1,2,0:T(8,128)(2,1)} async-done(((bf16[1,256,2048]{1,2,0:T(8,128)(2,1)}), bf16[1,1024,2048]{1,2,0:T(8,128)(2,1)}) %all-gather.8.cloned.1.call-update) | async-done | bytes 4194320 | tf_op jit(solution)/shard_map/all_gather | solution.py:114
  408.5 8.1 fusion.33
  420.3 12.1 reduce-scatter.17.cloned.1.call-start
  446.5 8.1 fusion.96
  454.6 96.2 %reduce-scatter.11.cloned.1.call-done = f32[1,256,2048]{1,2,0:T(8,128)} async-done(((f32[1,1024,2048]{1,2,0:T(8,128)}), f32[1,256,2048]{1,2,0:T(8,128)}) %reduce-scatter.11.cloned.1.call-update) | async-done | bytes 2097168 | tf_op jit(solution)/shard_map/reduce_scatter | solution.py:191
  554.3 144.0 %reduce-scatter.13.cloned.1.call-done = f32[1,256,2048]{1,2,0:T(8,128)} async-done(((f32[1,1024,2048]{1,2,0:T(8,128)}), f32[1,256,2048]{1,2,0:T(8,128)}) %reduce-scatter.13.cloned.1.call-update) | async-done | bytes 2097168 | tf_op jit(solution)/shard_map/reduce_scatter | solution.py:197
  721.9 13.7 fusion.8
  735.7 21.6 fusion.86
  757.3 302.0 %all-gather.12.cloned.1.call-done = bf16[2048,16384]{1,0:T(8,128)(2,1)} async-done(((bf16[64,16384]{1,0:T(8,128)(2,1)}), bf16[2048,16384]{1,0:T(8,128)(2,1)}) %all-gather.12.cloned.1.call-update) | async-done | bytes 67108880 | tf_op jit(solution)/shard_map/all_gather | solution.py:90
  1059.3 17.6 fusion.12
  1076.9 32.9 convert_reduce_fusion
  1109.8 16.3 fusion.119
  1130.2 43.5 pad_maximum_fusion.1
  1174.4 25.5 fusion.116
  1199.9 31.5 convolution_bitcast_fusion
  1231.4 86.6 %pad_maximum_fusion = f32[2048,16384]{1,0:T(8,128)} fusion(f32[2048,8192]{1,0:T(8,128)} %convolution_bitcast_fusion, f32[2048,8192]{1,0:T(8,128)} %fusion.116), kind=kLoop, calls=%fused_computation | loop fusion | flops 33554432 | bytes 268435456 | tf_op jit(solution)/shard_map/concatenate | solution.py:161
  1325.5 31.2 fusion.64
  1358.2 1314.5 %reduce-scatter.15.cloned.1.call-done = f32[64,8192]{1,0:T(8,128)} async-done(((f32[2048,8192]{1,0:T(8,128)}), f32[64,8192]{1,0:T(8,128)}) %reduce-scatter.15.cloned.1.call-update) | async-done | bytes 2097168 | tf_op jit(solution)/shard_map/reduce_scatter | solution.py:243
  2679.3 2800.3 %reduce-scatter.19.cloned.1.call-done = f32[64,16384]{1,0:T(8,128)} async-done(((f32[2048,16384]{1,0:T(8,128)}), f32[64,16384]{1,0:T(8,128)}) %reduce-scatter.19.cloned.1.call-update) | async-done | bytes 4194320
  5479.6 11.4 multiply_subtract_fusion
  (157 shorter events, 127.4 us)
Async XLA Ops:
  7.2 202.1 %all-gather.6.cloned.1.call-start = ((), (), s32[]{:S(2)}) async-start(), calls=%async_computation.5 | async-start | bytes 34603008 | tf_op jit(solution)/shard_map/all_gather | solution.py:89
  9.9 301.7 %all-gather.10.cloned.1.call-start = ((), (), s32[]{:S(2)}) async-start(), calls=%async_computation.7 | async-start | bytes 5242880 | tf_op jit(solution)/shard_map/all_gather | solution.py:111
  79.6 141.8 %copy-start.22 = (f32[256]{0:T(256)}, f32[256]{0:T(256)S(1)}, u32[]{:S(2)}) copy-start(f32[256]{0:T(256)S(1)} %broadcast_multiply_fusion.4) | copy-start | bytes 3076
  81.3 140.1 %copy-start.24 = (f32[256]{0:T(256)}, f32[256]{0:T(256)S(1)}, u32[]{:S(2)}) copy-start(f32[256]{0:T(256)S(1)} %add_rsqrt_fusion) | copy-start | bytes 3076
  81.9 139.5 %copy-start.18 = (f32[2048,1]{0,1:T(1,128)}, f32[2048,1]{0,1:T(1,128)S(1)}, u32[]{:S(2)}) copy-start(f32[2048,1]{0,1:T(1,128)S(1)} %get-tuple-element.61) | copy-start | bytes 24580
  81.9 139.5 %copy-start.20 = (f32[2048,1]{0,1:T(1,128)}, f32[2048,1]{0,1:T(1,128)S(1)}, u32[]{:S(2)}) copy-start(f32[2048,1]{0,1:T(1,128)S(1)} %get-tuple-element.60) | copy-start | bytes 24580
  81.9 977.4 %copy-start.16 = (f32[2048,1]{0,1:T(1,128)}, f32[2048,1]{0,1:T(1,128)S(1)}, u32[]{:S(2)}) copy-start(f32[2048,1]{0,1:T(1,128)S(1)} %get-tuple-element.58) | copy-start | bytes 24580
  233.0 159.6 %all-gather.8.cloned.1.call-start = ((), (), s32[]{:S(2)}) async-start(), calls=%async_computation.6 | async-start | bytes 5242880 | tf_op jit(solution)/shard_map/all_gather | solution.py:114
  238.1 312.7 %reduce-scatter.11.cloned.1.call-start = ((), (), s32[]{:S(2)}) async-start(), calls=%async_computation.9 | async-start | bytes 10485760 | tf_op jit(solution)/shard_map/reduce_scatter | solution.py:191
  408.4 289.9 %reduce-scatter.13.cloned.1.call-start = ((), (), s32[]{:S(2)}) async-start(), calls=%async_computation.10 | async-start | bytes 10485760 | tf_op jit(solution)/shard_map/reduce_scatter | solution.py:197
  416.5 642.8 %all-gather.12.cloned.1.call-start = ((), (), s32[]{:S(2)}) async-start(), calls=%async_computation.8 | async-start | bytes 69206016 | tf_op jit(solution)/shard_map/all_gather | solution.py:90
  420.3 936.4 %reduce-scatter.17.cloned.1.call-start = ((), (), s32[]{:S(2)}) async-start(), calls=%async_computation.12 | async-start | bytes 1081344
  721.9 13.8 copy-start.23
  721.9 13.8 copy-start.25
  735.7 323.6 %copy-start.29 = (f32[1,16,4,128]{3,1,2,0:T(8,128)S(1)}, f32[1,16,4,128]{3,1,2,0:T(8,128)}, u32[]{:S(2)}) copy-start(f32[1,16,4,128]{3,1,2,0:T(8,128)} %copy.110) | copy-start | bytes 98308
  1059.3 17.6 copy-start.10
  1109.8 18.6 copy-start.26
  1130.2 1542.5 %reduce-scatter.15.cloned.1.call-start = ((), (), s32[]{:S(2)}) async-start(), calls=%async_computation.11 | async-start | bytes 69206016 | tf_op jit(solution)/shard_map/reduce_scatter | solution.py:243
  1173.7 4305.9 %reduce-scatter.19.cloned.1.call-start = ((), (), s32[]{:S(2)}) async-start(), calls=%async_computation.13 | async-start | bytes 138412032
  1325.5 32.0 copy-start.28
  1325.5 32.0 copy-start.30
  1325.5 32.0 copy-start.31
  1325.5 1347.2 %copy-start.6 = (f32[64,8192]{1,0:T(8,128)S(1)}, f32[64,8192]{1,0:T(8,128)}, u32[]{:S(2)}) copy-start(f32[64,8192]{1,0:T(8,128)} %param.13) | copy-start | bytes 6291460
  1357.6 4133.4 %copy-start.27 = (f32[64,13]{0,1:T(8,128)}, f32[64,13]{0,1:T(8,128)S(1)}, u32[]{:S(2)}) copy-start(f32[64,13]{0,1:T(8,128)S(1)} %copy.101) | copy-start | bytes 9988
  (20 other events, 120.5 us)
Sparse Core Ops, SparseCore 0:
  11.5 197.7 all-gather.5
  233.1 78.5 all-gather.9
  313.8 78.7 all-gather.7
  408.5 142.2 reduce-scatter.10
  553.0 145.1 reduce-scatter.12
  701.7 357.5 all-gather.11
  1130.3 128.0 reduce-scatter.16
  1261.5 1411.1 reduce-scatter.14
  2675.8 2803.7 reduce-scatter.18
where the time goes:
time: 5510 us; the launch traced here: 5500 us
  waiting for transfers between devices  4920 us (89%)
  matrix products  258 us (5%)
  other arithmetic  182 us (3%)
  blocking collectives  65.9 us (1%)
    unnamed x11, waiting for transfers between devices  2800 us
    reduce_scatter x1, waiting for transfers between devices, body(): lax.psum_scatter(attn_term, ('dp', 'seq'), scatter_dimension=0, tiled=True)  1310 us
    all_gather x1, waiting for transfers between devices, body(): lax.all_gather(mlp_low, ('dp', 'seq'), axis=0, tiled=True)  302 us
    dot_general x8, matrix products, contract(): lax.dot_general(left_op, right_op, (((left_dim,), (right_dim,)), ((), ())...  155 us
    reduce_scatter x1, waiting for transfers between devices, body(): lax.psum_scatter(value_terms.reshape(seq_count, seq_length, model_width),...  144 us
    all_gather x1, waiting for transfers between devices, body(): lax.all_gather(attn_low, ('dp', 'seq'), axis=0, tiled=True)  127 us
  transfers between devices with their start and end apart: 9, of which 8 were waited for; matrix products, arithmetic and copies ran while one was open for 6% of the time, Pallas kernels for 0%

commit v1 on v0

v1 whole, which is shorter than its diff:
```python
from functools import partial

import jax
import jax.numpy as jnp
from jax import lax
from jax.experimental import pallas as pl
from jax.experimental.pallas import tpu as pltpu
from jax.sharding import PartitionSpec as P

HEADS = 8
STEP = 10
AXES = ("dp", "seq")
LANES = 128
VMEM_LIMIT = 56 * 2**20

norm_eps = 1e-05
masked_value = -1e30
beta_first = 0.9
beta_second = 0.95
adam_eps = 1e-08
decay_rate = 0.01
rate_attention = 0.06
rate_mlp = 0.02
rate_vector = 0.2

f32 = jnp.float32
bf16 = jnp.bfloat16


def normalize(values):
    row_mean = jnp.mean(values, axis=-1, keepdims=True)
    centred = values - row_mean
    spread = jnp.mean(centred * centred, axis=-1, keepdims=True)
    scaling = lax.rsqrt(spread + norm_eps)
    return (centred * scaling, scaling)


def dot(left_op, right_op, left_dim=1, right_dim=0):
    return lax.dot_general(
        left_op,
        right_op,
        (((left_dim,), (right_dim,)), ((), ())),
        preferred_element_type=f32,
    )


def adamw(master, gradient, first_old, second_old, step_rate):
    first_new = beta_first * first_old + (1.0 - beta_first) * gradient
    second_new = beta_second * second_old + (1.0 - beta_second) * gradient * gradient
    first_hat = first_new / (1.0 - beta_first**STEP)
    second_hat = second_new / (1.0 - beta_second**STEP)
    updated = master - step_rate * (
        first_hat / (jnp.sqrt(second_hat) + adam_eps) + decay_rate * master
    )
    return (gradient, updated, first_new, second_new)


def params(cost=None, **kw):
    return dict(
        compiler_params=pltpu.CompilerParams(vmem_limit_bytes=VMEM_LIMIT, **kw),
        cost_estimate=cost and pl.CostEstimate(flops=cost[0], bytes_accessed=cost[1], transcendentals=0),
    )


class Layout:
    def __init__(self, nd, nz):
        self.nd, self.nz = nd, nz
        self.pair = HEADS // nz
        self.groups = nd // self.pair
        self.dp = lax.axis_index("dp")
        self.z = lax.axis_index("seq")
        self.g = self.dp // self.pair
        self.c = self.dp % self.pair
        self.t = self.z * self.pair + self.c

    def perm(self, target):
        pairs = []
        for dp in range(self.nd):
            for z in range(self.nz):
                goal = target(dp // self.pair, dp % self.pair, z)
                if goal is not None:
                    g, c, s = goal
                    pairs.append((dp * self.nz + z, (g * self.pair + c) * self.nz + s))
        return pairs

    def hop(self, value, target):
        return lax.ppermute(value, AXES, self.perm(target))

    def group_hop(self, value, bit):
        return self.hop(value, lambda g, c, z: (g ^ bit, c, z))

    def core_hop(self, value, r):
        return self.hop(value, lambda g, c, z: (g, c ^ r, z))

    def ring(self, value):
        return self.hop(value, lambda g, c, z: (g, c, (z + 1) % self.nz))

    def flat_hop(self, value, bit):
        return lax.ppermute(value, AXES, [(i, i ^ bit) for i in range(self.nd * self.nz)])

    def head_owner_perm(self):
        pairs = []
        for r in range(self.nd * self.nz):
            head, quarter = r // self.groups, r % self.groups
            s, c = head // self.pair, head % self.pair
            pairs.append((r, (quarter * self.pair + c) * self.nz + s))
        return pairs


def bits_of(count, descending):
    bits = []
    bit = 1
    while bit < count:
        bits.append(bit)
        bit *= 2
    return bits[::-1] if descending else bits


def group_gather(lay, block, descending):
    held = {0: block}
    for bit in bits_of(lay.groups, descending):
        for m in list(held):
            held[m ^ bit] = lay.group_hop(held[m], bit)
    return held


def group_scatter(lay, blocks, descending):
    held = dict(blocks)
    for bit in bits_of(lay.groups, descending):
        kept = {}
        for m in held:
            if not m & bit:
                got = lay.group_hop(held[m ^ bit].astype(bf16), bit)
                kept[m] = held[m].astype(f32) + got.astype(f32)
        held = kept
    return held[0]


def total_sum(lay, vector):
    bit = 1
    while bit < lay.nd * lay.nz:
        vector = vector + lay.flat_hop(vector, bit)
        bit *= 2
    return vector


def norm_kernel(pair, first, pos_ref, *refs):
    x_refs = refs[:pair]
    vec_ref = refs[pair]
    out_refs = refs[-3:]
    for r in range(pair):
        normed, _ = normalize(x_refs[r][0].astype(f32))
        out_refs[0][r, 0, 0] = (normed * vec_ref[0:1] + vec_ref[1:2]).astype(bf16)
        out_refs[1][r, 0, 0] = (normed * vec_ref[2:3] + vec_ref[3:4]).astype(bf16)
        out_refs[2][r, 0, 0] = normed.astype(bf16)


def norm_place(lay, pieces, vec, where, held):
    count, span, width = pieces[0].shape
    pair = lay.pair
    tile = min(span, 128)
    out = jax.ShapeDtypeStruct((pair, count, lay.nz, span, width), bf16)
    x_spec = pl.BlockSpec((1, tile, width), lambda i, j, pos: (i, j, 0))
    v_spec = pl.BlockSpec(vec.shape, lambda i, j, pos: (0, 0))
    o_spec = pl.BlockSpec((pair, 1, 1, tile, width), lambda i, j, pos: (0, i, pos[0], j, 0))
    in_specs = [x_spec] * pair + [v_spec]
    aliases = {}
    if held:
        in_specs += [pl.BlockSpec(memory_space=pl.ANY)] * 3
        aliases = {pair + 2 + k: k for k in range(3)}
    return pl.pallas_call(
        partial(norm_kernel, pair, not held),
        grid_spec=pltpu.PrefetchScalarGridSpec(
            num_scalar_prefetch=1,
            grid=(count, span // tile),
            in_specs=in_specs,
            out_specs=[o_spec] * 3,
        ),
        out_shape=[out] * 3,
        input_output_aliases=aliases,
        name="norm_place",
        **params((20 * pair * count * span * width, 8 * pair * count * span * width)),
    )(jnp.reshape(where, (1,)).astype(jnp.int32), *pieces, vec, *held)


def turn(values, cosine, low_sine, high_sine, quarter):
    head = values[:, :LANES]
    turned = (
        head * cosine
        + pltpu.roll(head, LANES - quarter, 1) * low_sine
        + pltpu.roll(head, quarter, 1) * high_sine
    )
    return jnp.concatenate([turned, values[:, LANES:]], axis=1)


def attn_fwd_kernel(quarter, scale, tile, a_ref, wq_ref, wk_ref, wv_ref, b_ref, tab_ref, qkv_ref, o_ref, lse_ref):
    length, hd = o_ref.shape[1:]
    cosine, low_sine, high_sine = tab_ref[0], tab_ref[1], tab_ref[2]
    a = a_ref[0]
    q = dot(a, wq_ref[...]) + b_ref[0:1, :hd]
    qkv_ref[0, :, :hd] = turn(q, cosine, low_sine, high_sine, quarter).astype(bf16)
    k = dot(a, wk_ref[...]) + b_ref[0:1, hd : 2 * hd]
    qkv_ref[0, :, hd : 2 * hd] = turn(k, cosine, low_sine, high_sine, quarter).astype(bf16)
    v = dot(a, wv_ref[...]) + b_ref[0:1, 2 * hd :]
    qkv_ref[0, :, 2 * hd :] = v.astype(bf16)
    for i in range(length // tile):
        end = (i + 1) * tile
        q_i = qkv_ref[0, i * tile : end, :hd]
        scores = dot(q_i, qkv_ref[0, :end, hd : 2 * hd], 1, 1) * scale
        row = lax.broadcasted_iota(jnp.int32, scores.shape, 0) + i * tile
        col = lax.broadcasted_iota(jnp.int32, scores.shape, 1)
        scores = jnp.where(col <= row, scores, masked_value)
        row_max = jnp.max(scores, axis=1, keepdims=True)
        terms = jnp.exp(scores - row_max)
        row_sum = jnp.sum(terms, axis=1, keepdims=True)
        probs = (terms / row_sum).astype(bf16)
        o_ref[0, i * tile : end] = dot(probs, qkv_ref[0, :end, 2 * hd :]).astype(bf16)
        lse_ref[0, i * tile : end] = jnp.broadcast_to(row_max + jnp.log(row_sum), (tile, LANES))


def attn_forward(a, w_qu, bias, tables, unit, hd, scale):
    seqs, length, width = a.shape
    first = unit // hd
    w_spec = [pl.BlockSpec((width, hd), lambda s, j=j: (0, first + j)) for j in range(3)]
    flops = 2 * seqs * length * (3 * hd * width + 2 * length * hd)
    return pl.pallas_call(
        partial(attn_fwd_kernel, hd // 8, scale, min(256, length)),
        grid=(seqs,),
        in_specs=[pl.BlockSpec((1, length, width), lambda s: (s, 0, 0))]
        + w_spec
        + [
            pl.BlockSpec(bias.shape, lambda s: (0, 0)),
            pl.BlockSpec(tables.shape, lambda s: (0, 0, 0)),
        ],
        out_specs=[
            pl.BlockSpec((1, length, 3 * hd), lambda s: (s, 0, 0)),
            pl.BlockSpec((1, length, hd), lambda s: (s, 0, 0)),
            pl.BlockSpec((1, length, LANES), lambda s: (s, 0, 0)),
        ],
        out_shape=[
            jax.ShapeDtypeStruct((seqs, length, 3 * hd), bf16),
            jax.ShapeDtypeStruct((seqs, length, hd), bf16),
            jax.ShapeDtypeStruct((seqs, length, LANES), f32),
        ],
        name="attn_forward",
        **params((flops, 12 * seqs * length * width)),
    )(a, w_qu, w_qu, w_qu, bias, tables)


def attn_bwd_kernel(quarter, scale, tile, dy_ref, wo_ref, qkv_ref, lse_ref, tab_ref, dp_ref, sum_ref, do_s, dk_s, dv_s):
    length = dy_ref.shape[1]
    hd = wo_ref.shape[0]
    cosine, low_sine, high_sine = tab_ref[0], -tab_ref[1], -tab_ref[2]
    do_s[...] = dot(dy_ref[0], wo_ref[...], 1, 1).astype(bf16)
    steps = length // tile
    for i in reversed(range(steps)):
        end = (i + 1) * tile
        q_i = qkv_ref[0, i * tile : end, :hd]
        k = qkv_ref[0, :end, hd : 2 * hd]
        do_i = do_s[i * tile : end]
        scores = dot(q_i, k, 1, 1) * scale
        row = lax.broadcasted_iota(jnp.int32, scores.shape, 0) + i * tile
        col = lax.broadcasted_iota(jnp.int32, scores.shape, 1)
        probs = jnp.where(col <= row, jnp.exp(scores - lse_ref[0, i * tile : end, 0:1]), 0.0)
        probs_grad = dot(do_i, qkv_ref[0, :end, 2 * hd :], 1, 1)
        row_dot = jnp.sum(probs * probs_grad, axis=1, keepdims=True)
        score_grad = (probs * (probs_grad - row_dot)).astype(bf16)
        dq = dot(score_grad, k) * scale
        dp_ref[0, i * tile : end, :hd] = turn(
            dq,
            cosine[i * tile : end],
            low_sine[i * tile : end],
            high_sine[i * tile : end],
            quarter,
        ).astype(bf16)
        dk = dot(score_grad, q_i, 0, 0)
        dv = dot(probs.astype(bf16), do_i, 0, 0)
        if i == steps - 1:
            dk_s[...] = dk
            dv_s[...] = dv
        else:
            dk_s[:end] += dk
            dv_s[:end] += dv
    dp_ref[0, :, hd : 2 * hd] = turn(
        dk_s[...] * scale, cosine, low_sine, high_sine, quarter
    ).astype(bf16)
    dp_ref[0, :, 2 * hd :] = dv_s[...].astype(bf16)
    total = jnp.sum(dp_ref[0].astype(f32), axis=0, keepdims=True)
    sum_ref[0] = jnp.broadcast_to(total, sum_ref.shape[1:])


def attn_backward(dy, w_out, qkv, lse, tables, scale):
    seqs, length, width = dy.shape
    hd = w_out.shape[0]
    flops = 2 * seqs * length * (hd * width + 5 * length * hd)
    return pl.pallas_call(
        partial(attn_bwd_kernel, hd // 8, scale, min(256, length)),
        grid=(seqs,),
        in_specs=[
            pl.BlockSpec((1, length, width), lambda s: (s, 0, 0)),
            pl.BlockSpec(w_out.shape, lambda s: (0, 0)),
            pl.BlockSpec((1, length, 3 * hd), lambda s: (s, 0, 0)),
            pl.BlockSpec((1, length, LANES), lambda s: (s, 0, 0)),
            pl.BlockSpec(tables.shape, lambda s: (0, 0, 0)),
        ],
        out_specs=[
            pl.BlockSpec((1, length, 3 * hd), lambda s: (s, 0, 0)),
            pl.BlockSpec((1, 8, 3 * hd), lambda s: (s, 0, 0)),
        ],
        out_shape=[
            jax.ShapeDtypeStruct((seqs, length, 3 * hd), bf16),
            jax.ShapeDtypeStruct((seqs, 8, 3 * hd), f32),
        ],
        scratch_shapes=[
            pltpu.VMEM((length, hd), bf16),
            pltpu.VMEM((length, hd), f32),
            pltpu.VMEM((length, hd), f32),
        ],
        name="attn_backward",
        **params((flops, 8 * seqs * length * width)),
    )(dy, w_out, qkv, lse, tables)


def mlp_fwd_kernel(m_ref, wu_ref, b_ref, wd_ref, o_ref, wo_ref, g_ref, slope_ref, out_ref):
    u = dot(m_ref[...], wu_ref[...]) + b_ref[0:1]
    half = 0.5 * (1.0 + lax.erf(u * (0.5**0.5)))
    g_ref[...] = (u * half).astype(bf16)
    slope = half + u * (jnp.exp(-0.5 * u * u) * 0.3989422804014327)
    slope_ref[...] = slope.astype(bf16)
    total = dot(g_ref[...], wd_ref[...], 1, 1) + dot(o_ref[...], wo_ref[...])
    out_ref[...] = total.astype(bf16)


def mlp_forward(m, w_qu, bias, w_down, o, w_out, tile):
    tokens, width = m.shape
    unit, hd = w_down.shape[1], o.shape[1]
    flops = 2 * tokens * width * (2 * unit + hd)
    return pl.pallas_call(
        mlp_fwd_kernel,
        grid=(tokens // tile,),
        in_specs=[
            pl.BlockSpec((tile, width), lambda i: (i, 0)),
            pl.BlockSpec((width, unit), lambda i: (0, 0)),
            pl.BlockSpec(bias.shape, lambda i: (0, 0)),
            pl.BlockSpec(w_down.shape, lambda i: (0, 0)),
            pl.BlockSpec((tile, hd), lambda i: (i, 0)),
            pl.BlockSpec(w_out.shape, lambda i: (0, 0)),
        ],
        out_specs=[
            pl.BlockSpec((tile, unit), lambda i: (i, 0)),
            pl.BlockSpec((tile, unit), lambda i: (i, 0)),
            pl.BlockSpec((tile, width), lambda i: (i, 0)),
        ],
        out_shape=[
            jax.ShapeDtypeStruct((tokens, unit), bf16),
            jax.ShapeDtypeStruct((tokens, unit), bf16),
            jax.ShapeDtypeStruct((tokens, width), bf16),
        ],
        name="mlp_forward",
        **params((flops, 12 * tokens * width)),
    )(m, w_qu, bias, w_down, o, w_out)


def mlp_bwd_kernel(hd, dy_ref, wd_ref, slope_ref, dp_ref, wu_ref, wq_ref, wk_ref, wv_ref, vec_ref, du_ref, sum_ref, z_ref):
    dg = dot(dy_ref[...], wd_ref[...])
    du_ref[...] = (dg * slope_ref[...].astype(f32)).astype(bf16)
    total = jnp.sum(du_ref[...].astype(f32), axis=0, keepdims=True)
    total = jnp.broadcast_to(total, sum_ref.shape)

    @pl.when(pl.program_id(0) == 0)
    def _():
        sum_ref[...] = total

    @pl.when(pl.program_id(0) > 0)
    def _():
        sum_ref[...] += total

    da = (
        dot(dp_ref[:, :hd], wq_ref[...], 1, 1)
        + dot(dp_ref[:, hd : 2 * hd], wk_ref[...], 1, 1)
        + dot(dp_ref[:, 2 * hd :], wv_ref[...], 1, 1)
    )
    dm = dot(du_ref[...], wu_ref[...], 1, 1)
    z_ref[...] = (da * vec_ref[0:1] + dm * vec_ref[2:3]).astype(bf16)


def mlp_backward(dy, w_down, slope, dp, w_qu, vec, tile):
    tokens, width = dy.shape
    unit, hd = w_down.shape[1], dp.shape[1] // 3
    first = unit // hd
    flops = 2 * tokens * width * (2 * unit + 3 * hd)
    return pl.pallas_call(
        partial(mlp_bwd_kernel, hd),
        grid=(tokens // tile,),
        in_specs=[
            pl.BlockSpec((tile, width), lambda i: (i, 0)),
            pl.BlockSpec(w_down.shape, lambda i: (0, 0)),
            pl.BlockSpec((tile, unit), lambda i: (i, 0)),
            pl.BlockSpec((tile, 3 * hd), lambda i: (i, 0)),
            pl.BlockSpec((width, unit), lambda i: (0, 0)),
        ]
        + [pl.BlockSpec((width, hd), lambda i, j=j: (0, first + j)) for j in range(3)]
        + [pl.BlockSpec(vec.shape, lambda i: (0, 0))],
        out_specs=[
            pl.BlockSpec((tile, unit), lambda i: (i, 0)),
            pl.BlockSpec((8, unit), lambda i: (0, 0)),
            pl.BlockSpec((tile, width), lambda i: (i, 0)),
        ],
        out_shape=[
            jax.ShapeDtypeStruct((tokens, unit), bf16),
            jax.ShapeDtypeStruct((8, unit), f32),
            jax.ShapeDtypeStruct((tokens, width), bf16),
        ],
        name="mlp_backward",
        **params((flops, 12 * tokens * width)),
    )(dy, w_down, slope, dp, w_qu, w_qu, w_qu, w_qu, vec)


def adam_kernel(pair, rate, folded, c_ref, *refs):
    g_refs = refs[:pair]
    w_ref, m_ref, v_ref = refs[pair : pair + 3]
    outs = refs[-5:] if folded else refs[-4:]
    parts = [r[0].astype(f32) for r in g_refs]
    if pair == 2:
        swapped = c_ref[0] == 1
        parts = [jnp.where(swapped, parts[1], parts[0]), jnp.where(swapped, parts[0], parts[1])]
    raw = parts[0] if pair == 1 else jnp.concatenate(parts, axis=1)
    w = w_ref[...]
    if folded:
        vec_ref, colsum_ref = refs[pair + 3 : pair + 5]
        low = w.astype(bf16).astype(f32)
        colsum = colsum_ref[0:1]
        grad = raw * vec_ref[:, 0:1] + colsum * vec_ref[:, 1:2]
        moment = jnp.sum(low * raw, axis=1, keepdims=True)
        plain = jnp.sum(low * colsum, axis=1, keepdims=True)
        lane = lax.broadcasted_iota(jnp.int32, outs[4].shape, 1)
        sums = jnp.where(lane == 0, moment, jnp.where(lane == 1, plain, 0.0))
        start = pl.program_id(0) == 0
        if len(c_ref.shape) and True:
            for d in range(1, 2):
                start = jnp.logical_and(start, pl.program_id(d) == 0)

        @pl.when(start)
        def _():
            outs[4][...] = sums

        @pl.when(jnp.logical_not(start))
        def _():
            outs[4][...] += sums
    else:
        grad = raw
    result = adamw(w, grad, m_ref[...], v_ref[...], rate)
    for ref, value in zip(outs, result, strict=False):
        ref[...] = value


def adam_columns(lay, rate, parts, state, start, kinds, piece, held, fold=None):
    pair, nz = lay.pair, lay.nz
    rows, total = state[0].shape
    wide = pair * piece
    first = start // wide

    def col(j, z, c):
        return (0, first + j * nz + z)

    w_spec = pl.BlockSpec((rows, wide), col)
    in_specs = [pl.BlockSpec((1, rows, piece), lambda j, z, c: (z, 0, j))] * pair + [w_spec] * 3
    operands = list(parts) + list(state)
    out_specs = [w_spec] * 4
    out_shape = [jax.ShapeDtypeStruct((rows, total), f32)] * 4
    if fold is not None:
        vec, colsum = fold
        in_specs += [
            pl.BlockSpec(vec.shape, lambda j, z, c: (0, 0)),
            pl.BlockSpec((8, wide), lambda j, z, c: (0, j * nz + z)),
        ]
        operands += [vec, colsum]
        out_specs += [pl.BlockSpec((rows, LANES), lambda j, z, c: (0, 0))]
        out_shape += [jax.ShapeDtypeStruct((rows, LANES), f32)]
    aliases = {}
    if held:
        aliases = {1 + len(operands) + k: k for k in range(4)}
        in_specs += [pl.BlockSpec(memory_space=pl.ANY)] * 4
        operands += list(held)
    return pl.pallas_call(
        partial(adam_kernel, pair, rate, fold is not None),
        grid_spec=pltpu.PrefetchScalarGridSpec(
            num_scalar_prefetch=1, grid=(kinds, nz), in_specs=in_specs, out_specs=out_specs
        ),
        out_shape=out_shape,
        input_output_aliases=aliases,
        name="adam_columns",
        **params((30 * rows * kinds * piece * HEADS, 30 * rows * kinds * piece * HEADS)),
    )(jnp.reshape(lay.c, (1,)).astype(jnp.int32), *operands)


def gather_pieces(lay, own):
    piece = own
    for k in range(lay.nz):
        if k:
            piece = lay.ring(piece)
        pieces = [piece] + [lay.core_hop(piece, r) for r in range(1, lay.pair)]
        yield (lay.z - k) % lay.nz, pieces


def gather_tokens(lay, own):
    count, span, width = own.shape
    out = jnp.zeros((lay.pair * count * lay.nz, span, width), own.dtype)
    for where, pieces in gather_pieces(lay, own):
        for r, piece in enumerate(pieces):
            for s in range(count):
                out = lax.dynamic_update_index_in_dim(
                    out, piece[s], (r * count + s) * lay.nz + where, 0
                )
    return out.reshape(lay.pair * count, lay.nz * span, width)


def scatter_tokens(lay, partial_sum, count):
    total, length, width = partial_sum.shape
    span = length // lay.nz
    parts = [partial_sum[:count].reshape(count, lay.nz, span, width)]
    for r in range(1, lay.pair):
        other = lay.core_hop(partial_sum[r * count : (r + 1) * count], r)
        parts.append(other.reshape(count, lay.nz, span, width))

    def chunk(place):
        place = place % lay.nz
        return sum(
            lax.dynamic_index_in_dim(p, place, 1, keepdims=False).astype(f32) for p in parts
        )

    acc = chunk(lay.z - 1)
    for k in range(1, lay.nz):
        got = lay.ring(acc.astype(bf16))
        acc = got.astype(f32) + chunk(lay.z - 1 - k)
    return acc


def body(
    inputs,
    cotangent,
    attn_params,
    attn_first,
    attn_second,
    mlp_params,
    mlp_first,
    mlp_second,
    small,
    small_first,
    small_second,
):
    lay = Layout(lax.axis_size("dp"), lax.axis_size("seq"))
    groups, nz, pair = lay.groups, lay.nz, lay.pair
    count, span, width = inputs.shape
    rows = attn_params.shape[0]
    ff = mlp_params.shape[1] // 2
    hd = width // HEADS
    unit = ff // HEADS
    rot_dims = hd // 4
    score_scale = hd ** (-0.5)
    first_row = (lay.dp * nz + lay.z) * rows
    seqs, length = count * pair, span * nz
    tokens_here = seqs * length

    vec = small.astype(bf16)
    placed = jnp.concatenate([vec.T, jnp.zeros((3, rows), bf16)], axis=0)
    placed = lax.dynamic_update_slice(jnp.zeros((16, width), bf16), placed, (0, first_row))
    vectors = total_sum(lay, placed).astype(f32)
    norm_vec = vectors[:8]
    qkv_bias = vectors[6:9].reshape(3, HEADS, hd)
    qkv_bias = lax.dynamic_index_in_dim(qkv_bias, lay.t, 1, keepdims=False).reshape(1, 3 * hd)
    up_bias = lax.dynamic_slice(vectors[9:13].reshape(-1), (lay.t * unit,), (unit,))[None]
    out_bias = vectors[4] + vectors[5]

    attn_low = attn_params.astype(bf16)
    mlp_low = mlp_params.astype(bf16)

    def by_target(columns, kinds):
        piece = columns.shape[1] // kinds // HEADS
        blocks = columns.reshape(rows, kinds, nz, pair, piece).transpose(3, 2, 0, 1, 4)
        return blocks.reshape(pair, nz, rows, kinds * piece)

    def to_columns(blocks):
        halves = []
        for r in range(pair):
            half = lax.dynamic_index_in_dim(blocks, lay.c ^ r, 0, keepdims=False)
            if r:
                half = lay.core_hop(half, r)
            half = lax.all_to_all(half, "seq", 0, 0, tiled=True)
            halves.append(half.reshape(nz * rows, -1))
        return halves

    def whole(halves):
        n = halves[0].shape[1]
        out = jnp.zeros((groups * pair, nz * rows, n), bf16)
        for r, half in enumerate(halves):
            for m, v in group_gather(lay, half, bool(r)).items():
                out = lax.dynamic_update_index_in_dim(
                    out, v, (lay.g ^ m) * pair + (lay.c ^ r), 0
                )
        return out.reshape(width, n)

    qu_blocks = jnp.concatenate(
        [by_target(mlp_low[:, :ff], 1), by_target(attn_low[:, : 3 * width], 3)], axis=-1
    )
    w_qu = whole(to_columns(qu_blocks))
    w_down = whole(to_columns(by_target(mlp_low[:, ff:], 1)))
    w_out = lax.ppermute(attn_low[:, 3 * width :], AXES, lay.head_owner_perm())
    w_out_buf = jnp.zeros((groups, rows, width), bf16)
    for m, v in group_gather(lay, w_out, True).items():
        w_out_buf = lax.dynamic_update_index_in_dim(w_out_buf, v, lay.g ^ m, 0)
    w_out = w_out_buf.reshape(hd, width)

    held = ()
    for where, pieces in gather_pieces(lay, inputs):
        held = norm_place(lay, pieces, norm_vec, where, held)
    a_all, m_all, x_all = (v.reshape(seqs, length, width) for v in held)
    dy_all = gather_tokens(lay, cotangent)

    positions = jnp.arange(length, dtype=f32)
    frequency = 10000.0 ** (-(jnp.arange(rot_dims // 2, dtype=f32) * 2.0) / rot_dims)
    angles = positions[:, None] * frequency[None, :]
    cosine, sine = jnp.cos(angles), jnp.sin(angles)
    blank = jnp.zeros_like(sine)
    rest = jnp.zeros((length, LANES - rot_dims), f32)
    tables = jnp.stack(
        [
            jnp.concatenate([cosine, cosine, rest + 1.0], axis=1),
            jnp.concatenate([-sine, blank, rest], axis=1),
            jnp.concatenate([blank, sine, rest], axis=1),
        ]
    )

    tile = min(512, tokens_here)
    qkv, o, lse = attn_forward(a_all, w_qu, qkv_bias, tables, unit, hd, score_scale)
    flat = (tokens_here, width)
    o = o.reshape(tokens_here, hd)
    g, slope, out_part = mlp_forward(m_all.reshape(flat), w_qu, up_bias, w_down, o, w_out, tile)
    out_sum = scatter_tokens(lay, out_part.reshape(seqs, length, width), count)
    outputs = (inputs.astype(f32) + out_sum + out_bias).astype(bf16)

    dy_flat, x_flat = dy_all.reshape(flat), x_all.reshape(flat)
    dp, dp_sums = attn_backward(dy_all, w_out, qkv, lse, tables, score_scale)
    dp = dp.reshape(tokens_here, 3 * hd)
    du, du_sums, z_part = mlp_backward(dy_flat, w_down, slope, dp, w_qu, norm_vec, tile)
    normed_grad = scatter_tokens(lay, z_part.reshape(seqs, length, width), count)
    normed, scaling = normalize(inputs.astype(f32))
    grad_mean = jnp.mean(normed_grad, axis=-1, keepdims=True)
    grad_proj = jnp.mean(normed_grad * normed, axis=-1, keepdims=True)
    upstream = cotangent.astype(f32)
    input_grad = upstream + scaling * (normed_grad - grad_mean - normed * grad_proj)

    def own_rows(partial_sum):
        n = partial_sum.shape[-1]
        stacked = partial_sum.reshape(groups * pair, nz * rows, n)
        parts = []
        for r in range(pair):
            blocks = {
                m: lax.dynamic_index_in_dim(
                    stacked, (lay.g ^ m) * pair + (lay.c ^ r), 0, keepdims=False
                )
                for m in range(groups)
            }
            half = group_scatter(lay, blocks, bool(r)).astype(bf16).reshape(nz, rows, n)
            half = lax.all_to_all(half, "seq", 0, 0, tiled=True)
            parts.append(lay.core_hop(half, r) if r else half)
        return parts

    down_parts = own_rows(dot(dy_flat, g, 0, 0).astype(bf16))
    up_parts = own_rows(dot(x_flat, du, 0, 0).astype(bf16))
    qkv_parts = own_rows(dot(x_flat, dp, 0, 0).astype(bf16))
    out_grad = dot(o, dy_flat, 0, 0).astype(bf16).reshape(groups, rows, width)
    out_grad = {
        m: lax.dynamic_index_in_dim(out_grad, lay.g ^ m, 0, keepdims=False) for m in range(groups)
    }
    out_grad = group_scatter(lay, out_grad, True).astype(bf16)
    out_grad = lax.ppermute(out_grad, AXES, [(b, a) for a, b in lay.head_owner_perm()])

    qkv_sum = jnp.sum(dp_sums[:, 0], axis=0).reshape(3, 1, hd)
    qkv_sum = lax.dynamic_update_slice(jnp.zeros((3, HEADS, hd), f32), qkv_sum, (0, lay.t, 0))
    up_sum = lax.dynamic_update_slice(jnp.zeros((ff,), f32), du_sums[0], (lay.t * unit,))
    upstream_sum = jnp.sum(upstream, axis=(0, 1))
    sums = jnp.concatenate([qkv_sum.reshape(-1), up_sum, upstream_sum]).reshape(8, width)
    sums = total_sum(lay, sums)
    qkv_sum = jnp.broadcast_to(sums[:3].reshape(1, -1), (8, 3 * width))
    up_sum = jnp.broadcast_to(sums[3:7].reshape(1, -1), (8, ff))

    own_vec = vec.astype(f32)
    mlp_state = (mlp_params, mlp_first, mlp_second)
    attn_state = (attn_params, attn_first, attn_second)
    mlp_result = adam_columns(lay, rate_mlp, down_parts, mlp_state, ff, 1, unit, ())
    *mlp_result, up_small = adam_columns(
        lay, rate_mlp, up_parts, mlp_state, 0, 1, unit, mlp_result, (own_vec[:, 2:4], up_sum)
    )
    *attn_result, qkv_small = adam_columns(
        lay, rate_attention, qkv_parts, attn_state, 0, 3, hd, (), (own_vec[:, 0:2], qkv_sum)
    )
    out_state = tuple(v[:, 3 * width :] for v in attn_state)
    out_result = adamw(out_state[0], out_grad.astype(f32), out_state[1], out_state[2], rate_attention)
    attn_result = [
        lax.dynamic_update_slice(v, n, (0, 3 * width)) for v, n in zip(attn_result, out_result)
    ]
    own_sums = lax.dynamic_slice(sums, (0, first_row), (8, rows)).T
    small_grad = jnp.concatenate(
        [
            qkv_small[:, 0:2],
            up_small[:, 0:2],
            own_sums[:, 7:8],
            own_sums[:, 7:8],
            own_sums[:, :7],
        ],
        axis=1,
    )
    small_result = adamw(small, small_grad, small_first, small_second, rate_vector)
    return (outputs, input_grad, *attn_result, *mlp_result, *small_result)


def solution(mesh):
    tokens, weights = P("dp", "seq", None), P(("dp", "seq"), None)
    return jax.shard_map(
        body,
        mesh=mesh,
        in_specs=(tokens,) * 2 + (weights,) * 9,
        out_specs=(tokens,) * 2 + (weights,) * 12,
        check_vma=False,
    )
```

time: 5510 us -> 784 us (0.14)
  waiting for transfers between devices: 4920 us -> 280 us
  matrix products: 258 us -> 30.9 us
  Pallas kernels: 0 us -> 143 us
  starting transfers between devices: 12.7 us -> 129 us
  other arithmetic: 182 us -> 76.4 us
  local copies, waits for them, and re-layouts: 46.5 us -> 115 us
  blocking collectives: 65.9 us -> 0 us
    unnamed x11 -> x0, waiting for transfers between devices: 2800 us -> none
    reduce_scatter x3 -> x0, waiting for transfers between devices: 1550 us -> none  [the longest x1 1310 us: body(): lax.psum_scatter(attn_term, ('dp', 'seq'), scatter_dimension=0, tiled=True)]
    all_gather x4 -> x0, waiting for transfers between devices: 563 us -> none  [the longest x1 302 us: body(): lax.all_gather(mlp_low, ('dp', 'seq'), axis=0, tiled=True)]
    dot_general x18 -> x4, matrix products: 258 us -> 30.9 us  [dot(): lax.dot_general(left_op, right_op, (((left_dim,), (right_dim,)), ((), ())...]
    ppermute x0 -> x75, waiting for transfers between devices: none -> 173 us  [the longest x63 105 us: hop(): return lax.ppermute(value, AXES, self.perm(target))]
    pallas_call x0 -> x11, Pallas kernels: none -> 143 us  [the longest x1 33.1 us: mlp_backward(): pl.pallas_call(partial(mlp_bwd_kernel, hd), grid=(tokens // tile,), in_sp...]
    concatenate x4 -> x2, other arithmetic: 133 us -> 6.9 us  [the longest x1 6.09 us: body(): jnp.concatenate([by_target(mlp_low[:, :ff], 1), by_target(attn_low[:, :3...]
    all_to_all x0 -> x10, waiting for transfers between devices: none -> 107 us  [the longest x6 80.3 us: own_rows(): half = lax.all_to_all(half, 'seq', 0, 0, tiled=True)]
  transfers between devices with their start and end apart: 9 -> 85, of which waited for: 8 -> 19; matrix products, arithmetic and copies ran while one was open for 6% -> 26% of each run, Pallas kernels for 0% -> 8%
where the time goes in v1:
time: 784 us; the launch traced here: 776 us
  waiting for transfers between devices  280 us (36%)
  Pallas kernels  143 us (18%)
  starting transfers between devices  129 us (16%)
  local copies, waits for them, and re-layouts  115 us (15%)
  other arithmetic  76.4 us (10%)
  matrix products  30.9 us (4%)
    ppermute x63, waiting for transfers between devices, hop(): return lax.ppermute(value, AXES, self.perm(target))  105 us
    all_to_all x6, waiting for transfers between devices, own_rows(): half = lax.all_to_all(half, 'seq', 0, 0, tiled=True)  80.3 us
    ppermute x10, waiting for transfers between devices, flat_hop(): lax.ppermute(value, AXES, [(i, i ^ bit) for i in range(self.nd * self.nz)])  68 us
    ppermute x63, starting transfers between devices, hop(): return lax.ppermute(value, AXES, self.perm(target))  60.1 us
    pallas_call x1, Pallas kernels, mlp_backward(): pl.pallas_call(partial(mlp_bwd_kernel, hd), grid=(tokens // tile,), in_sp...  33.1 us
    dot_general x4, matrix products, dot(): lax.dot_general(left_op, right_op, (((left_dim,), (right_dim,)), ((), ())...  30.9 us
    pallas_call x1, Pallas kernels, mlp_forward(): pl.pallas_call(mlp_fwd_kernel, grid=(tokens // tile,), in_specs=[pl.Block...  29 us
    all_to_all x4, waiting for transfers between devices, to_columns(): half = lax.all_to_all(half, 'seq', 0, 0, tiled=True)  26.9 us
  transfers between devices with their start and end apart: 85, of which 19 were waited for; matrix products, arithmetic and copies ran while one was open for 26% of the time, Pallas kernels for 8%

profile of v1, /device:TPU:5, one launch (start us, length us, event | category | flops | bytes accessed | tf_op | source)
XLA Modules:
  0.0 776.1 jit_solution(12570727531375207507)
XLA Ops:
  49.7 21.1 %collective-permute-done.4 = bf16[16,2048]{0,1:T(8,128)(2,1)} collective-permute-done((bf16[16,2048]{0,1:T(8,128)(2,1)}, bf16[16,2048]{0,1:T(8,128)(2,1)}, u32[]{:S(2)}, u32[]{:S(2)}) %collective-permute-start.4) | collective-permute-done | bytes 65568 | tf_op jit(solution)/shard_map/ppermute | solution.py:99
  72.6 25.2 %collective-permute-done.5 = bf16[16,2048]{0,1:T(8,128)(2,1)S(1)} collective-permute-done((bf16[16,2048]{0,1:T(8,128)(2,1)}, bf16[16,2048]{0,1:T(8,128)(2,1)S(1)}, u32[]{:S(2)}, u32[]{:S(2)}) %collective-permute-start.5) | collective-permute-done | bytes 65568 | tf_op jit(solution)/shard_map/ppermute | solution.py:99
  101.7 9.3 %collective-permute-start.7 = (bf16[16,2048]{0,1:T(8,128)(2,1)S(1)}, bf16[16,2048]{0,1:T(8,128)(2,1)}, u32[]{:S(2)}, u32[]{:S(2)}) collective-permute-start(bf16[16,2048]{0,1:T(8,128)(2,1)S(1)} %add.565), channel_id=1, source_target_pairs={{0,8},{1,9},{2,10},{3,11},{4,12},{5,13},{6,14},{7,15},{8,0},{9,1},... | collective-permute-start | bytes 196616 | tf_op jit(solution)/shard_map/ppermute | solution.py:99
  129.1 11.2 %collective-permute-done.8 = bf16[16,2048]{0,1:T(8,128)(2,1)S(1)} collective-permute-done((bf16[16,2048]{0,1:T(8,128)(2,1)S(1)}, bf16[16,2048]{0,1:T(8,128)(2,1)S(1)}, u32[]{:S(2)}, u32[]{:S(2)}) %collective-permute-start.8) | collective-permute-done | bytes 65568 | tf_op jit(solution)/shard_map/ppermute | solution.py:99
  158.1 8.6 %all-to-all-done.3 = bf16[4,64,1024]{2,1,0:T(8,128)(2,1)S(1)} async-done(((bf16[4,64,1024]{2,1,0:T(8,128)(2,1)}), bf16[4,64,1024]{2,1,0:T(8,128)(2,1)S(1)}, u32[]{:S(2)}, u32[]{:S(2)}) %all-to-all-start.3) | async-done | bytes 524320 | tf_op jit(solution)/shard_map/all_to_all | solution.py:589
  197.0 18.2 %all-to-all-done = bf16[4,64,1792]{2,1,0:T(8,128)(2,1)S(1)} async-done(((bf16[4,64,1792]{2,1,0:T(8,128)(2,1)}), bf16[4,64,1792]{2,1,0:T(8,128)(2,1)S(1)}, u32[]{:S(2)}, u32[]{:S(2)}) %all-to-all-start) | async-done | bytes 917536 | tf_op jit(solution)/shard_map/all_to_all | solution.py:589
  237.5 21.4 %collective-permute-done.37 = bf16[1,256,2048]{2,1,0:T(8,128)(2,1)} collective-permute-done((bf16[1,256,2048]{2,1,0:T(8,128)(2,1)}, bf16[1,256,2048]{2,1,0:T(8,128)(2,1)}, u32[]{:S(2)}, u32[]{:S(2)}) %collective-permute-start.37) | collective-permute-done | bytes 1048608 | tf_op jit(solution)/shard_map/ppermute | solution.py:87
  285.8 10.8 %collective-permute-done.39 = bf16[1,256,2048]{2,1,0:T(8,128)(2,1)} collective-permute-done((bf16[1,256,2048]{2,1,0:T(8,128)(2,1)}, bf16[1,256,2048]{2,1,0:T(8,128)(2,1)}, u32[]{:S(2)}, u32[]{:S(2)}) %collective-permute-start.39) | collective-permute-done | bytes 1048608 | tf_op jit(solution)/shard_map/ppermute | solution.py:87
  299.9 19.0 %collective-permute-done.2.refs_0_ = bf16[1,256,2048]{2,1,0:T(8,128)(2,1)S(1)} collective-permute-done((bf16[1,256,2048]{2,1,0:T(8,128)(2,1)S(1)}, bf16[1,256,2048]{2,1,0:T(8,128)(2,1)S(1)}, u32[]{:S(2)}, u32[]{:S(2)}) %collective-permute-start.2) | collective-permute-done | bytes 1048608 | tf_op jit(solution)/shard_map/ppermute | solution.py:87
  329.4 17.6 %collective-permute-done.18 = bf16[256,1792]{1,0:T(8,128)(2,1)S(1)} collective-permute-done((bf16[256,1792]{1,0:T(8,128)(2,1)S(1)}, bf16[256,1792]{1,0:T(8,128)(2,1)S(1)}, u32[]{:S(2)}, u32[]{:S(2)}) %collective-permute-start.18) | collective-permute-done | bytes 917536 | tf_op jit(solution)/shard_map/ppermute | solution.py:87
  354.0 17.1 %attn_forward.1 = (bf16[2,1024,768]{2,1,0:T(8,128)(2,1)}, bf16[2,1024,256]{2,1,0:T(8,128)(2,1)}, f32[2,1024,128]{2,1,0:T(8,128)}) custom-call(bf16[2,1024,2048]{2,1,0:T(8,128)(2,1)} %bitcast.241, bf16[2048,1792]{1,0:T(8,128)(2,1)} %bitcast.21.wq_ref.wk_ref.wv_ref.wu_ref, bf16[2048,1792]{1,0:T(8,128)(2,1)} %bitcast.21.wq_ref.wk_ref.wv_ref.wu_ref, ...), custom_call_target="tpu_custom_call" | custom-call | flops 8589934592 | bytes 50331648 | tf_op jit(solution)/shard_map/attn_forward/pallas_call | solution.py:226
  372.3 17.5 %attn_backward.1 = (bf16[2,1024,768]{2,1,0:T(8,128)(2,1)}, f32[2,8,768]{2,1,0:T(8,128)}) custom-call(bf16[2,1024,2048]{2,1,0:T(8,128)(2,1)} %bitcast.247, bf16[256,2048]{1,0:T(8,128)(2,1)} %bitcast.300, bf16[2,1024,768]{2,1,0:T(8,128)(2,1)} %get-tuple-element.65.qkv_ref, f32[2,1024,128]{2,1,0:T(8,128)} %get-tuple-element.66.lse_ref, ...), custom_call_target="tpu_custom_call" | custom-call | flops 7516192768 | bytes 33554432 | tf_op jit(solution)/shard_map/attn_backward/pallas_call | solution.py:296
  389.8 29.0 %mlp_forward.1 = (bf16[2048,1024]{1,0:T(8,128)(2,1)}, bf16[2048,1024]{1,0:T(8,128)(2,1)}, bf16[2048,2048]{1,0:T(8,128)(2,1)}) custom-call(bf16[2048,2048]{1,0:T(8,128)(2,1)} %bitcast.242, bf16[2048,1792]{1,0:T(8,128)(2,1)} %bitcast.21.wq_ref.wk_ref.wv_ref.wu_ref, f32[1,1024]{1,0:T(1,128)} %bitcast.316, bf16[2048,1024]{1,0:T(8,128)(2,1)} %bitcast.37.wd_ref, ...), custom_call_target="tpu_custom_call" | custom-call | flops 19327352832 | bytes 50331648 | tf_op jit(solution)/shard_map/mlp_forward/pallas_call | solution.py:338
  418.8 33.1 %mlp_backward.1 = (bf16[2048,1024]{1,0:T(8,128)(2,1)}, f32[8,1024]{1,0:T(8,128)}, bf16[2048,2048]{1,0:T(8,128)(2,1)}) custom-call(bf16[2048,2048]{1,0:T(8,128)(2,1)} %bitcast.248, bf16[2048,1024]{1,0:T(8,128)(2,1)} %bitcast.37.wd_ref, bf16[2048,1024]{1,0:T(8,128)(2,1)} %get-tuple-element.64.slope_ref, bf16[2048,768]{1,0:T(8,128)(2,1)} %bitcast.317, ...), custom_call_target="tpu_custom_call" | custom-call | flops 23622320128 | bytes 50331648 | tf_op jit(solution)/shard_map/mlp_backward/pallas_call | solution.py:392
  467.3 7.4 convolution_convert_fusion.2
  477.8 11.5 %convolution_convert_fusion.1 = bf16[2048,1024]{1,0:T(8,128)(2,1)S(1)} fusion(bf16[2048,2048]{1,0:T(8,128)(2,1)S(1)} %bitcast.246, bf16[2048,1024]{1,0:T(8,128)(2,1)} %get-tuple-element.76), kind=kOutput, calls=%fused_computation.3 | convolution fusion | flops 8592031744 | bytes 16777216 | tf_op jit(solution)/shard_map/dot_general | solution.py:39
  495.1 9.6 %convolution_convert_fusion = bf16[2048,1024]{1,0:T(8,128)(2,1)S(1)} fusion(bf16[2048,2048]{1,0:T(8,128)(2,1)S(1)} %bitcast.252, bf16[2048,1024]{1,0:T(8,128)(2,1)S(1)} %copy-done.50), kind=kOutput, calls=%fused_computation.2 | convolution fusion | flops 8592031744 | bytes 16777216 | tf_op jit(solution)/shard_map/dot_general | solution.py:39
  536.6 18.9 %collective-permute-done.31 = bf16[1,256,2048]{2,1,0:T(8,128)(2,1)S(1)} collective-permute-done((bf16[1,256,2048]{2,1,0:T(8,128)(2,1)}, bf16[1,256,2048]{2,1,0:T(8,128)(2,1)S(1)}, u32[]{:S(2)}, u32[]{:S(2)}) %collective-permute-start.31) | collective-permute-done | bytes 1048608 | tf_op jit(solution)/shard_map/ppermute | solution.py:87
  570.9 8.7 %collective-permute-done.43 = bf16[1,256,2048]{2,1,0:T(8,128)(2,1)} collective-permute-done((bf16[1,256,2048]{2,1,0:T(8,128)(2,1)}, bf16[1,256,2048]{2,1,0:T(8,128)(2,1)}, u32[]{:S(2)}, u32[]{:S(2)}) %collective-permute-start.43) | collective-permute-done | bytes 1048608 | tf_op jit(solution)/shard_map/ppermute | solution.py:87
  585.2 28.3 %all-to-all-done.5 = bf16[4,64,768]{2,1,0:T(8,128)(2,1)S(1)} async-done(((bf16[4,64,768]{2,1,0:T(8,128)(2,1)}), bf16[4,64,768]{2,1,0:T(8,128)(2,1)S(1)}, u32[]{:S(2)}, u32[]{:S(2)}) %all-to-all-start.5) | async-done | bytes 393248 | tf_op jit(solution)/shard_map/all_to_all | solution.py:665
  628.1 45.1 %all-to-all-done.4.refs_0_ = bf16[4,64,768]{2,1,0:T(8,128)(2,1)S(1)} async-done(((bf16[4,64,768]{2,1,0:T(8,128)(2,1)}), bf16[4,64,768]{2,1,0:T(8,128)(2,1)S(1)}, u32[]{:S(2)}, u32[]{:S(2)}) %all-to-all-start.4) | async-done | bytes 393248 | tf_op jit(solution)/shard_map/all_to_all | solution.py:665
  742.4 8.1 %adam_columns.4 = (f32[64,16384]{1,0:T(8,128)}, f32[64,16384]{1,0:T(8,128)}, f32[64,16384]{1,0:T(8,128)}, f32[64,16384]{1,0:T(8,128)}) custom-call(s32[1]{0:T(128)} %bitcast.66.c_ref, bf16[4,64,1024]{2,1,0:T(8,128)(2,1)} %copy-done.20, bf16[4,64,1024]{2,1,0:T(8,128)(2,1)} %copy-done.35, f32[64,16384]{1,0:T(8,128)} %refs_2_.5, f32[64,16384]{1,0:T(8,128)} %refs_3_.5, ...), custom_call_target="tpu_custom_call" | custom-call | flops 15728640 | bytes 15728640 | tf_op jit(solution)/shard_map/adam_columns/pallas_call | solution.py:485
  751.3 10.2 %adam_columns.3 = (f32[64,8192]{1,0:T(8,128)}, f32[64,8192]{1,0:T(8,128)}, f32[64,8192]{1,0:T(8,128)}, f32[64,8192]{1,0:T(8,128)}, f32[64,128]{1,0:T(8,128)}) custom-call(s32[1]{0:T(128)} %bitcast.66.c_ref, bf16[4,64,768]{2,1,0:T(8,128)(2,1)} %copy-done.21, bf16[4,64,768]{2,1,0:T(8,128)(2,1)} %collective-permute-done.51.refs_1_, f32[64,8192]{1,0:T(8,128)} %refs_2_.3, ...), custom_call_target="tpu_custom_call" | custom-call | flops 11796480 | bytes 11796480 | tf_op jit(solution)/shard_map/adam_columns/pallas_call | solution.py:485
  763.5 7.8 %adam_columns.5 = (f32[64,16384]{1,0:T(8,128)}, f32[64,16384]{1,0:T(8,128)}, f32[64,16384]{1,0:T(8,128)}, f32[64,16384]{1,0:T(8,128)}, f32[64,128]{1,0:T(8,128)}) custom-call(s32[1]{0:T(128)} %bitcast.66.c_ref, bf16[4,64,1024]{2,1,0:T(8,128)(2,1)} %copy-done.17, ...), custom_call_target="tpu_custom_call", output_to_operand_aliasing={{0}: (8, {}), {1}: (9, {}), {2}: (10, {}), {3}: (11, {})} | custom-call | flops 15728640 | bytes 15728640 | tf_op jit(solution)/shard_map/adam_columns/pallas_call | solution.py:485
  (409 shorter events, 359.7 us)
Async XLA Ops:
  0.6 176.7 %collective-permute-start.34 = (bf16[1,256,2048]{2,1,0:T(8,128)(2,1)}, bf16[1,256,2048]{2,1,0:T(8,128)(2,1)}, u32[]{:S(2)}, u32[]{:S(2)}) collective-permute-start(bf16[1,256,2048]{2,1,0:T(8,128)(2,1)} %param.12), channel_id=1, source_target_pairs={{0,4},{1,5},{2,6},{3,7},{4,0},{5,1},{6,2},{7,3},{8,12},{9,13},{10,... | collective-permute-start | bytes 3145736 | tf_op jit(solution)/shard_map/ppermute | solution.py:87
  1.4 177.4 %collective-permute-start.35 = (bf16[1,256,2048]{2,1,0:T(8,128)(2,1)}, bf16[1,256,2048]{2,1,0:T(8,128)(2,1)}, u32[]{:S(2)}, u32[]{:S(2)}) collective-permute-start(bf16[1,256,2048]{2,1,0:T(8,128)(2,1)} %param.12), channel_id=1, source_target_pairs={{0,1},{1,2},{2,3},{3,0},{4,5},{5,6},{6,7},{7,4},{8,9},{9,10},{10,1... | collective-permute-start | bytes 3145736 | tf_op jit(solution)/shard_map/ppermute | solution.py:87
  14.5 134.7 %all-to-all-start.2 = ((bf16[4,64,1024]{2,1,0:T(8,128)(2,1)}), bf16[4,64,1024]{2,1,0:T(8,128)(2,1)}, u32[]{:S(2)}, u32[]{:S(2)}) async-start(bf16[4,64,1024]{2,1,0:T(8,128)(2,1)} %bitcast.293), calls=%async_computation.2 | async-start | bytes 1048576 | tf_op jit(solution)/shard_map/all_to_all | solution.py:589
  18.7 162.4 %collective-permute-start = (bf16[1,256,2048]{2,1,0:T(8,128)(2,1)S(1)}, bf16[1,256,2048]{2,1,0:T(8,128)(2,1)}, u32[]{:S(2)}, u32[]{:S(2)}) collective-permute-start(bf16[1,256,2048]{2,1,0:T(8,128)(2,1)S(1)} %copy-done.1), channel_id=1, source_target_pairs={{0,1},{1,2},{2,3},{3,0},{4,5},{5,6},{6,7},{7,4},{8,9},{9,10},{10,1... | collective-permute-start | bytes 3145736 | tf_op jit(solution)/shard_map/ppermute | solution.py:87
  21.7 49.1 %collective-permute-start.4 = (bf16[16,2048]{0,1:T(8,128)(2,1)}, bf16[16,2048]{0,1:T(8,128)(2,1)}, u32[]{:S(2)}, u32[]{:S(2)}) collective-permute-start(bf16[16,2048]{0,1:T(8,128)(2,1)} %constant_dynamic-update-slice_fusion.9), channel_id=1, source_target_pairs={{0,1},{1,0},{2,3},{3,2},{4,5},{5,4},{6,7},{7,6},{8,9},{9,8},{10,11... | collective-permute-start | bytes 196616 | tf_op jit(solution)/shard_map/ppermute | solution.py:99
  24.7 100.5 %collective-permute-start.26 = (bf16[64,2048]{1,0:T(8,128)(2,1)}, bf16[64,2048]{1,0:T(8,128)(2,1)}, u32[]{:S(2)}, u32[]{:S(2)}) collective-permute-start(bf16[64,2048]{1,0:T(8,128)(2,1)} %slice.121), channel_id=1, source_target_pairs={{0,0},{1,8},{2,16},{3,24},{4,4},{5,12},{6,20},{7,28},{8,1},{9,9},{... | collective-permute-start | bytes 786440 | tf_op jit(solution)/shard_map/ppermute | solution.py:608
  166.7 48.6 %all-to-all-start = ((bf16[4,64,1792]{2,1,0:T(8,128)(2,1)}), bf16[4,64,1792]{2,1,0:T(8,128)(2,1)S(1)}, u32[]{:S(2)}, u32[]{:S(2)}) async-start(bf16[4,64,1792]{2,1,0:T(8,128)(2,1)} %bitcast.230), calls=%async_computation | async-start | bytes 1835008 | tf_op jit(solution)/shard_map/all_to_all | solution.py:589
  181.1 50.0 %collective-permute-start.36 = (bf16[1,256,2048]{2,1,0:T(8,128)(2,1)}, bf16[1,256,2048]{2,1,0:T(8,128)(2,1)}, u32[]{:S(2)}, u32[]{:S(2)}) collective-permute-start(bf16[1,256,2048]{2,1,0:T(8,128)(2,1)} %collective-permute-done.35), channel_id=1, source_target_pairs={{0,4},{1,5},{2,6},{3,7},{4,0},{5,1},{6,2},{7,3},{8,12},{9,13},{10,... | collective-permute-start | bytes 3145736 | tf_op jit(solution)/shard_map/ppermute | solution.py:87
  181.4 51.5 %collective-permute-start.1 = (bf16[1,256,2048]{2,1,0:T(8,128)(2,1)}, bf16[1,256,2048]{2,1,0:T(8,128)(2,1)S(1)}, u32[]{:S(2)}, u32[]{:S(2)}) collective-permute-start(bf16[1,256,2048]{2,1,0:T(8,128)(2,1)} %collective-permute-done.refs_0_), channel_id=1, source_target_pairs={{0,1},{1,2},{2,3},{3,0},{4,5},{5,6},{6,7},{7,4},{8,9},{9,10},{10,1... | collective-permute-start | bytes 3145736 | tf_op jit(solution)/shard_map/ppermute | solution.py:87
  215.3 61.0 %all-to-all-start.1 = ((bf16[4,64,1792]{2,1,0:T(8,128)(2,1)}), bf16[4,64,1792]{2,1,0:T(8,128)(2,1)S(1)}, u32[]{:S(2)}, u32[]{:S(2)}) async-start(bf16[4,64,1792]{2,1,0:T(8,128)(2,1)} %copy-done.27), calls=%async_computation.1 | async-start | bytes 1835008 | tf_op jit(solution)/shard_map/all_to_all | solution.py:589
  276.3 49.2 %collective-permute-start.16 = (bf16[256,1792]{1,0:T(8,128)(2,1)S(1)}, bf16[256,1792]{1,0:T(8,128)(2,1)S(1)}, u32[]{:S(2)}, u32[]{:S(2)}) collective-permute-start(bf16[256,1792]{1,0:T(8,128)(2,1)S(1)} %bitcast.281), channel_id=1, source_target_pairs={{0,16},{1,17},{2,18},{3,19},{4,20},{5,21},{6,22},{7,23},{8,24},{9,... | collective-permute-start | bytes 2752520 | tf_op jit(solution)/shard_map/ppermute | solution.py:87
  276.3 49.2 %collective-permute-start.14 = (bf16[256,1792]{1,0:T(8,128)(2,1)}, bf16[256,1792]{1,0:T(8,128)(2,1)S(1)}, u32[]{:S(2)}, u32[]{:S(2)}) collective-permute-start(bf16[256,1792]{1,0:T(8,128)(2,1)} %copy-done.28), channel_id=1, source_target_pairs={{0,16},{1,17},{2,18},{3,19},{4,20},{5,21},{6,22},{7,23},{8,24},{9,... | collective-permute-start | bytes 2752520 | tf_op jit(solution)/shard_map/ppermute | solution.py:87
  296.6 74.6 %collective-permute-start.40 = (bf16[1,256,2048]{2,1,0:T(8,128)(2,1)}, bf16[1,256,2048]{2,1,0:T(8,128)(2,1)S(1)}, u32[]{:S(2)}, u32[]{:S(2)}) collective-permute-start(bf16[1,256,2048]{2,1,0:T(8,128)(2,1)} %collective-permute-done.39), channel_id=1, source_target_pairs={{0,4},{1,5},{2,6},{3,7},{4,0},{5,1},{6,2},{7,3},{8,12},{9,13},{10,... | collective-permute-start | bytes 3145736 | tf_op jit(solution)/shard_map/ppermute | solution.py:87
  457.3 48.9 %collective-permute-start.41 = (bf16[1,1024,2048]{2,1,0:T(8,128)(2,1)}, bf16[1,1024,2048]{2,1,0:T(8,128)(2,1)S(1)}, u32[]{:S(2)}, u32[]{:S(2)}) collective-permute-start(bf16[1,1024,2048]{2,1,0:T(8,128)(2,1)} %get-tuple-element.94), channel_id=1, source_target_pairs={{0,4},{1,5},{2,6},{3,7},{4,0},{5,1},{6,2},{7,3},{8,12},{9,13},{10,... | collective-permute-start | bytes 12582920 | tf_op jit(solution)/shard_map/ppermute | solution.py:87
  476.0 48.4 %collective-permute-start.48 = (bf16[256,768]{1,0:T(8,128)(2,1)}, bf16[256,768]{1,0:T(8,128)(2,1)}, u32[]{:S(2)}, u32[]{:S(2)}) collective-permute-start(bf16[256,768]{1,0:T(8,128)(2,1)} %get-tuple-element.111), channel_id=1, source_target_pairs={{0,16},{1,17},{2,18},{3,19},{4,20},{5,21},{6,22},{7,23},{8,24},{9,... | collective-permute-start | bytes 1179656 | tf_op jit(solution)/shard_map/ppermute | solution.py:87
  557.6 59.4 %collective-permute-start.32 = (bf16[1,256,2048]{2,1,0:T(8,128)(2,1)S(1)}, bf16[1,256,2048]{2,1,0:T(8,128)(2,1)}, u32[]{:S(2)}, u32[]{:S(2)}) collective-permute-start(bf16[1,256,2048]{2,1,0:T(8,128)(2,1)S(1)} %fusion.13), channel_id=1, source_target_pairs={{0,1},{1,2},{2,3},{3,0},{4,5},{5,6},{6,7},{7,4},{8,9},{9,10},{10,1... | collective-permute-start | bytes 3145736 | tf_op jit(solution)/shard_map/ppermute | solution.py:87
  563.0 50.5 %all-to-all-start.5 = ((bf16[4,64,768]{2,1,0:T(8,128)(2,1)}), bf16[4,64,768]{2,1,0:T(8,128)(2,1)S(1)}, u32[]{:S(2)}, u32[]{:S(2)}) async-start(bf16[4,64,768]{2,1,0:T(8,128)(2,1)} %bitcast.78), calls=%async_computation.5 | async-start | bytes 786432 | tf_op jit(solution)/shard_map/all_to_all | solution.py:665
  567.8 58.3 %collective-permute-start.71 = (bf16[256,1024]{1,0:T(8,128)(2,1)}, bf16[256,1024]{1,0:T(8,128)(2,1)}, u32[]{:S(2)}, u32[]{:S(2)}) collective-permute-start(bf16[256,1024]{1,0:T(8,128)(2,1)} %get-tuple-element.99), channel_id=1, source_target_pairs={{0,16},{1,17},{2,18},{3,19},{4,20},{5,21},{6,22},{7,23},{8,24},{9,... | collective-permute-start | bytes 1572872 | tf_op jit(solution)/shard_map/ppermute | solution.py:87
  613.5 59.7 %all-to-all-start.4 = ((bf16[4,64,768]{2,1,0:T(8,128)(2,1)}), bf16[4,64,768]{2,1,0:T(8,128)(2,1)S(1)}, u32[]{:S(2)}, u32[]{:S(2)}) async-start(bf16[4,64,768]{2,1,0:T(8,128)(2,1)} %bitcast.73), calls=%async_computation.4 | async-start | bytes 786432 | tf_op jit(solution)/shard_map/all_to_all | solution.py:665
  617.0 63.5 %collective-permute-start.44 = (bf16[1,256,2048]{2,1,0:T(8,128)(2,1)}, bf16[1,256,2048]{2,1,0:T(8,128)(2,1)S(1)}, u32[]{:S(2)}, u32[]{:S(2)}) collective-permute-start(bf16[1,256,2048]{2,1,0:T(8,128)(2,1)} %fusion.10), channel_id=1, source_target_pairs={{0,1},{1,2},{2,3},{3,0},{4,5},{5,6},{6,7},{7,4},{8,9},{9,10},{10,1... | collective-permute-start | bytes 3145736 | tf_op jit(solution)/shard_map/ppermute | solution.py:87
  621.9 61.5 %collective-permute-start.33 = (bf16[1,256,2048]{2,1,0:T(8,128)(2,1)}, bf16[1,256,2048]{2,1,0:T(8,128)(2,1)}, u32[]{:S(2)}, u32[]{:S(2)}) collective-permute-start(bf16[1,256,2048]{2,1,0:T(8,128)(2,1)} %fusion.12), channel_id=1, source_target_pairs={{0,1},{1,2},{2,3},{3,0},{4,5},{5,6},{6,7},{7,4},{8,9},{9,10},{10,1... | collective-permute-start | bytes 3145736 | tf_op jit(solution)/shard_map/ppermute | solution.py:87
  626.1 90.8 %collective-permute-start.58 = (bf16[64,2048]{1,0:T(8,128)(2,1)}, bf16[64,2048]{1,0:T(8,128)(2,1)}, u32[]{:S(2)}, u32[]{:S(2)}) collective-permute-start(bf16[64,2048]{1,0:T(8,128)(2,1)} %get-tuple-element.123), channel_id=1, source_target_pairs={{0,16},{1,17},{2,18},{3,19},{4,20},{5,21},{6,22},{7,23},{8,24},{9,... | collective-permute-start | bytes 786440 | tf_op jit(solution)/shard_map/ppermute | solution.py:87
  626.6 93.0 %collective-permute-start.61 = (bf16[256,1024]{1,0:T(8,128)(2,1)}, bf16[256,1024]{1,0:T(8,128)(2,1)}, u32[]{:S(2)}, u32[]{:S(2)}) collective-permute-start(bf16[256,1024]{1,0:T(8,128)(2,1)} %get-tuple-element.108), channel_id=1, source_target_pairs={{0,8},{1,9},{2,10},{3,11},{4,12},{5,13},{6,14},{7,15},{8,0},{9,1},... | collective-permute-start | bytes 1572872 | tf_op jit(solution)/shard_map/ppermute | solution.py:87
  627.3 75.8 %collective-permute-start.68 = (bf16[256,1024]{1,0:T(8,128)(2,1)}, bf16[256,1024]{1,0:T(8,128)(2,1)}, u32[]{:S(2)}, u32[]{:S(2)}) collective-permute-start(bf16[256,1024]{1,0:T(8,128)(2,1)} %get-tuple-element.102), channel_id=1, source_target_pairs={{0,8},{1,9},{2,10},{3,11},{4,12},{5,13},{6,14},{7,15},{8,0},{9,1},... | collective-permute-start | bytes 1572872 | tf_op jit(solution)/shard_map/ppermute | solution.py:87
  (116 other events, 2412.3 us)

commit v2 on v1

v2 whole, which is shorter than its diff:
```python
from functools import partial

import jax
import jax.numpy as jnp
from jax import lax
from jax.experimental import pallas as pl
from jax.experimental.pallas import tpu as pltpu
from jax.sharding import PartitionSpec as P

HEADS = 8
STEP = 10
AXES = ("dp", "seq")
LANES = 128
VMEM_LIMIT = 56 * 2**20

norm_eps = 1e-05
masked_value = -1e30
beta_first = 0.9
beta_second = 0.95
adam_eps = 1e-08
decay_rate = 0.01
rate_attention = 0.06
rate_mlp = 0.02
rate_vector = 0.2

f32 = jnp.float32
bf16 = jnp.bfloat16


def normalize(values):
    row_mean = jnp.mean(values, axis=-1, keepdims=True)
    centred = values - row_mean
    spread = jnp.mean(centred * centred, axis=-1, keepdims=True)
    scaling = lax.rsqrt(spread + norm_eps)
    return (centred * scaling, scaling)


def dot(left_op, right_op, left_dim=1, right_dim=0):
    return lax.dot_general(
        left_op,
        right_op,
        (((left_dim,), (right_dim,)), ((), ())),
        preferred_element_type=f32,
    )


def adamw(master, gradient, first_old, second_old, step_rate):
    first_new = beta_first * first_old + (1.0 - beta_first) * gradient
    second_new = beta_second * second_old + (1.0 - beta_second) * gradient * gradient
    first_hat = first_new / (1.0 - beta_first**STEP)
    second_hat = second_new / (1.0 - beta_second**STEP)
    updated = master - step_rate * (
        first_hat / (jnp.sqrt(second_hat) + adam_eps) + decay_rate * master
    )
    return (gradient, updated, first_new, second_new)


def params(cost=None, **kw):
    return dict(
        compiler_params=pltpu.CompilerParams(vmem_limit_bytes=VMEM_LIMIT, **kw),
        cost_estimate=cost and pl.CostEstimate(flops=cost[0] // 1000 + 1, bytes_accessed=cost[1] // 1000 + 1, transcendentals=0),
    )


class Layout:
    def __init__(self, nd, nz):
        self.nd, self.nz = nd, nz
        self.pair = HEADS // nz
        self.groups = nd // self.pair
        self.dp = lax.axis_index("dp")
        self.z = lax.axis_index("seq")
        self.g = self.dp // self.pair
        self.c = self.dp % self.pair
        self.t = self.z * self.pair + self.c

    def perm(self, target):
        pairs = []
        for dp in range(self.nd):
            for z in range(self.nz):
                goal = target(dp // self.pair, dp % self.pair, z)
                if goal is not None:
                    g, c, s = goal
                    pairs.append((dp * self.nz + z, (g * self.pair + c) * self.nz + s))
        return pairs

    def hop(self, value, target):
        return lax.ppermute(value, AXES, self.perm(target))

    def group_hop(self, value, bit):
        return self.hop(value, lambda g, c, z: (g ^ bit, c, z))

    def core_hop(self, value, r):
        return self.hop(value, lambda g, c, z: (g, c ^ r, z))

    def ring(self, value):
        return self.hop(value, lambda g, c, z: (g, c, (z + 1) % self.nz))

    def flat_hop(self, value, bit):
        return lax.ppermute(value, AXES, [(i, i ^ bit) for i in range(self.nd * self.nz)])

    def head_owner_perm(self):
        pairs = []
        for r in range(self.nd * self.nz):
            head, quarter = r // self.groups, r % self.groups
            s, c = head // self.pair, head % self.pair
            pairs.append((r, (quarter * self.pair + c) * self.nz + s))
        return pairs


def after(values, *deps):
    flat, tree = jax.tree.flatten((values, deps))
    return jax.tree.unflatten(tree, lax.optimization_barrier(flat))[0]


def join(*values):
    return after(values)


def bits_of(count, descending):
    bits = []
    bit = 1
    while bit < count:
        bits.append(bit)
        bit *= 2
    return bits[::-1] if descending else bits


class GroupGather:
    def __init__(self, lay, block, descending):
        self.lay = lay
        self.rows = block.shape[0]
        self.held = {0: (block, 0)}
        self.rounds = [[] for _ in bits_of(lay.groups, False)]
        known = [0]
        for bit in bits_of(lay.groups, descending):
            for m in list(known):
                self.rounds[bin(m).count("1")].append((m, bit))
                known.append(m ^ bit)

    def block(self, m):
        array, first = self.held[m]
        return array[first : first + self.rows]

    def send(self, depth):
        if depth < len(self.rounds):
            for m, bit in self.rounds[depth]:
                self.held[m ^ bit] = (self.lay.group_hop(self.block(m), bit), 0)

    @staticmethod
    def send_first(halves):
        lay = halves[0].lay
        stack = jnp.concatenate([h.block(0) for h in halves])
        for bit in bits_of(lay.groups, False):
            got = lay.group_hop(stack, bit)
            first = 0
            for h in halves:
                h.held[bit] = (got, first)
                first += h.rows

    @property
    def state(self):
        return {m: v for m, (v, _) in self.held.items()}

    @state.setter
    def state(self, state):
        for m, v in state.items():
            self.held[m] = (v, self.held[m][1])

    def rest(self, depth):
        while depth < len(self.rounds):
            self.send(depth)
            depth += 1
        return self.held


class GroupScatter:
    def __init__(self, lay, keep, send, descending):
        self.lay = lay
        self.keep, self.send = keep, send
        self.bits = bits_of(lay.groups, descending)
        self.at = 0

    @staticmethod
    def member(lay, index, descending):
        bits = bits_of(lay.groups, descending)
        return sum(bit for j, bit in enumerate(bits) if index >> (len(bits) - 1 - j) & 1)

    @property
    def state(self):
        return (self.keep, self.send)

    @state.setter
    def state(self, state):
        self.keep, self.send = state

    def step(self):
        if self.at < len(self.bits):
            self.send = self.lay.group_hop(self.send, self.bits[self.at])
            self.at += 1

    def fold(self):
        total = self.keep.astype(f32) + self.send.astype(f32)
        half = total.shape[0] // 2
        self.keep, self.send = total[:half], total[half:].astype(bf16)

    def result(self):
        return (self.keep.astype(f32) + self.send.astype(f32))[0]


def cast_kernel(c_ref, *refs):
    out_ref = refs[-1]
    at = 0
    for ref in refs[:-1]:
        out_ref[0, :, at : at + ref.shape[1]] = ref[...].astype(bf16)
        at += ref.shape[1]


def prepare(lay, r, sources):
    rows, pair, nz = sources[0][0].shape[0], lay.pair, lay.nz

    def spec(first, width):
        if first is None:
            return pl.BlockSpec((rows, width), lambda z, c: (0, 0))
        return pl.BlockSpec((rows, width), lambda z, c: (0, first + z * pair + (c[0] ^ r)))

    total = sum(width for _, _, width in sources)
    return pl.pallas_call(
        cast_kernel,
        grid_spec=pltpu.PrefetchScalarGridSpec(
            num_scalar_prefetch=1,
            grid=(nz,),
            in_specs=[spec(first, width) for _, first, width in sources],
            out_specs=pl.BlockSpec((1, rows, total), lambda z, c: (z, 0, 0)),
        ),
        out_shape=jax.ShapeDtypeStruct((nz, rows, total), bf16),
        name="prepare",
        **params((rows * total * nz, rows * total * nz * 6)),
    )(jnp.reshape(lay.c, (1,)).astype(jnp.int32), *[v for v, _, _ in sources])


def place_kernel(count, tile, slot_ref, *refs):
    out_ref, sems = refs[-2], refs[-1]
    here = pl.ds(pl.multiple_of(pl.program_id(0) * tile, tile), tile)

    def copy(i):
        return pltpu.make_async_copy(refs[i], out_ref.at[slot_ref[i], here], sems.at[i])

    for i in range(count):

        @pl.when(slot_ref[i] >= 0)
        def _(i=i):
            copy(i).start()

    for i in range(count):

        @pl.when(slot_ref[i] >= 0)
        def _(i=i):
            copy(i).wait()


def place(blocks, slots, rows, total, held=None):
    count = len(blocks)
    width = blocks[0][0].shape[1]
    tile = max(min(64, rows), rows // 2)
    operands = [v for v, _ in blocks] + ([] if held is None else [held])
    any_spec = pl.BlockSpec(memory_space=pl.ANY)
    return pl.pallas_call(
        partial(place_kernel, count, tile),
        grid_spec=pltpu.PrefetchScalarGridSpec(
            num_scalar_prefetch=1,
            grid=(rows // tile,),
            in_specs=[
                pl.BlockSpec(
                    (tile, width),
                    lambda i, slot, first=first, j=j: (
                        first // tile + jnp.where(slot[j] >= 0, i, 0),
                        0,
                    ),
                )
                for j, (_, first) in enumerate(blocks)
            ]
            + [any_spec] * (len(operands) - count),
            out_specs=any_spec,
            scratch_shapes=[pltpu.SemaphoreType.DMA((count,))],
        ),
        out_shape=jax.ShapeDtypeStruct((total, rows, width), blocks[0][0].dtype),
        input_output_aliases={} if held is None else {count + 1: 0},
        name="place",
        **params((count, 4 * count * rows * width)),
    )(jnp.stack([jnp.asarray(v, jnp.int32) for v in slots]), *operands)


def flip_kernel(in_ref, out_ref):
    out_ref[...] = in_ref[...].astype(f32).T


def last_columns(array):
    rows, total = array.shape
    return pl.pallas_call(
        flip_kernel,
        grid=(1,),
        in_specs=[pl.BlockSpec((rows, LANES), lambda i: (0, total // LANES - 1))],
        out_specs=pl.BlockSpec((LANES, rows), lambda i: (0, 0)),
        out_shape=jax.ShapeDtypeStruct((LANES, rows), f32),
        name="last_columns",
        **params(),
    )(array)


def block_order(lay):
    order = []
    for part in (1, 0):
        for r in range(lay.pair):
            for i in range(lay.groups // 2):
                m = GroupScatter.member(lay, part * (lay.groups // 2) + i, bool(r))
                order.append((lay.g ^ m) * lay.pair + (lay.c ^ r))
    return jnp.stack(order).astype(jnp.int32)


def write_block(half, outs, at, value):
    i = pl.program_id(0)
    for k, out in enumerate(outs):

        @pl.when(jnp.logical_and(i >= k * half, i < (k + 1) * half))
        def _(out=out):
            out[0, :, at : at + value.shape[1]] = value


def gradient_kernel(half, block_ref, left_ref, right_ref, *outs):
    write_block(half, outs, 0, dot(left_ref[...], right_ref[...], 0, 0).astype(bf16))


def folded_kernel(half, first, gain, rides, block_ref, x_ref, right_ref, sums_ref, w_ref, small_ref, *refs):
    others, outs = (refs[:2], refs[2:]) if rides else ((), refs[:-1])
    vec = small_ref[...].astype(f32)
    raw = dot(x_ref[...], right_ref[...], 0, 0)
    sums = sums_ref[0:1]
    grad = raw * vec[:, gain : gain + 1] + sums * vec[:, gain + 1 : gain + 2]
    write_block(half, outs, 0, grad.astype(bf16))
    w = w_ref[:, first : first + raw.shape[1]].astype(f32)
    lane = lax.broadcasted_iota(jnp.int32, vec.shape, 1)
    moment = jnp.sum(w * raw, axis=1, keepdims=True)
    plain = jnp.sum(w * sums, axis=1, keepdims=True)
    lanes = jnp.where(lane == gain, moment, jnp.where(lane == gain + 1, plain, 0.0))
    if rides:
        lanes = lanes + others[0][...] + others[1][...]
        write_block(half, outs, raw.shape[1], lanes.astype(bf16))
    else:
        refs[-1][...] = lanes


def gradient_call(lay, kernel, left, rights, by_rows, n, more=()):
    tokens, width = left.shape
    pair, half = lay.pair, lay.groups // 2
    rows = width // (lay.groups * pair)
    outs = 2 * pair

    def out_map(k):
        return lambda i, block: (jnp.clip(i - k * half, 0, half - 1), 0, 0)

    def row_map(column):
        return lambda i, block: (block[i], column)

    values = pl.pallas_call(
        partial(kernel, half),
        grid_spec=pltpu.PrefetchScalarGridSpec(
            num_scalar_prefetch=1,
            grid=(outs * half,),
            in_specs=[pl.BlockSpec((tokens, rows), lambda i, block: (0, block[i]))]
            + [pl.BlockSpec(v.shape, lambda i, block: (0, 0)) for v in rights]
            + [pl.BlockSpec((rows, size), row_map(column)) for _, size, column in by_rows],
            out_specs=[pl.BlockSpec((1, rows, n), out_map(k)) for k in range(outs)]
            + [pl.BlockSpec((rows, size), row_map(0)) for size in more],
        ),
        out_shape=[jax.ShapeDtypeStruct((half, rows, n), bf16)] * outs
        + [jax.ShapeDtypeStruct((width, size), f32) for size in more],
        name="gradient",
        **params((2 * tokens * width * n, 2 * (tokens * width + tokens * n + width * n))),
    )(block_order(lay), left, *rights, *[v for v, _, _ in by_rows])
    parts = [GroupScatter(lay, values[pair + r], values[r], bool(r)) for r in range(pair)]
    return (parts, *values[outs:])


def gradient(lay, left, right):
    return gradient_call(lay, gradient_kernel, left, [right], [], right.shape[1])[0]


def folded_gradient(lay, x, right, sums, w_qu, first, gain, others=()):
    total = w_qu.shape[1]
    by_rows = [(w_qu, total, 0), (w_qu, LANES, total // LANES - 1)]
    by_rows += [(v, LANES, 0) for v in others]
    rides = len(others) > 0

    def call(half, *refs):
        folded_kernel(half, first, gain, rides, *refs)

    n = right.shape[1] + (LANES if rides else 0)
    return gradient_call(lay, call, x, [right, sums], by_rows, n, () if rides else (LANES,))


def fold_kernel(*refs):
    count = len(refs) // 4
    for p in range(count):
        keep, got, next_keep, next_send = refs[p], refs[count + p], refs[2 * count + p], refs[3 * count + p]
        half = next_keep.shape[0]
        total = keep[...].astype(f32) + got[...].astype(f32)
        next_keep[...] = total[:half]
        next_send[...] = total[half:].astype(bf16)


def fold(parts):
    held, rows, n = parts[0].keep.shape
    half = held // 2
    tile = min(64, rows)
    full = pl.BlockSpec((held, tile, n), lambda i: (0, i, 0))
    part = pl.BlockSpec((half, tile, n), lambda i: (0, i, 0))
    count = len(parts)
    values = pl.pallas_call(
        fold_kernel,
        grid=(rows // tile,),
        in_specs=[full] * (2 * count),
        out_specs=[part] * (2 * count),
        out_shape=[jax.ShapeDtypeStruct((half, rows, n), f32)] * count
        + [jax.ShapeDtypeStruct((half, rows, n), bf16)] * count,
        name="fold",
        **params((held * rows * n, 8 * held * rows * n)),
    )(*[p.keep for p in parts], *[p.send for p in parts])
    for k, p in enumerate(parts):
        p.keep, p.send = values[k], values[count + k]


def blocks_kernel(count, *refs):
    out_ref = refs[-1]
    for p in range(count):
        out_ref[0, p] = (refs[p][0].astype(f32) + refs[count + p][0].astype(f32)).astype(bf16)


def final_blocks(parts, nz):
    _, total, n = parts[0].keep.shape
    rows, count = total // nz, len(parts)
    return pl.pallas_call(
        partial(blocks_kernel, count),
        grid=(nz,),
        in_specs=[pl.BlockSpec((1, rows, n), lambda i: (0, i, 0))] * (2 * count),
        out_specs=pl.BlockSpec((1, count, rows, n), lambda i: (i, 0, 0, 0)),
        out_shape=jax.ShapeDtypeStruct((nz, count, rows, n), bf16),
        name="final_blocks",
        **params((count * total * n, 8 * count * total * n)),
    )(*[p.keep for p in parts], *[p.send for p in parts])


def chunk_kernel(count, ways, slot_ref, *refs):
    for k in range(ways):

        @pl.when(slot_ref[k] >= 0)
        def _(k=k):
            total = sum(refs[k * count + p][...].astype(f32) for p in range(count))
            out = refs[-ways + k]
            out[...] = total.astype(out.dtype)


def chunk_sums(parts, slots, received):
    count, _, span, width = parts[0].shape
    tile = min(span, 128)
    ways = len(slots)

    def whole(k):
        return lambda i, slot: (0, jnp.where(slot[k] >= 0, i, 0), 0)

    def part(k):
        return lambda i, slot: (0, jnp.maximum(slot[k], 0), jnp.where(slot[k] >= 0, i, 0), 0)

    in_specs, operands = [], []
    for k in range(ways):
        for p in parts:
            in_specs.append(pl.BlockSpec((count, None, tile, width), part(k)))
            operands.append(p)
        if received:
            in_specs.append(pl.BlockSpec((count, tile, width), whole(k)))
            operands.append(received[k])
    shape = jax.ShapeDtypeStruct((count, span, width), bf16)
    return pl.pallas_call(
        partial(chunk_kernel, len(operands) // ways, ways),
        grid_spec=pltpu.PrefetchScalarGridSpec(
            num_scalar_prefetch=1,
            grid=(span // tile,),
            in_specs=in_specs,
            out_specs=[pl.BlockSpec((count, tile, width), whole(k)) for k in range(ways)],
        ),
        out_shape=[shape] * ways,
        name="chunk_sums",
        **params((8 * count * span * width, 16 * count * span * width)),
    )(jnp.stack(slots).astype(jnp.int32), *operands)


def turn(values, cosine, low_sine, high_sine, quarter):
    head = values[:, :LANES]
    turned = (
        head * cosine
        + pltpu.roll(head, LANES - quarter, 1) * low_sine
        + pltpu.roll(head, quarter, 1) * high_sine
    )
    return jnp.concatenate([turned, values[:, LANES:]], axis=1)


def piece_kernel(pair, places, quarter, pos_ref, *refs):
    x_refs, refs = refs[: pair * places], refs[pair * places :]
    for p in range(places):

        @pl.when(pl.program_id(1) == p)
        def _(p=p):
            piece_rows(pair, quarter, x_refs[p * pair : (p + 1) * pair], refs)


def piece_rows(pair, quarter, x_refs, refs):
    vec_ref, w_ref, qkv_bias_ref, up_bias_ref, tab_ref = refs[:5]
    x_out, qkv_out, g_out, slope_out = refs[-4:]
    tile = x_refs[0].shape[1]
    unit, wide = g_out.shape[-1], qkv_out.shape[-1]
    hd = wide // 3
    x = jnp.concatenate([ref[0].astype(f32) for ref in x_refs])
    normed, _ = normalize(x)
    a = (normed * vec_ref[0:1] + vec_ref[1:2]).astype(bf16)
    m = (normed * vec_ref[2:3] + vec_ref[3:4]).astype(bf16)
    cosine, low_sine, high_sine = (jnp.concatenate([tab_ref[k]] * pair) for k in range(3))

    def put(out, at, value):
        value = value.astype(bf16)
        for r in range(pair):
            out[r, 0, 0, :, at : at + value.shape[1]] = value[r * tile : (r + 1) * tile]

    put(x_out, 0, normed)
    for j in range(3):
        part = dot(a, w_ref[:, unit + j * hd : unit + (j + 1) * hd])
        part = part + qkv_bias_ref[0:1, j * hd : (j + 1) * hd]
        put(qkv_out, j * hd, turn(part, cosine, low_sine, high_sine, quarter) if j < 2 else part)
    u = dot(m, w_ref[:, :unit]) + up_bias_ref[0:1]
    half = 0.5 * (1.0 + lax.erf(u * (0.5**0.5)))
    put(g_out, 0, u * half)
    put(slope_out, 0, half + u * (jnp.exp(-0.5 * u * u) * 0.3989422804014327))


def piece_forward(lay, pieces, where, vec, w_qu, qkv_bias, up_bias, tables, held):
    count, span, width = pieces[0].shape
    pair, nz, places = lay.pair, lay.nz, len(where)
    unit, wide = up_bias.shape[1], qkv_bias.shape[1]
    tile = min(span, 128)
    steps = span // tile

    def out(n):
        return (
            jax.ShapeDtypeStruct((pair, count, nz, span, n), bf16),
            pl.BlockSpec((pair, 1, 1, tile, n), lambda i, p, j, pos: (0, i, pos[p], j, 0)),
        )

    def whole(v):
        return pl.BlockSpec(v.shape, lambda i, p, j, pos: (0,) * v.ndim)

    def row_map(q):
        return lambda i, p, j, pos: (i, jnp.where(p == q, j, jnp.where(p < q, 0, steps - 1)), 0)

    outs = [out(n) for n in (width, wide, unit, unit)]
    in_specs = [pl.BlockSpec((1, tile, width), row_map(q)) for q in range(places) for _ in range(pair)]
    in_specs += [whole(v) for v in (vec, w_qu, qkv_bias, up_bias)]
    in_specs += [pl.BlockSpec((3, tile, LANES), lambda i, p, j, pos: (0, pos[p] * steps + j, 0))]
    in_specs += [pl.BlockSpec(memory_space=pl.ANY)] * len(held)
    tokens = pair * places * count * span
    return pl.pallas_call(
        partial(piece_kernel, pair, places, wide // 24),
        grid_spec=pltpu.PrefetchScalarGridSpec(
            num_scalar_prefetch=1,
            grid=(count, places, steps),
            in_specs=in_specs,
            out_specs=[o[1] for o in outs],
        ),
        out_shape=[o[0] for o in outs],
        input_output_aliases={pair * places + 6 + k: k for k in range(len(held))},
        name="piece_forward",
        **params((2 * tokens * width * (unit + wide), 12 * tokens * width)),
    )(
        jnp.stack(where).astype(jnp.int32),
        *pieces,
        vec,
        w_qu,
        qkv_bias,
        up_bias,
        tables,
        *held,
    )


def attn_fwd_kernel(scale, tile, qkv_ref, o_ref, lse_ref):
    length, hd = o_ref.shape[1:]
    for i in range(length // tile):
        end = (i + 1) * tile
        q_i = qkv_ref[0, i * tile : end, :hd]
        scores = dot(q_i, qkv_ref[0, :end, hd : 2 * hd], 1, 1) * scale
        row = lax.broadcasted_iota(jnp.int32, scores.shape, 0) + i * tile
        col = lax.broadcasted_iota(jnp.int32, scores.shape, 1)
        scores = jnp.where(col <= row, scores, masked_value)
        row_max = jnp.max(scores, axis=1, keepdims=True)
        terms = jnp.exp(scores - row_max)
        row_sum = jnp.sum(terms, axis=1, keepdims=True)
        probs = (terms / row_sum).astype(bf16)
        o_ref[0, i * tile : end] = dot(probs, qkv_ref[0, :end, 2 * hd :]).astype(bf16)
        lse_ref[0, i * tile : end] = jnp.broadcast_to(row_max + jnp.log(row_sum), (tile, LANES))


def attn_forward(qkv, scale):
    seqs, length, wide = qkv.shape
    hd = wide // 3
    return pl.pallas_call(
        partial(attn_fwd_kernel, scale, min(256, length)),
        grid=(seqs,),
        in_specs=[pl.BlockSpec((1, length, wide), lambda s: (s, 0, 0))],
        out_specs=[
            pl.BlockSpec((1, length, hd), lambda s: (s, 0, 0)),
            pl.BlockSpec((1, length, LANES), lambda s: (s, 0, 0)),
        ],
        out_shape=[
            jax.ShapeDtypeStruct((seqs, length, hd), bf16),
            jax.ShapeDtypeStruct((seqs, length, LANES), f32),
        ],
        name="attn_forward",
        **params((4 * seqs * length * length * hd, 8 * seqs * length * wide)),
    )(qkv)


def attn_bwd_kernel(quarter, scale, tile, dy_ref, wo_ref, qkv_ref, lse_ref, tab_ref, dp_ref, sum_ref, do_s, dk_s, dv_s):
    length = dy_ref.shape[1]
    hd = wo_ref.shape[0]
    cosine, low_sine, high_sine = tab_ref[0], -tab_ref[1], -tab_ref[2]
    do_s[...] = dot(dy_ref[0], wo_ref[...], 1, 1).astype(bf16)
    steps = length // tile
    for i in reversed(range(steps)):
        end = (i + 1) * tile
        q_i = qkv_ref[0, i * tile : end, :hd]
        k = qkv_ref[0, :end, hd : 2 * hd]
        do_i = do_s[i * tile : end]
        scores = dot(q_i, k, 1, 1) * scale
        row = lax.broadcasted_iota(jnp.int32, scores.shape, 0) + i * tile
        col = lax.broadcasted_iota(jnp.int32, scores.shape, 1)
        probs = jnp.where(col <= row, jnp.exp(scores - lse_ref[0, i * tile : end, 0:1]), 0.0)
        probs_grad = dot(do_i, qkv_ref[0, :end, 2 * hd :], 1, 1)
        row_dot = jnp.sum(probs * probs_grad, axis=1, keepdims=True)
        score_grad = (probs * (probs_grad - row_dot)).astype(bf16)
        dq = dot(score_grad, k) * scale
        dp_ref[0, i * tile : end, :hd] = turn(
            dq,
            cosine[i * tile : end],
            low_sine[i * tile : end],
            high_sine[i * tile : end],
            quarter,
        ).astype(bf16)
        dk = dot(score_grad, q_i, 0, 0)
        dv = dot(probs.astype(bf16), do_i, 0, 0)
        if i == steps - 1:
            dk_s[...] = dk
            dv_s[...] = dv
        else:
            dk_s[:end] += dk
            dv_s[:end] += dv
    dp_ref[0, :, hd : 2 * hd] = turn(
        dk_s[...] * scale, cosine, low_sine, high_sine, quarter
    ).astype(bf16)
    dp_ref[0, :, 2 * hd :] = dv_s[...].astype(bf16)
    total = jnp.sum(dp_ref[0].astype(f32), axis=0, keepdims=True)
    sum_ref[0] = jnp.broadcast_to(total, sum_ref.shape[1:])


def attn_backward(dy, w_out, qkv, lse, tables, scale):
    seqs, length, width = dy.shape
    hd = w_out.shape[0]
    flops = 2 * seqs * length * (hd * width + 5 * length * hd)
    return pl.pallas_call(
        partial(attn_bwd_kernel, hd // 8, scale, min(256, length)),
        grid=(seqs,),
        in_specs=[
            pl.BlockSpec((1, length, width), lambda s: (s, 0, 0)),
            pl.BlockSpec(w_out.shape, lambda s: (0, 0)),
            pl.BlockSpec((1, length, 3 * hd), lambda s: (s, 0, 0)),
            pl.BlockSpec((1, length, LANES), lambda s: (s, 0, 0)),
            pl.BlockSpec(tables.shape, lambda s: (0, 0, 0)),
        ],
        out_specs=[
            pl.BlockSpec((1, length, 3 * hd), lambda s: (s, 0, 0)),
            pl.BlockSpec((1, 8, 3 * hd), lambda s: (s, 0, 0)),
        ],
        out_shape=[
            jax.ShapeDtypeStruct((seqs, length, 3 * hd), bf16),
            jax.ShapeDtypeStruct((seqs, 8, 3 * hd), f32),
        ],
        scratch_shapes=[
            pltpu.VMEM((length, hd), bf16),
            pltpu.VMEM((length, hd), f32),
            pltpu.VMEM((length, hd), f32),
        ],
        name="attn_backward",
        **params((flops, 8 * seqs * length * width)),
    )(dy, w_out, qkv, lse, tables)


def output_kernel(g_ref, wd_ref, o_ref, wo_ref, out_ref):
    total = dot(g_ref[...], wd_ref[...], 1, 1) + dot(o_ref[...], wo_ref[...])
    out_ref[...] = total.astype(bf16)


def output_forward(g, w_down, o, w_out, tile, part, parts):
    tokens, unit = g.shape[0] // parts, g.shape[1]
    width, hd = w_down.shape[0], o.shape[1]
    first = part * tokens // tile
    return pl.pallas_call(
        output_kernel,
        grid=(tokens // tile,),
        in_specs=[
            pl.BlockSpec((tile, unit), lambda i: (first + i, 0)),
            pl.BlockSpec(w_down.shape, lambda i: (0, 0)),
            pl.BlockSpec((tile, hd), lambda i: (first + i, 0)),
            pl.BlockSpec(w_out.shape, lambda i: (0, 0)),
        ],
        out_specs=pl.BlockSpec((tile, width), lambda i: (i, 0)),
        out_shape=jax.ShapeDtypeStruct((tokens, width), bf16),
        name="output_forward",
        **params((2 * tokens * width * (unit + hd), 8 * tokens * width)),
    )(g, w_down, o, w_out)


def hidden_kernel(dy_ref, wd_ref, slope_ref, du_ref, sum_ref):
    dg = dot(dy_ref[...], wd_ref[...])
    du_ref[...] = (dg * slope_ref[...].astype(f32)).astype(bf16)
    total = jnp.sum(du_ref[...].astype(f32), axis=0, keepdims=True)
    total = jnp.broadcast_to(total, sum_ref.shape)

    @pl.when(pl.program_id(0) == 0)
    def _():
        sum_ref[...] = total

    @pl.when(pl.program_id(0) > 0)
    def _():
        sum_ref[...] += total


def hidden_backward(dy, w_down, slope, tile):
    tokens, width = dy.shape
    unit = w_down.shape[1]
    return pl.pallas_call(
        hidden_kernel,
        grid=(tokens // tile,),
        in_specs=[
            pl.BlockSpec((tile, width), lambda i: (i, 0)),
            pl.BlockSpec(w_down.shape, lambda i: (0, 0)),
            pl.BlockSpec((tile, unit), lambda i: (i, 0)),
        ],
        out_specs=[
            pl.BlockSpec((tile, unit), lambda i: (i, 0)),
            pl.BlockSpec((8, unit), lambda i: (0, 0)),
        ],
        out_shape=[
            jax.ShapeDtypeStruct((tokens, unit), bf16),
            jax.ShapeDtypeStruct((8, unit), f32),
        ],
        name="hidden_backward",
        **params((2 * tokens * width * unit, 6 * tokens * width)),
    )(dy, w_down, slope)


def input_kernel(hd, du_ref, dp_ref, wu_ref, wq_ref, wk_ref, wv_ref, vec_ref, z_ref):
    da = (
        dot(dp_ref[:, :hd], wq_ref[...], 1, 1)
        + dot(dp_ref[:, hd : 2 * hd], wk_ref[...], 1, 1)
        + dot(dp_ref[:, 2 * hd :], wv_ref[...], 1, 1)
    )
    dm = dot(du_ref[...], wu_ref[...], 1, 1)
    z_ref[...] = (da * vec_ref[0:1] + dm * vec_ref[2:3]).astype(bf16)


def input_backward(du, dp, w_qu, vec, tile, seq, seqs):
    tokens, unit = du.shape
    width, hd = w_qu.shape[0], dp.shape[1] // 3
    first = unit // hd
    steps = tokens // seqs // tile
    flops = 2 * tokens // seqs * width * (unit + 3 * hd)
    return pl.pallas_call(
        partial(input_kernel, hd),
        grid=(steps,),
        in_specs=[
            pl.BlockSpec((tile, unit), lambda i: (seq * steps + i, 0)),
            pl.BlockSpec((tile, 3 * hd), lambda i: (seq * steps + i, 0)),
            pl.BlockSpec((width, unit), lambda i: (0, 0)),
        ]
        + [pl.BlockSpec((width, hd), lambda i, j=j: (0, first + j)) for j in range(3)]
        + [pl.BlockSpec(vec.shape, lambda i: (0, 0))],
        out_specs=pl.BlockSpec((tile, width), lambda i: (i, 0)),
        out_shape=jax.ShapeDtypeStruct((tokens // seqs, width), bf16),
        name="input_backward",
        **params((flops, 12 * tokens // seqs * width)),
    )(du, dp, w_qu, w_qu, w_qu, w_qu, vec)


def adam_kernel(pair, places, rate, c_ref, *refs):
    g_refs, (w_ref, m_ref, v_ref), outs = refs[:pair], refs[pair : pair + 3], refs[-4:]
    pieces = []
    for z in range(places):
        parts = [ref[z].astype(f32) for ref in g_refs]
        if pair == 2:
            swapped = c_ref[0] == 1
            parts = [jnp.where(swapped, parts[1], parts[0]), jnp.where(swapped, parts[0], parts[1])]
        pieces += parts
    grad = pieces[0] if len(pieces) == 1 else jnp.concatenate(pieces, axis=1)
    result = adamw(w_ref[...], grad, m_ref[...], v_ref[...], rate)
    for ref, value in zip(outs, result, strict=True):
        ref[...] = value


def adam_columns(lay, rate, parts, at, piece, state, start, kinds, held):
    nz, rows, _ = parts[0].shape
    pair = len(parts)
    total = state[0].shape[1]
    places = max(1, min(nz, 2048 // (pair * piece)))
    wide = places * pair * piece
    steps = nz // places
    first = start // wide

    w_spec = pl.BlockSpec((rows, wide), lambda j, z, c: (0, first + j * steps + z))
    g_spec = pl.BlockSpec((places, rows, piece), lambda j, z, c: (z, 0, at // piece + j))
    operands = list(parts) + list(state) + list(held)
    return pl.pallas_call(
        partial(adam_kernel, pair, places, rate),
        grid_spec=pltpu.PrefetchScalarGridSpec(
            num_scalar_prefetch=1,
            grid=(kinds, steps),
            in_specs=[g_spec] * pair
            + [w_spec] * 3
            + [pl.BlockSpec(memory_space=pl.ANY)] * len(held),
            out_specs=[w_spec] * 4,
        ),
        out_shape=[jax.ShapeDtypeStruct((rows, total), f32)] * 4,
        input_output_aliases={1 + pair + 3 + k: k for k in range(len(held))},
        name="adam_columns",
        **params((30 * rows * kinds * piece * HEADS, 30 * rows * kinds * piece * HEADS)),
    )(jnp.reshape(lay.c, (1,)).astype(jnp.int32), *operands)


class LineGather:
    def __init__(self, lay, own):
        self.lay = lay
        self.up = self.down = own
        self.fresh = [(own, lay.z, lambda z: True)]
        self.todo = []
        self.out = None
        self.count = own.shape[0]

    def step(self, k):
        lay, n = self.lay, self.lay.nz
        self.up = lay.hop(self.up, lambda g, c, z: (g, c, z + 1) if k - 1 <= z < n - 1 else None)
        self.down = lay.hop(self.down, lambda g, c, z: (g, c, z - 1) if 1 <= z <= n - k else None)
        self.fresh.append((self.up, lay.z - k, lambda z: z >= k))
        self.fresh.append((self.down, lay.z + k, lambda z: z + k < n))

    def cross(self, keep=0):
        lay = self.lay
        due = len(self.fresh) - keep
        now, self.fresh = self.fresh[:due], self.fresh[due:]
        for piece, where, valid in now:
            ok = jnp.logical_and(where >= 0, where < lay.nz)
            for r in range(lay.pair):
                got = piece
                if r:
                    got = lay.hop(piece, lambda g, c, z: (g, c ^ r, z) if valid(z) else None)
                for s in range(self.count):
                    slot = (r * self.count + s) * lay.nz + where
                    self.todo.append((got[s], jnp.where(ok, slot, -1)))

    @property
    def state(self):
        return (self.up, self.down, [v[0] for v in self.fresh], [v for v, _ in self.todo], self.out)

    @state.setter
    def state(self, state):
        self.up, self.down, fresh, blocks, self.out = state
        self.fresh = [(v,) + w[1:] for v, w in zip(fresh, self.fresh)]
        self.todo = [(v, w) for v, (_, w) in zip(blocks, self.todo)]

    def flush(self, keep=0):
        due = len(self.todo) - keep
        now, self.todo = self.todo[:due], self.todo[due:]
        total = self.lay.pair * self.lay.nz * self.count
        blocks, slots = [(v, 0) for v, _ in now], [w for _, w in now]
        self.out = place(blocks, slots, blocks[0][0].shape[0], total, self.out)
        return self.out


class SeqScatter:
    def __init__(self, lay, parts, count):
        _, length, width = parts[0].shape
        total = sum(p.astype(f32) for p in parts).astype(bf16)
        self.state = total.reshape(count, lay.nz, length // lay.nz, width)

    def send(self):
        self.state = lax.all_to_all(self.state, "seq", 1, 1, tiled=True)

    def result(self):
        return jnp.sum(self.state.astype(f32), axis=1)


def body(
    inputs,
    cotangent,
    attn_params,
    attn_first,
    attn_second,
    mlp_params,
    mlp_first,
    mlp_second,
    small,
    small_first,
    small_second,
):
    lay = Layout(lax.axis_size("dp"), lax.axis_size("seq"))
    groups, nz, pair = lay.groups, lay.nz, lay.pair
    count, span, width = inputs.shape
    rows = attn_params.shape[0]
    ff = mlp_params.shape[1] // 2
    hd = width // HEADS
    unit = ff // HEADS
    rot_dims = hd // 4
    score_scale = hd ** (-0.5)
    first_row = (lay.dp * nz + lay.z) * rows
    seqs, length = count * pair, span * nz
    tokens_here = seqs * length

    wide_small = jnp.pad(small, ((0, 0), (0, LANES - small.shape[1])))
    qu_sources = [(mlp_params, 0, unit)]
    qu_sources += [(attn_params, j * HEADS, hd) for j in range(3)]
    qu_sources += [(wide_small, None, LANES)]
    dn_sources = [(mlp_params, HEADS, unit)]

    def swap(sources, r):
        blocks = prepare(lay, r, sources)
        return lay.core_hop(blocks, r) if r else blocks

    def exchange(half):
        return lax.all_to_all(half, "seq", 0, 0, tiled=True).reshape(nz * rows, -1)

    class Whole:
        def __init__(self, halves, size=None, first=0):
            self.halves, self.seen, self.state = halves, set(), None
            self.size, self.first = size or halves[0].rows, first

        def flush(self):
            items = [
                (r, m, (v[0], v[1] + self.first))
                for r, half in enumerate(self.halves)
                for m, v in half.held.items()
                if (r, m) not in self.seen
            ]
            self.seen |= {(r, m) for r, m, _ in items}
            if items:
                count = len(self.halves)
                slots = [
                    (lay.g ^ m) * count + (lay.c ^ r if count > 1 else 0) for r, m, _ in items
                ]
                blocks = [v for _, _, v in items]
                self.state = place(blocks, slots, self.size, groups * count, self.state)

        def result(self):
            self.flush()
            return self.state.reshape(-1, self.state.shape[-1])

    def joined(parts, *values):
        *values, states = join(*values, [p.state for p in parts])
        for p, v in zip(parts, states):
            p.state = v
        return values

    def crossed(piece):
        return [piece] + [lay.core_hop(piece, r) for r in range(1, pair)]

    positions = jnp.arange(length, dtype=f32)
    frequency = 10000.0 ** (-(jnp.arange(rot_dims // 2, dtype=f32) * 2.0) / rot_dims)
    angles = positions[:, None] * frequency[None, :]
    cosine, sine = jnp.cos(angles), jnp.sin(angles)
    blank = jnp.zeros_like(sine)
    rest = jnp.zeros((length, LANES - rot_dims), f32)
    tables = jnp.stack(
        [
            jnp.concatenate([cosine, cosine, rest + 1.0], axis=1),
            jnp.concatenate([-sine, blank, rest], axis=1),
            jnp.concatenate([blank, sine, rest], axis=1),
        ]
    )

    first = exchange(swap(qu_sources, 0))
    rest = [swap(qu_sources, r) for r in range(1, pair)]
    w_out = attn_params[:, 3 * width :].astype(bf16)
    dn = jnp.stack([prepare(lay, r, dn_sources) for r in range(pair)], axis=1)
    first, rest, w_out, dn = join(first, rest, w_out, dn)

    qu = [GroupGather(lay, first, False)]
    w_out = lax.ppermute(w_out, AXES, lay.head_owner_perm())
    for r in range(1, pair):
        one = exchange(rest[r - 1])
        qu[-1].send(0)
        one, w_out, dn = joined(qu, one, w_out, dn)
        qu.append(GroupGather(lay, one, bool(r % 2)))
    dn = lax.all_to_all(dn, "seq", 0, 0, tiled=True)
    qu[-1].send(0)
    pieces = crossed(inputs)
    newest, dn, pieces, w_out = joined(qu, inputs, dn, pieces, w_out)

    w_qu = Whole(qu)
    newest = lay.ring(newest)
    dn = [lay.core_hop(dn[:, r], r) if r else dn[:, r] for r in range(pair)]
    dn = [v.reshape(nz * rows, unit) for v in dn]
    dn[-1] = jnp.concatenate([dn[-1], w_out.reshape(-1, unit)])
    dn = [GroupGather(lay, v, bool(r)) for r, v in enumerate(dn)]
    w_qu.flush()
    for v in qu:
        v.send(1)
    newest, pieces = joined(qu + dn + [w_qu], newest, pieces)
    for v in qu:
        v.rest(2)

    w_qkvu = w_qu.result()
    vectors = last_columns(w_qkvu)
    norm_vec = vectors[:8]
    qkv_bias = vectors[6:9].reshape(3, HEADS, hd)
    qkv_bias = lax.dynamic_index_in_dim(qkv_bias, lay.t, 1, keepdims=False).reshape(1, 3 * hd)
    up_bias = lax.dynamic_slice(vectors[9:13].reshape(-1), (lay.t * unit,), (unit,))[None]
    out_bias = vectors[4] + vectors[5]
    held = ()

    def forward_piece(pieces, steps_away, held):
        where = [(lay.z - k) % nz for k in steps_away]
        return piece_forward(
            lay, pieces, where, norm_vec, w_qkvu, qkv_bias, up_bias, tables, held
        )

    dy = LineGather(lay, cotangent)
    w_dn, w_wo = Whole(dn, nz * rows), Whole(dn[-1:], rows * width // unit, nz * rows)
    for k in range(2, nz):
        last, newest = newest, lay.ring(newest)
        if k == 2:
            GroupGather.send_first(dn)
        elif k == 3:
            for v in dn:
                v.send(1)
            w_dn.flush()
            w_wo.flush()
            dy.cross()
        next_pieces = crossed(last)
        held = forward_piece(pieces, [k - 2], held)
        newest, pieces, held = joined(dn + [w_dn, w_wo, dy], newest, next_pieces, held)
    for v in dn:
        v.rest(2)

    dy.step(1)
    last_pieces = crossed(newest)
    held = forward_piece(pieces + last_pieces, [nz - 2, nz - 1], held)
    w_down = w_dn.result()
    w_out = w_wo.result().reshape(hd, width)
    held, w_down, w_out = joined([dy], held, w_down, w_out)
    tile = min(512, length)
    flat = (tokens_here, width)
    x_flat, qkv, g, slope = (v.reshape(seqs, length, -1) for v in held)
    x_flat, g, slope = (v.reshape(tokens_here, -1) for v in (x_flat, g, slope))

    dy.cross()
    dy.step(2)
    o, lse = attn_forward(qkv, score_scale)
    o = o.reshape(tokens_here, hd)
    out_parts = {}

    def output_part(r):
        part = output_forward(g, w_down, o, w_out, tile, r, pair)
        return part.reshape(count, length, width)

    for r in range(1, pair):
        out_parts[r] = output_part(r)
    out_parts, o, lse, g = joined([dy], out_parts, o, lse, g)

    for k in range(3, nz):
        dy.step(k)
    for r in range(1, pair):
        out_parts[r] = lay.core_hop(out_parts[r], r)
    dy.cross(2 * (nz - 3))
    out_parts[0] = output_part(0)
    out_sum = SeqScatter(lay, [out_parts[r] for r in range(pair)], count)
    o, g = joined([dy, out_sum], o, g)

    def steps(*parts):
        for p in parts:
            p.step()

    def to_owners(blocks):
        return lax.all_to_all(blocks, "seq", 0, 0, tiled=True)

    def at_owner(blocks):
        parts = [blocks[:, r] for r in range(pair)]
        return [lay.core_hop(v, r) if r else v for r, v in enumerate(parts)]

    def more_rounds(parts):
        while parts[0].at < len(parts[0].bits):
            if len(parts) == pair and parts[0].keep.shape[2] < width:
                fold(parts)
            else:
                for p in parts:
                    p.fold()
            steps(*parts)

    out_sum.send()
    dy.cross()
    dy_all = dy.flush().reshape(seqs, length, width)
    dy_flat = dy_all.reshape(flat)
    du, du_sums = hidden_backward(dy_flat, w_down, slope, tile)
    dy_flat, du, du_sums = join(dy_flat, du, du_sums)

    dp, dp_sums = attn_backward(
        dy_flat.reshape(seqs, length, width), w_out, qkv, lse, tables, score_scale
    )
    dp = dp.reshape(tokens_here, 3 * hd)

    def input_part(r):
        part = input_backward(du, dp, w_qkvu, norm_vec, tile, r, pair)
        return part.reshape(count, length, width)

    z_parts = {r: input_part(r) for r in range(1, pair)}
    z_parts, du, dp, du_sums, dp_sums = join(z_parts, du, dp, du_sums, dp_sums)

    for r in range(1, pair):
        z_parts[r] = lay.core_hop(z_parts[r], r)
    z_parts[0] = input_part(0)
    up, lanes = folded_gradient(lay, x_flat, after(du, z_parts[0]), du_sums, w_qkvu, 0, 2)
    z_sum = SeqScatter(lay, [z_parts[r] for r in range(pair)], count)
    dy_flat, dp, du_sums, dp_sums, lanes = joined(
        up + [out_sum, z_sum], dy_flat, dp, du_sums, dp_sums, lanes
    )

    z_sum.send()
    upstream = cotangent.astype(f32)
    upstream_sum = jnp.sum(upstream, axis=(0, 1))[:, None]
    dp_sums = jnp.sum(dp_sums[:, 0], axis=0)
    qkv_columns = lax.dynamic_update_slice(
        jnp.zeros((width, 3), f32), dp_sums.reshape(3, hd).T, (lay.t * hd, 0)
    )
    up_columns = lax.dynamic_update_slice(jnp.zeros((ff,), f32), du_sums[0], (lay.t * unit,))
    up_columns = up_columns.reshape(ff // width, width).T
    others = jnp.concatenate(
        [jnp.zeros((width, 4), f32), upstream_sum, upstream_sum, qkv_columns, up_columns], axis=1
    )
    others = jnp.pad(others, ((0, 0), (0, LANES - others.shape[1])))
    dp_sums = jnp.broadcast_to(dp_sums[None], (8, 3 * hd))

    steps(*up)
    (dqkv,) = folded_gradient(lay, x_flat, dp, dp_sums, w_qkvu, unit, 0, (lanes, others))
    (dy_flat,) = joined(up + dqkv, dy_flat)

    more_rounds(up)
    steps(*dqkv)
    down = gradient(lay, dy_flat, g)
    outputs = (inputs.astype(f32) + out_sum.result() + out_bias).astype(bf16)
    dy_flat, outputs = joined(up + dqkv + down, dy_flat, outputs)

    more_rounds(dqkv)
    steps(*down)
    up_blocks = final_blocks(up, nz)
    out_whole = dot(o, dy_flat, 0, 0)
    out_whole = out_whole.astype(bf16).reshape(groups, rows, width)
    out_whole = jnp.stack(
        [
            lax.dynamic_index_in_dim(
                out_whole, lay.g ^ GroupScatter.member(lay, i, True), 0, keepdims=False
            )
            for i in range(groups)
        ]
    )
    wo = GroupScatter(lay, out_whole[: groups // 2], out_whole[groups // 2 :], True)
    (up_blocks,) = joined(dqkv + [wo, z_sum], up_blocks)

    mlp_state = (mlp_params, mlp_first, mlp_second)
    attn_state = (attn_params, attn_first, attn_second)
    up_blocks = to_owners(up_blocks)
    more_rounds(down)
    steps(wo)
    dqkv_blocks = final_blocks(dqkv, nz)
    normed_grad = z_sum.result()
    normed, scaling = normalize(inputs.astype(f32))
    grad_mean = jnp.mean(normed_grad, axis=-1, keepdims=True)
    grad_proj = jnp.mean(normed_grad * normed, axis=-1, keepdims=True)
    input_grad = upstream + scaling * (normed_grad - grad_mean - normed * grad_proj)
    up_blocks, dqkv_blocks, input_grad = joined(down + [wo], up_blocks, dqkv_blocks, input_grad)

    dqkv_blocks = to_owners(dqkv_blocks)
    more_rounds([wo])
    down_blocks = final_blocks(down, nz)
    up_parts = at_owner(up_blocks)
    mlp_result = adam_columns(lay, rate_mlp, up_parts, 0, unit, mlp_state, 0, 1, ())
    dqkv_blocks, down_blocks, mlp_result = joined([wo], dqkv_blocks, down_blocks, mlp_result)

    down_blocks = to_owners(down_blocks)
    out_grad = wo.result().astype(bf16)
    out_grad = lax.ppermute(out_grad, AXES, [(b, a) for a, b in lay.head_owner_perm()])
    dqkv_parts = at_owner(dqkv_blocks)
    attn_result = adam_columns(lay, rate_attention, dqkv_parts, 0, hd, attn_state, 0, 3, ())
    at = 3 * hd
    small_grad = sum(
        jnp.sum(v[:, :, at : at + small.shape[1]].astype(f32), axis=0) for v in dqkv_parts
    )
    small_result = adamw(small, small_grad, small_first, small_second, rate_vector)
    out_grad = [out_grad[None]]
    attn_result = adam_columns(
        lay, rate_attention, out_grad, 0, width, attn_state, 3 * width, 1, attn_result
    )
    down_blocks, attn_result, small_result, mlp_result = join(
        down_blocks, attn_result, small_result, mlp_result
    )

    mlp_result = adam_columns(
        lay, rate_mlp, at_owner(down_blocks), 0, unit, mlp_state, ff, 1, mlp_result
    )
    return (outputs, input_grad, *attn_result, *mlp_result, *small_result)


def solution(mesh):
    tokens, weights = P("dp", "seq", None), P(("dp", "seq"), None)
    return jax.shard_map(
        body,
        mesh=mesh,
        in_specs=(tokens,) * 2 + (weights,) * 9,
        out_specs=(tokens,) * 2 + (weights,) * 12,
        check_vma=False,
    )
```

time: 784 us -> 605 us (0.77)
  waiting for transfers between devices: 280 us -> 147 us
  Pallas kernels: 143 us -> 268 us
  local copies, waits for them, and re-layouts: 115 us -> 30.4 us
  other arithmetic: 76.4 us -> 41 us
  starting transfers between devices: 129 us -> 101 us
  matrix products: 30.9 us -> 5.72 us
    pallas_call x10 -> x32, Pallas kernels: 125 us -> 251 us  [the longest x3 52.3 us: gradient_call(): pl.pallas_call(partial(kernel, half), grid_spec=pltpu.PrefetchScalarGridS...]
    all_to_all x10 -> x8, waiting for transfers between devices: 107 us -> 18.4 us  [the longest x2 9.9 us: exchange(): return lax.all_to_all(half, 'seq', 0, 0, tiled=True).reshape(nz * rows, -1)]
    dynamic_update_slice x30 -> x1, local copies, waits for them, and re-layouts: 41.5 us -> 0.01 us  [body(): lax.dynamic_update_slice(jnp.zeros((width, 3), f32), dp_sums.reshape(3, h...]
    ppermute x11 -> x1, waiting for transfers between devices: 68 us -> 28.3 us  [body(): w_out = lax.ppermute(w_out, AXES, lay.head_owner_perm())]
    convert_element_type x20 -> x3, other arithmetic: 44.1 us -> 14 us  [the longest x2 13 us: __init__(): total = sum((p.astype(f32) for p in parts)).astype(bf16)]
    ppermute x63 -> x51, waiting for transfers between devices: 105 us -> 79.1 us  [hop(): return lax.ppermute(value, AXES, self.perm(target))]
    dot_general x4 -> x1, matrix products: 30.9 us -> 5.72 us  [dot(): lax.dot_general(left_op, right_op, (((left_dim,), (right_dim,)), ((), ())...]
    ppermute x1, waiting for transfers between devices: 0.01 us -> 20.8 us  [body(): lax.ppermute(out_grad, AXES, [(b, a) for a, b in lay.head_owner_perm()])]
  transfers between devices with their start and end apart: 85 -> 61, of which waited for: 19 -> 24; matrix products, arithmetic and copies ran while one was open for 26% -> 11% of each run, Pallas kernels for 8% -> 43%
where the time goes in v2:
time: 605 us; the launch traced here: 595 us
  Pallas kernels  268 us (44%)
  waiting for transfers between devices  147 us (24%)
  starting transfers between devices  101 us (17%)
  other arithmetic  41 us (7%)
  local copies, waits for them, and re-layouts  30.4 us (5%)
    ppermute x51, waiting for transfers between devices, hop(): return lax.ppermute(value, AXES, self.perm(target))  79.1 us
    ppermute x51, starting transfers between devices, hop(): return lax.ppermute(value, AXES, self.perm(target))  58 us
    pallas_call x3, Pallas kernels, gradient_call(): pl.pallas_call(partial(kernel, half), grid_spec=pltpu.PrefetchScalarGridS...  52.3 us
    pallas_call x3, Pallas kernels, piece_forward(): pl.pallas_call(partial(piece_kernel, pair, places, wide // 24), grid_spec...  41.2 us
    ppermute x1, waiting for transfers between devices, body(): w_out = lax.ppermute(w_out, AXES, lay.head_owner_perm())  28.3 us
    pallas_call x2, Pallas kernels, input_backward(): pl.pallas_call(partial(input_kernel, hd), grid=(steps,), in_specs=[pl.Blo...  26.3 us
    pallas_call x5, Pallas kernels, place(): pl.pallas_call(partial(place_kernel, count, tile), grid_spec=pltpu.Prefet...  26 us
    pallas_call x4, Pallas kernels, adam_columns(): pl.pallas_call(partial(adam_kernel, pair, places, rate), grid_spec=pltpu....  25.3 us
  transfers between devices with their start and end apart: 61, of which 24 were waited for; matrix products, arithmetic and copies ran while one was open for 11% of the time, Pallas kernels for 43%

profile of v2, /device:TPU:5, one launch (start us, length us, event | category | flops | bytes accessed | tf_op | source)
XLA Modules:
  0.0 595.1 jit_solution(5159790268983722952)
XLA Ops:
  24.1 9.9 %all-to-all-done = bf16[4,64,1920]{2,1,0:T(8,128)(2,1)S(1)} async-done(((bf16[4,64,1920]{2,1,0:T(8,128)(2,1)}), bf16[4,64,1920]{2,1,0:T(8,128)(2,1)S(1)}, u32[]{:S(2)}, u32[]{:S(2)}) %all-to-all-start) | async-done | bytes 983072 | tf_op jit(solution)/shard_map/all_to_all | solution.py:943
  44.1 28.3 %collective-permute-done.1 = bf16[64,2048]{1,0:T(8,128)(2,1)S(1)} collective-permute-done((bf16[64,2048]{1,0:T(8,128)(2,1)}, bf16[64,2048]{1,0:T(8,128)(2,1)S(1)}, u32[]{:S(2)}, u32[]{:S(2)}) %collective-permute-start.1) | collective-permute-done | bytes 262176 | tf_op jit(solution)/shard_map/ppermute | solution.py:1000
  82.5 21.3 %collective-permute-done.6.refs_4_ = bf16[256,1920]{1,0:T(8,128)(2,1)S(1)} collective-permute-done((bf16[256,1920]{1,0:T(8,128)(2,1)}, bf16[256,1920]{1,0:T(8,128)(2,1)S(1)}, u32[]{:S(2)}, u32[]{:S(2)}) %collective-permute-start.6) | collective-permute-done | bytes 983072 | tf_op jit(solution)/shard_map/ppermute | solution.py:87
  116.1 13.2 %collective-permute-done.8.refs_0_ = bf16[256,1920]{1,0:T(8,128)(2,1)} collective-permute-done((bf16[256,1920]{1,0:T(8,128)(2,1)}, bf16[256,1920]{1,0:T(8,128)(2,1)}, u32[]{:S(2)}, u32[]{:S(2)}) %collective-permute-start.8) | collective-permute-done | bytes 983072 | tf_op jit(solution)/shard_map/ppermute | solution.py:87
  149.5 11.2 %piece_forward.3 = (bf16[2,1,4,256,2048]{4,3,2,1,0:T(8,128)(2,1)}, bf16[2,1,4,256,768]{4,3,2,1,0:T(8,128)(2,1)}, bf16[2,1,4,256,1024]{4,3,2,1,0:T(8,128)(2,1)}, bf16[2,1,4,256,1024]{4,3,2,1,0:T(8,128)(2,1)}) custom-call(s32[1]{0:T(128)} %bitcast.30.pos_ref, bf16[1,256,2048]{2,1,0:T(8,128)(2,1)} %refs_0_.8, bf16[1,256,2048]{2,1,0:T(8,128)(2,1)} %copy-done.17, ...), custom_call_target="tpu_custom_call" | custom-call | flops 3758097 | bytes 12583 | tf_op jit(solution)/shard_map/piece_forward/pallas_call | solution.py:568
  169.5 11.2 %piece_forward.4 = (bf16[2,1,4,256,2048]{4,3,2,1,0:T(8,128)(2,1)}, bf16[2,1,4,256,768]{4,3,2,1,0:T(8,128)(2,1)}, bf16[2,1,4,256,1024]{4,3,2,1,0:T(8,128)(2,1)}, bf16[2,1,4,256,1024]{4,3,2,1,0:T(8,128)(2,1)}) custom-call(s32[1]{0:T(128)} %bitcast.39.pos_ref, ...), custom_call_target="tpu_custom_call", output_to_operand_aliasing={{0}: (8, {}), {1}: (9, {}), {2}: (10, {}), {3}: (11, {})} | custom-call | flops 3758097 | bytes 12583 | tf_op jit(solution)/shard_map/piece_forward/pallas_call | solution.py:568
  200.0 18.8 %piece_forward.5 = (bf16[2,1,4,256,2048]{4,3,2,1,0:T(8,128)(2,1)}, bf16[2,1,4,256,768]{4,3,2,1,0:T(8,128)(2,1)}, bf16[2,1,4,256,1024]{4,3,2,1,0:T(8,128)(2,1)}, bf16[2,1,4,256,1024]{4,3,2,1,0:T(8,128)(2,1)}) custom-call(s32[2]{0:T(128)} %pad_add_fusion.pos_ref, ...), custom_call_target="tpu_custom_call", output_to_operand_aliasing={{0}: (10, {}), {1}: (11, {}), {2}: (12, {}), {3}: (13, {})} | custom-call | flops 7516193 | bytes 25166 | tf_op jit(solution)/shard_map/piece_forward/pallas_call | solution.py:568
  235.9 10.1 %output_forward.2 = bf16[1024,2048]{1,0:T(8,128)(2,1)} custom-call(bf16[2048,1024]{1,0:T(8,128)(2,1)} %bitcast.143, bf16[2048,1024]{1,0:T(8,128)(2,1)} %bitcast.146, bf16[2048,256]{1,0:T(8,128)(2,1)} %bitcast.157, bf16[256,2048]{1,0:T(8,128)(2,1)} %reshape_reshape.15.wo_ref), custom_call_target="tpu_custom_call" | custom-call | flops 5368710 | bytes 16778 | tf_op jit(solution)/shard_map/output_forward/pallas_call | solution.py:712
  246.0 7.3 %collective-permute-done.24 = bf16[1,256,2048]{2,1,0:T(8,128)(2,1)S(1)} collective-permute-done((bf16[1,256,2048]{2,1,0:T(8,128)(2,1)S(1)}, bf16[1,256,2048]{2,1,0:T(8,128)(2,1)S(1)}, u32[]{:S(2)}, u32[]{:S(2)}) %collective-permute-start.24) | collective-permute-done | bytes 1048608 | tf_op jit(solution)/shard_map/ppermute | solution.py:87
  262.6 10.0 %output_forward.3 = bf16[1024,2048]{1,0:T(8,128)(2,1)} custom-call(bf16[2048,1024]{1,0:T(8,128)(2,1)} %bitcast.144, bf16[2048,1024]{1,0:T(8,128)(2,1)} %bitcast.147, bf16[2048,256]{1,0:T(8,128)(2,1)} %bitcast.158, bf16[256,2048]{1,0:T(8,128)(2,1)} %reshape_reshape.15.wo_ref), custom_call_target="tpu_custom_call" | custom-call | flops 5368710 | bytes 16778 | tf_op jit(solution)/shard_map/output_forward/pallas_call | solution.py:712
  272.6 6.5 %fusion.1 = bf16[1,1024,2048]{2,1,0:T(8,128)(2,1)} fusion(bf16[1,1024,2048]{2,1,0:T(8,128)(2,1)S(1)} %collective-permute-done.31, bf16[1024,2048]{1,0:T(8,128)(2,1)} %output_forward.3), kind=kLoop, calls=%fused_computation.5 | loop fusion | flops 8388608 | bytes 12582912 | tf_op jit(solution)/shard_map/convert_element_type | solution.py:896
  295.4 8.1 %place.9 = bf16[8,256,2048]{2,1,0:T(8,128)(2,1)} custom-call(s32[14]{0:T(128)} %stack.189.slot_ref, bf16[256,2048]{1,0:T(8,128)(2,1)} %bitcast.44.refs_0_, bf16[256,2048]{1,0:T(8,128)(2,1)} %bitcast.45.refs_1_, bf16[256,2048]{1,0:T(8,128)(2,1)} %bitcast.173, bf16[256,2048]{1,0:T(8,128)(2,1)} %bitcast.177, bf16[256,2048]{1,0:T(8,128)(2,1)} %bitcast.174, ...), custom_call_target="tpu_custom_call" | custom-call | flops 1 | bytes 29361 | tf_op jit(solution)/shard_map/place/pallas_call | solution.py:267
  303.5 13.8 %hidden_backward.1 = (bf16[2048,1024]{1,0:T(8,128)(2,1)}, f32[8,1024]{1,0:T(8,128)}) custom-call(bf16[2048,2048]{1,0:T(8,128)(2,1)} %bitcast.137, bf16[2048,1024]{1,0:T(8,128)(2,1)} %bitcast.148, bf16[2048,1024]{1,0:T(8,128)(2,1)} %bitcast.151), custom_call_target="tpu_custom_call" | custom-call | flops 8589935 | bytes 25166 | tf_op jit(solution)/shard_map/hidden_backward/pallas_call | solution.py:746
  317.3 17.1 %attn_backward.1 = (bf16[2,1024,768]{2,1,0:T(8,128)(2,1)}, f32[2,8,768]{2,1,0:T(8,128)}) custom-call(bf16[2,1024,2048]{2,1,0:T(8,128)(2,1)} %bitcast.138, bf16[256,2048]{1,0:T(8,128)(2,1)} %reshape_reshape.15.wo_ref, bf16[2,1024,768]{2,1,0:T(8,128)(2,1)} %bitcast.150, f32[2,1024,128]{2,1,0:T(8,128)} %get-tuple-element.364.lse_ref, ...), custom_call_target="tpu_custom_call" | custom-call | flops 7516193 | bytes 33555 | tf_op jit(solution)/shard_map/attn_backward/pallas_call | solution.py:675
  334.4 13.1 %input_backward.2 = bf16[1024,2048]{1,0:T(8,128)(2,1)} custom-call(bf16[2048,1024]{1,0:T(8,128)(2,1)} %get-tuple-element.372.du_ref.refs_2_, bf16[2048,768]{1,0:T(8,128)(2,1)} %bitcast.152, bf16[2048,1920]{1,0:T(8,128)(2,1)} %bitcast.125, bf16[2048,1920]{1,0:T(8,128)(2,1)} %bitcast.126, bf16[2048,1920]{1,0:T(8,128)(2,1)} %bitcast.127, ...), custom_call_target="tpu_custom_call" | custom-call | flops 7516193 | bytes 25166 | tf_op jit(solution)/shard_map/input_backward/pallas_call | solution.py:783
  348.5 13.2 %input_backward.3 = bf16[1024,2048]{1,0:T(8,128)(2,1)} custom-call(bf16[2048,1024]{1,0:T(8,128)(2,1)} %get-tuple-element.372.du_ref.refs_2_, bf16[2048,768]{1,0:T(8,128)(2,1)} %bitcast.153, bf16[2048,1920]{1,0:T(8,128)(2,1)} %bitcast.129, bf16[2048,1920]{1,0:T(8,128)(2,1)} %bitcast.130, bf16[2048,1920]{1,0:T(8,128)(2,1)} %bitcast.131, ...), custom_call_target="tpu_custom_call" | custom-call | flops 7516193 | bytes 25166 | tf_op jit(solution)/shard_map/input_backward/pallas_call | solution.py:783
  361.7 19.4 %gradient.3 = (bf16[2,256,1024]{2,1,0:T(8,128)(2,1)}, bf16[2,256,1024]{2,1,0:T(8,128)(2,1)}, bf16[2,256,1024]{2,1,0:T(8,128)(2,1)}, bf16[2,256,1024]{2,1,0:T(8,128)(2,1)}, f32[2048,128]{1,0:T(8,128)}) custom-call(s32[8]{0:T(128)} %stack.218.refs_0_.block_ref, bf16[2048,2048]{1,0:T(8,128)(2,1)} %bitcast.141, ...), custom_call_target="tpu_custom_call" | custom-call | flops 8589935 | bytes 16778 | tf_op jit(solution)/shard_map/gradient/pallas_call | solution.py:364
  381.1 6.5 %fusion = bf16[1,1024,2048]{2,1,0:T(8,128)(2,1)} fusion(bf16[1,1024,2048]{2,1,0:T(8,128)(2,1)} %collective-permute-done.34, bf16[1024,2048]{1,0:T(8,128)(2,1)S(1)} %copy-done.3), kind=kLoop, calls=%fused_computation.3 | loop fusion | flops 8388608 | bytes 12582912 | tf_op jit(solution)/shard_map/convert_element_type | solution.py:896
  400.5 17.0 %gradient.4 = (bf16[2,256,896]{2,1,0:T(8,128)(2,1)}, bf16[2,256,896]{2,1,0:T(8,128)(2,1)}, bf16[2,256,896]{2,1,0:T(8,128)(2,1)}, bf16[2,256,896]{2,1,0:T(8,128)(2,1)}) custom-call(s32[8]{0:T(128)} %stack.218.refs_0_.block_ref, bf16[2048,2048]{1,0:T(8,128)(2,1)} %bitcast.142, bf16[2048,768]{1,0:T(8,128)(2,1)} %bitcast.154, ...), custom_call_target="tpu_custom_call" | custom-call | flops 7516193 | bytes 15729 | tf_op jit(solution)/shard_map/gradient/pallas_call | solution.py:364
  430.6 15.9 %gradient.5 = (bf16[2,256,1024]{2,1,0:T(8,128)(2,1)}, bf16[2,256,1024]{2,1,0:T(8,128)(2,1)}, bf16[2,256,1024]{2,1,0:T(8,128)(2,1)}, bf16[2,256,1024]{2,1,0:T(8,128)(2,1)}) custom-call(s32[8]{0:T(128)} %stack.218.refs_0_.block_ref, bf16[2048,2048]{1,0:T(8,128)(2,1)} %bitcast.139, bf16[2048,1024]{1,0:T(8,128)(2,1)} %bitcast.145), custom_call_target="tpu_custom_call" | custom-call | flops 8589935 | bytes 16778 | tf_op jit(solution)/shard_map/gradient/pallas_call | solution.py:364
  526.9 7.6 %adam_columns.4 = (f32[64,16384]{1,0:T(8,128)}, f32[64,16384]{1,0:T(8,128)}, f32[64,16384]{1,0:T(8,128)}, f32[64,16384]{1,0:T(8,128)}) custom-call(s32[1]{0:T(128)} %bitcast.16.c_ref, bf16[4,64,1024]{2,1,0:T(8,128)(2,1)} %get-tuple-element.513.refs_0_, bf16[4,64,1024]{2,1,0:T(8,128)(2,1)} %copy-done.39, f32[64,16384]{1,0:T(8,128)} %refs_2_.11, ...), custom_call_target="tpu_custom_call" | custom-call | flops 15729 | bytes 15729 | tf_op jit(solution)/shard_map/adam_columns/pallas_call | solution.py:827
  549.1 7.0 %adam_columns.5 = (f32[64,8192]{1,0:T(8,128)}, f32[64,8192]{1,0:T(8,128)}, f32[64,8192]{1,0:T(8,128)}, f32[64,8192]{1,0:T(8,128)}) custom-call(s32[1]{0:T(128)} %bitcast.16.c_ref, bf16[4,64,896]{2,1,0:T(8,128)(2,1)} %copy-done.13, bf16[4,64,896]{2,1,0:T(8,128)(2,1)} %copy-done.34, f32[64,8192]{1,0:T(8,128)} %refs_1_.5, f32[64,8192]{1,0:T(8,128)} %refs_2_.10, ...), custom_call_target="tpu_custom_call" | custom-call | flops 11797 | bytes 11797 | tf_op jit(solution)/shard_map/adam_columns/pallas_call | solution.py:827
  556.0 20.8 %collective-permute-done.50 = bf16[64,2048]{1,0:T(8,128)(2,1)S(1)} collective-permute-done((bf16[64,2048]{1,0:T(8,128)(2,1)S(1)}, bf16[64,2048]{1,0:T(8,128)(2,1)S(1)}, u32[]{:S(2)}, u32[]{:S(2)}) %collective-permute-start.50) | collective-permute-done | bytes 262176 | tf_op jit(solution)/shard_map/ppermute | solution.py:1202
  587.1 7.6 %adam_columns.7 = (f32[64,16384]{1,0:T(8,128)}, f32[64,16384]{1,0:T(8,128)}, f32[64,16384]{1,0:T(8,128)}, f32[64,16384]{1,0:T(8,128)}) custom-call(s32[1]{0:T(128)} %bitcast.16.c_ref, bf16[4,64,1024]{2,1,0:T(8,128)(2,1)} %get-tuple-element.511.refs_0_, ...), custom_call_target="tpu_custom_call", output_to_operand_aliasing={{0}: (6, {}), {1}: (7, {}), {2}: (8, {}), {3}: (9, {})} | custom-call | flops 15729 | bytes 15729 | tf_op jit(solution)/shard_map/adam_columns/pallas_call | solution.py:827
  (299 shorter events, 278.2 us)
Async XLA Ops:
  5.5 28.4 %all-to-all-start = ((bf16[4,64,1920]{2,1,0:T(8,128)(2,1)}), bf16[4,64,1920]{2,1,0:T(8,128)(2,1)S(1)}, u32[]{:S(2)}, u32[]{:S(2)}) async-start(bf16[4,64,1920]{2,1,0:T(8,128)(2,1)} %prepare.4), calls=%async_computation | async-start | bytes 1966080 | tf_op jit(solution)/shard_map/all_to_all | solution.py:943
  34.0 39.4 %all-to-all-start.1 = ((bf16[4,64,1920]{2,1,0:T(8,128)(2,1)}), bf16[4,64,1920]{2,1,0:T(8,128)(2,1)S(1)}, u32[]{:S(2)}, u32[]{:S(2)}) async-start(bf16[4,64,1920]{2,1,0:T(8,128)(2,1)} %copy-done.29), calls=%async_computation.1 | async-start | bytes 1966080 | tf_op jit(solution)/shard_map/all_to_all | solution.py:943
  37.5 35.0 %collective-permute-start.3 = (bf16[256,1920]{1,0:T(8,128)(2,1)S(1)}, bf16[256,1920]{1,0:T(8,128)(2,1)S(1)}, u32[]{:S(2)}, u32[]{:S(2)}) collective-permute-start(bf16[256,1920]{1,0:T(8,128)(2,1)S(1)} %bitcast.165), channel_id=1, source_target_pairs={{0,16},{1,17},{2,18},{3,19},{4,20},{5,21},{6,22},{7,23},{8,24},{9,... | collective-permute-start | bytes 2949128 | tf_op jit(solution)/shard_map/ppermute | solution.py:87
  37.8 35.6 %collective-permute-start.2 = (bf16[256,1920]{1,0:T(8,128)(2,1)S(1)}, bf16[256,1920]{1,0:T(8,128)(2,1)}, u32[]{:S(2)}, u32[]{:S(2)}) collective-permute-start(bf16[256,1920]{1,0:T(8,128)(2,1)S(1)} %bitcast.166), channel_id=1, source_target_pairs={{0,8},{1,9},{2,10},{3,11},{4,12},{5,13},{6,14},{7,15},{8,0},{9,1},... | collective-permute-start | bytes 2949128 | tf_op jit(solution)/shard_map/ppermute | solution.py:87
  39.0 33.5 %collective-permute-start.1 = (bf16[64,2048]{1,0:T(8,128)(2,1)}, bf16[64,2048]{1,0:T(8,128)(2,1)S(1)}, u32[]{:S(2)}, u32[]{:S(2)}) collective-permute-start(bf16[64,2048]{1,0:T(8,128)(2,1)} %slice.126), channel_id=1, source_target_pairs={{0,0},{1,8},{2,16},{3,24},{4,4},{5,12},{6,20},{7,28},{8,1},{9,9},{... | collective-permute-start | bytes 786440 | tf_op jit(solution)/shard_map/ppermute | solution.py:1000
  74.7 30.2 %all-to-all-start.2 = ((bf16[4,2,64,1024]{3,2,1,0:T(8,128)(2,1)}), bf16[4,2,64,1024]{3,2,1,0:T(8,128)(2,1)S(1)}, u32[]{:S(2)}, u32[]{:S(2)}) async-start(bf16[4,2,64,1024]{3,2,1,0:T(8,128)(2,1)} %copy.77), calls=%async_computation.2 | async-start | bytes 2097152 | tf_op jit(solution)/shard_map/all_to_all | solution.py:1006
  104.8 26.6 %collective-permute-start.7 = (bf16[1,256,2048]{2,1,0:T(8,128)(2,1)S(1)}, bf16[1,256,2048]{2,1,0:T(8,128)(2,1)}, u32[]{:S(2)}, u32[]{:S(2)}) collective-permute-start(bf16[1,256,2048]{2,1,0:T(8,128)(2,1)S(1)} %copy-done), channel_id=1, source_target_pairs={{0,1},{1,2},{2,3},{3,0},{4,5},{5,6},{6,7},{7,4},{8,9},{9,10},{10,1... | collective-permute-start | bytes 3145736 | tf_op jit(solution)/shard_map/ppermute | solution.py:87
  131.5 31.8 %collective-permute-start.14 = (bf16[640,1024]{1,0:T(8,128)(2,1)S(1)}, bf16[640,1024]{1,0:T(8,128)(2,1)S(1)}, u32[]{:S(2)}, u32[]{:S(2)}) collective-permute-start(bf16[640,1024]{1,0:T(8,128)(2,1)S(1)} %constant_dynamic-update-slice_fusion), channel_id=1, source_target_pairs={{0,16},{1,17},{2,18},{3,19},{4,20},{5,21},{6,22},{7,23},{8,24},{9,... | collective-permute-start | bytes 3932168 | tf_op jit(solution)/shard_map/ppermute | solution.py:87
  131.6 31.7 %collective-permute-start.13 = (bf16[640,1024]{1,0:T(8,128)(2,1)S(1)}, bf16[640,1024]{1,0:T(8,128)(2,1)S(1)}, u32[]{:S(2)}, u32[]{:S(2)}) collective-permute-start(bf16[640,1024]{1,0:T(8,128)(2,1)S(1)} %constant_dynamic-update-slice_fusion), channel_id=1, source_target_pairs={{0,8},{1,9},{2,10},{3,11},{4,12},{5,13},{6,14},{7,15},{8,0},{9,1},... | collective-permute-start | bytes 3932168 | tf_op jit(solution)/shard_map/ppermute | solution.py:87
  136.5 26.8 %collective-permute-start.11 = (bf16[1,256,2048]{2,1,0:T(8,128)(2,1)}, bf16[1,256,2048]{2,1,0:T(8,128)(2,1)}, u32[]{:S(2)}, u32[]{:S(2)}) collective-permute-start(bf16[1,256,2048]{2,1,0:T(8,128)(2,1)} %collective-permute-done.7.refs_0_), channel_id=1, source_target_pairs={{0,1},{1,2},{2,3},{3,0},{4,5},{5,6},{6,7},{7,4},{8,9},{9,10},{10,1... | collective-permute-start | bytes 3145736 | tf_op jit(solution)/shard_map/ppermute | solution.py:87
  163.4 30.5 %collective-permute-start.19 = (bf16[1,256,2048]{2,1,0:T(8,128)(2,1)}, bf16[1,256,2048]{2,1,0:T(8,128)(2,1)}, u32[]{:S(2)}, u32[]{:S(2)}) collective-permute-start(bf16[1,256,2048]{2,1,0:T(8,128)(2,1)} %param.12), channel_id=1, source_target_pairs={{0,4},{1,5},{2,6},{3,7},{4,0},{5,1},{6,2},{7,3},{8,12},{9,13},{10,... | collective-permute-start | bytes 3145736 | tf_op jit(solution)/shard_map/ppermute | solution.py:87
  164.3 29.6 %collective-permute-start.16 = (bf16[1,256,2048]{2,1,0:T(8,128)(2,1)}, bf16[1,256,2048]{2,1,0:T(8,128)(2,1)}, u32[]{:S(2)}, u32[]{:S(2)}) collective-permute-start(bf16[1,256,2048]{2,1,0:T(8,128)(2,1)} %collective-permute-done.11.refs_0_), channel_id=1, source_target_pairs={{0,4},{1,5},{2,6},{3,7},{4,0},{5,1},{6,2},{7,3},{8,12},{9,13},{10,... | collective-permute-start | bytes 3145736 | tf_op jit(solution)/shard_map/ppermute | solution.py:87
  164.4 29.5 %collective-permute-start.15 = (bf16[1,256,2048]{2,1,0:T(8,128)(2,1)}, bf16[1,256,2048]{2,1,0:T(8,128)(2,1)}, u32[]{:S(2)}, u32[]{:S(2)}) collective-permute-start(bf16[1,256,2048]{2,1,0:T(8,128)(2,1)} %collective-permute-done.11.refs_0_), channel_id=1, source_target_pairs={{0,1},{1,2},{2,3},{3,0},{4,5},{5,6},{6,7},{7,4},{8,9},{9,10},{10,1... | collective-permute-start | bytes 3145736 | tf_op jit(solution)/shard_map/ppermute | solution.py:87
  224.2 29.2 %collective-permute-start.24 = (bf16[1,256,2048]{2,1,0:T(8,128)(2,1)S(1)}, bf16[1,256,2048]{2,1,0:T(8,128)(2,1)S(1)}, u32[]{:S(2)}, u32[]{:S(2)}) collective-permute-start(bf16[1,256,2048]{2,1,0:T(8,128)(2,1)S(1)} %collective-permute-done.22), channel_id=1, source_target_pairs={{1,0},{2,1},{5,4},{6,5},{9,8},{10,9},{13,12},{14,13},{17,16},{18,1... | collective-permute-start | bytes 3145736 | tf_op jit(solution)/shard_map/ppermute | solution.py:87
  225.5 27.9 %collective-permute-start.25 = (bf16[1,256,2048]{2,1,0:T(8,128)(2,1)S(1)}, bf16[1,256,2048]{2,1,0:T(8,128)(2,1)S(1)}, u32[]{:S(2)}, u32[]{:S(2)}) collective-permute-start(bf16[1,256,2048]{2,1,0:T(8,128)(2,1)S(1)} %collective-permute-done.21), channel_id=1, source_target_pairs={{1,5},{2,6},{3,7},{5,1},{6,2},{7,3},{9,13},{10,14},{11,15},{13,9},... | collective-permute-start | bytes 3145736 | tf_op jit(solution)/shard_map/ppermute | solution.py:87
  226.2 27.1 %collective-permute-start.26 = (bf16[1,256,2048]{2,1,0:T(8,128)(2,1)S(1)}, bf16[1,256,2048]{2,1,0:T(8,128)(2,1)S(1)}, u32[]{:S(2)}, u32[]{:S(2)}) collective-permute-start(bf16[1,256,2048]{2,1,0:T(8,128)(2,1)S(1)} %collective-permute-done.22), channel_id=1, source_target_pairs={{0,4},{1,5},{2,6},{4,0},{5,1},{6,2},{8,12},{9,13},{10,14},{12,8},{... | collective-permute-start | bytes 3145736 | tf_op jit(solution)/shard_map/ppermute | solution.py:87
  257.7 26.9 %collective-permute-start.28 = (bf16[1,256,2048]{2,1,0:T(8,128)(2,1)}, bf16[1,256,2048]{2,1,0:T(8,128)(2,1)S(1)}, u32[]{:S(2)}, u32[]{:S(2)}) collective-permute-start(bf16[1,256,2048]{2,1,0:T(8,128)(2,1)} %copy-done.19), channel_id=1, source_target_pairs={{1,0},{5,4},{9,8},{13,12},{17,16},{21,20},{25,24},{29,28}} | collective-permute-start | bytes 3145736 | tf_op jit(solution)/shard_map/ppermute | solution.py:87
  284.6 103.0 %all-to-all-start.3 = ((bf16[1,4,256,2048]{3,2,0,1:T(8,128)(2,1)}), bf16[1,4,256,2048]{3,2,0,1:T(8,128)(2,1)}, u32[]{:S(2)}, u32[]{:S(2)}) async-start(bf16[1,4,256,2048]{3,2,0,1:T(8,128)(2,1)} %bitcast.156), calls=%async_computation.3 | async-start | bytes 8388608 | tf_op jit(solution)/shard_map/all_to_all | solution.py:900
  347.5 33.6 %collective-permute-start.34 = (bf16[1,1024,2048]{2,1,0:T(8,128)(2,1)}, bf16[1,1024,2048]{2,1,0:T(8,128)(2,1)}, u32[]{:S(2)}, u32[]{:S(2)}) collective-permute-start(bf16[1,1024,2048]{2,1,0:T(8,128)(2,1)} %bitcast.164), channel_id=1, source_target_pairs={{0,4},{1,5},{2,6},{3,7},{4,0},{5,1},{6,2},{7,3},{8,12},{9,13},{10,... | collective-permute-start | bytes 12582920 | tf_op jit(solution)/shard_map/ppermute | solution.py:87
  387.6 97.9 %all-to-all-start.4 = ((bf16[1,4,256,2048]{3,2,0,1:T(8,128)(2,1)}), bf16[1,4,256,2048]{3,2,0,1:T(8,128)(2,1)}, u32[]{:S(2)}, u32[]{:S(2)}) async-start(bf16[1,4,256,2048]{3,2,0,1:T(8,128)(2,1)} %bitcast.155), calls=%async_computation.4 | async-start | bytes 8388608 | tf_op jit(solution)/shard_map/all_to_all | solution.py:900
  417.7 32.2 %collective-permute-start.39 = (bf16[2,256,896]{2,1,0:T(8,128)(2,1)}, bf16[2,256,896]{2,1,0:T(8,128)(2,1)S(1)}, u32[]{:S(2)}, u32[]{:S(2)}) collective-permute-start(bf16[2,256,896]{2,1,0:T(8,128)(2,1)} %get-tuple-element.404), channel_id=1, source_target_pairs={{0,8},{1,9},{2,10},{3,11},{4,12},{5,13},{6,14},{7,15},{8,0},{9,1},... | collective-permute-start | bytes 2752520 | tf_op jit(solution)/shard_map/ppermute | solution.py:87
  418.5 31.4 %collective-permute-start.40 = (bf16[2,256,896]{2,1,0:T(8,128)(2,1)}, bf16[2,256,896]{2,1,0:T(8,128)(2,1)S(1)}, u32[]{:S(2)}, u32[]{:S(2)}) collective-permute-start(bf16[2,256,896]{2,1,0:T(8,128)(2,1)} %get-tuple-element.406), channel_id=1, source_target_pairs={{0,16},{1,17},{2,18},{3,19},{4,20},{5,21},{6,22},{7,23},{8,24},{9,... | collective-permute-start | bytes 2752520 | tf_op jit(solution)/shard_map/ppermute | solution.py:87
  535.4 46.9 %all-to-all-start.7 = ((bf16[4,2,64,1024]{3,2,1,0:T(8,128)(2,1)}), bf16[4,2,64,1024]{3,2,1,0:T(8,128)(2,1)S(1)}, u32[]{:S(2)}, u32[]{:S(2)}) async-start(bf16[4,2,64,1024]{3,2,1,0:T(8,128)(2,1)} %final_blocks.5), calls=%async_computation.7 | async-start | bytes 2097152 | tf_op jit(solution)/shard_map/all_to_all | solution.py:1096
  543.4 33.4 %collective-permute-start.50 = (bf16[64,2048]{1,0:T(8,128)(2,1)S(1)}, bf16[64,2048]{1,0:T(8,128)(2,1)S(1)}, u32[]{:S(2)}, u32[]{:S(2)}) collective-permute-start(bf16[64,2048]{1,0:T(8,128)(2,1)S(1)} %fusion.14), channel_id=1, source_target_pairs={{0,0},{8,1},{16,2},{24,3},{4,4},{12,5},{20,6},{28,7},{1,8},{9,9},{... | collective-permute-start | bytes 786440 | tf_op jit(solution)/shard_map/ppermute | solution.py:1202
  (82 other events, 1074.9 us)

commit v3 on v2

--- a/solution.py
+++ b/solution.py
@@ -103,7 +103,7 @@
         for r in range(self.nd * self.nz):
             head, quarter = r // self.groups, r % self.groups
             s, c = head // self.pair, head % self.pair
-            pairs.append((r, (quarter * self.pair + c) * self.nz + s))
+            pairs.append((r, ((quarter ^ s) * self.pair + c) * self.nz + s))
         return pairs
 
 
@@ -147,9 +147,12 @@
                 self.held[m ^ bit] = (self.lay.group_hop(self.block(m), bit), 0)
 
     @staticmethod
-    def send_first(halves):
+    def stack(halves):
+        return jnp.concatenate([h.block(0) for h in halves])
+
+    @staticmethod
+    def send_first(halves, stack):
         lay = halves[0].lay
-        stack = jnp.concatenate([h.block(0) for h in halves])
         for bit in bits_of(lay.groups, False):
             got = lay.group_hop(stack, bit)
             first = 0
@@ -349,6 +352,46 @@
         refs[-1][...] = lanes
 
 
+def columns_kernel(unit, hd, t_ref, dy_ref, du_ref, *refs):
+    out_ref = refs[-1]
+    width = out_ref.shape[0]
+    t = t_ref[0]
+    place = lax.broadcasted_iota(jnp.int32, (1, width), 1)
+    dy = jnp.sum(dy_ref[...].astype(f32), axis=0, keepdims=True)
+    dp = sum(jnp.sum(ref[:, 0], axis=0, keepdims=True) for ref in refs[:-1])
+    blank = jnp.zeros((1, width), f32)
+    rows = [blank] * 4 + [dy, dy]
+    for j in range(3):
+        head = jnp.concatenate([dp[:, j * hd : (j + 1) * hd]] * (width // hd), axis=1)
+        rows.append(jnp.where(place // hd == t, head, 0.0))
+    share = width // unit
+    units = jnp.concatenate([du_ref[0:1]] * share, axis=1)
+    for k in range(HEADS // share):
+        rows.append(jnp.where(place // unit + k * share == t, units, 0.0))
+    rows += [blank] * (LANES - len(rows))
+    out_ref[...] = jnp.concatenate(rows).T
+
+
+def plain_columns(lay, dy, du_sums, dp_sums, unit, hd):
+    tokens, width = dy.shape
+
+    def whole(v):
+        return pl.BlockSpec(v.shape, lambda i, t: (0,) * v.ndim)
+
+    return pl.pallas_call(
+        partial(columns_kernel, unit, hd),
+        grid_spec=pltpu.PrefetchScalarGridSpec(
+            num_scalar_prefetch=1,
+            grid=(1,),
+            in_specs=[whole(v) for v in (dy, du_sums, *dp_sums)],
+            out_specs=pl.BlockSpec((width, LANES), lambda i, t: (0, 0)),
+        ),
+        out_shape=jax.ShapeDtypeStruct((width, LANES), f32),
+        name="plain_columns",
+        **params((tokens * width, 4 * tokens * width)),
+    )(jnp.reshape(lay.t, (1,)).astype(jnp.int32), dy, du_sums, *dp_sums)
+
+
 def gradient_call(lay, kernel, left, rights, by_rows, n, more=()):
     tokens, width = left.shape
     pair, half = lay.pair, lay.groups // 2
@@ -561,7 +604,8 @@
 
     outs = [out(n) for n in (width, wide, unit, unit)]
     in_specs = [pl.BlockSpec((1, tile, width), row_map(q)) for q in range(places) for _ in range(pair)]
-    in_specs += [whole(v) for v in (vec, w_qu, qkv_bias, up_bias)]
+    in_specs += [pl.BlockSpec((8, width), lambda i, p, j, pos: (0, 0))]
+    in_specs += [whole(v) for v in (w_qu, qkv_bias, up_bias)]
     in_specs += [pl.BlockSpec((3, tile, LANES), lambda i, p, j, pos: (0, pos[p] * steps + j, 0))]
     in_specs += [pl.BlockSpec(memory_space=pl.ANY)] * len(held)
     tokens = pair * places * count * span
@@ -626,7 +670,8 @@
     )(qkv)
 
 
-def attn_bwd_kernel(quarter, scale, tile, dy_ref, wo_ref, qkv_ref, lse_ref, tab_ref, dp_ref, sum_ref, do_s, dk_s, dv_s):
+def attn_bwd_kernel(quarter, scale, tile, dy_ref, wo_ref, qkv_ref, lse_ref, tab_ref, *refs):
+    dp_ref, sum_ref, do_s, dk_s, dv_s = refs[-5:]
     length = dy_ref.shape[1]
     hd = wo_ref.shape[0]
     cosine, low_sine, high_sine = tab_ref[0], -tab_ref[1], -tab_ref[2]
@@ -668,61 +713,95 @@
     sum_ref[0] = jnp.broadcast_to(total, sum_ref.shape[1:])
 
 
-def attn_backward(dy, w_out, qkv, lse, tables, scale):
+def attn_backward(dy, w_out, qkv, lse, tables, scale, part, parts, held):
     seqs, length, width = dy.shape
     hd = w_out.shape[0]
-    flops = 2 * seqs * length * (hd * width + 5 * length * hd)
+    share = seqs // parts
+    first = part * share
+    flops = 2 * share * length * (hd * width + 5 * length * hd)
+
+    def row_map(s):
+        return (first + s, 0, 0)
+
     return pl.pallas_call(
         partial(attn_bwd_kernel, hd // 8, scale, min(256, length)),
-        grid=(seqs,),
+        grid=(share,),
         in_specs=[
-            pl.BlockSpec((1, length, width), lambda s: (s, 0, 0)),
+            pl.BlockSpec((1, length, width), row_map),
             pl.BlockSpec(w_out.shape, lambda s: (0, 0)),
-            pl.BlockSpec((1, length, 3 * hd), lambda s: (s, 0, 0)),
-            pl.BlockSpec((1, length, LANES), lambda s: (s, 0, 0)),
+            pl.BlockSpec((1, length, 3 * hd), row_map),
+            pl.BlockSpec((1, length, LANES), row_map),
             pl.BlockSpec(tables.shape, lambda s: (0, 0, 0)),
-        ],
+        ]
+        + [pl.BlockSpec(memory_space=pl.ANY)] * len(held),
         out_specs=[
-            pl.BlockSpec((1, length, 3 * hd), lambda s: (s, 0, 0)),
+            pl.BlockSpec((1, length, 3 * hd), row_map),
             pl.BlockSpec((1, 8, 3 * hd), lambda s: (s, 0, 0)),
         ],
         out_shape=[
             jax.ShapeDtypeStruct((seqs, length, 3 * hd), bf16),
-            jax.ShapeDtypeStruct((seqs, 8, 3 * hd), f32),
+            jax.ShapeDtypeStruct((share, 8, 3 * hd), f32),
         ],
+        input_output_aliases={5 + k: k for k in range(len(held))},
         scratch_shapes=[
             pltpu.VMEM((length, hd), bf16),
             pltpu.VMEM((length, hd), f32),
             pltpu.VMEM((length, hd), f32),
         ],
         name="attn_backward",
-        **params((flops, 8 * seqs * length * width)),
-    )(dy, w_out, qkv, lse, tables)
-
-
-def output_kernel(g_ref, wd_ref, o_ref, wo_ref, out_ref):
+        **params((flops, 8 * share * length * width)),
+    )(dy, w_out, qkv, lse, tables, *held)
+
+
+def write_chunk(outs, more, total):
+    for ref in more:
+        total = total + ref[0].astype(f32)
+    total = total.astype(bf16)
+    if len(outs) == 1:
+        outs[0][0] = total
+    else:
+        for k, out in enumerate(outs):
+
+            @pl.when(pl.program_id(0) == k)
+            def _(out=out):
+                out[0] = total
+
+
+def chunk_outputs(order_len, span, width, separate):
+    if separate:
+        specs = [pl.BlockSpec((1, span, width), lambda i, order: (0, 0, 0))] * order_len
+        return specs, [jax.ShapeDtypeStruct((1, span, width), bf16)] * order_len
+    specs = [pl.BlockSpec((1, span, width), lambda i, order: (i, 0, 0))]
+    return specs, [jax.ShapeDtypeStruct((order_len, span, width), bf16)]
+
+
+def output_kernel(count, order_ref, g_ref, wd_ref, o_ref, wo_ref, *refs):
     total = dot(g_ref[...], wd_ref[...], 1, 1) + dot(o_ref[...], wo_ref[...])
-    out_ref[...] = total.astype(bf16)
-
-
-def output_forward(g, w_down, o, w_out, tile, part, parts):
-    tokens, unit = g.shape[0] // parts, g.shape[1]
-    width, hd = w_down.shape[0], o.shape[1]
-    first = part * tokens // tile
+    write_chunk(refs[count:], refs[:count], total)
+
+
+def output_forward(g, w_down, o, w_out, span, order, first, more=(), separate=False):
+    unit, width, hd = g.shape[1], w_down.shape[0], o.shape[1]
+    steps = order.shape[0]
+    out_specs, out_shape = chunk_outputs(steps, span, width, separate)
     return pl.pallas_call(
-        output_kernel,
-        grid=(tokens // tile,),
-        in_specs=[
-            pl.BlockSpec((tile, unit), lambda i: (first + i, 0)),
-            pl.BlockSpec(w_down.shape, lambda i: (0, 0)),
-            pl.BlockSpec((tile, hd), lambda i: (first + i, 0)),
-            pl.BlockSpec(w_out.shape, lambda i: (0, 0)),
-        ],
-        out_specs=pl.BlockSpec((tile, width), lambda i: (i, 0)),
-        out_shape=jax.ShapeDtypeStruct((tokens, width), bf16),
+        partial(output_kernel, len(more)),
+        grid_spec=pltpu.PrefetchScalarGridSpec(
+            num_scalar_prefetch=1,
+            grid=(steps,),
+            in_specs=[
+                pl.BlockSpec((span, unit), lambda i, order: (first + order[i], 0)),
+                pl.BlockSpec(w_down.shape, lambda i, order: (0, 0)),
+                pl.BlockSpec((span, hd), lambda i, order: (first + order[i], 0)),
+                pl.BlockSpec(w_out.shape, lambda i, order: (0, 0)),
+            ]
+            + [pl.BlockSpec((1, span, width), lambda i, order: (i, 0, 0))] * len(more),
+            out_specs=out_specs,
+        ),
+        out_shape=out_shape,
         name="output_forward",
-        **params((2 * tokens * width * (unit + hd), 8 * tokens * width)),
-    )(g, w_down, o, w_out)
+        **params((2 * steps * span * width * (unit + hd), 8 * steps * span * width)),
+    )(order, g, w_down, o, w_out, *more)
 
 
 def hidden_kernel(dy_ref, wd_ref, slope_ref, du_ref, sum_ref):
@@ -764,37 +843,40 @@
     )(dy, w_down, slope)
 
 
-def input_kernel(hd, du_ref, dp_ref, wu_ref, wq_ref, wk_ref, wv_ref, vec_ref, z_ref):
+def input_kernel(count, hd, order_ref, du_ref, dp_ref, wu_ref, wq_ref, wk_ref, wv_ref, vec_ref, *refs):
     da = (
         dot(dp_ref[:, :hd], wq_ref[...], 1, 1)
         + dot(dp_ref[:, hd : 2 * hd], wk_ref[...], 1, 1)
         + dot(dp_ref[:, 2 * hd :], wv_ref[...], 1, 1)
     )
     dm = dot(du_ref[...], wu_ref[...], 1, 1)
-    z_ref[...] = (da * vec_ref[0:1] + dm * vec_ref[2:3]).astype(bf16)
-
-
-def input_backward(du, dp, w_qu, vec, tile, seq, seqs):
-    tokens, unit = du.shape
-    width, hd = w_qu.shape[0], dp.shape[1] // 3
-    first = unit // hd
-    steps = tokens // seqs // tile
-    flops = 2 * tokens // seqs * width * (unit + 3 * hd)
+    write_chunk(refs[count:], refs[:count], da * vec_ref[0:1] + dm * vec_ref[2:3])
+
+
+def input_backward(du, dp, w_qu, vec, span, order, first, more=(), separate=False):
+    unit, width, hd = du.shape[1], w_qu.shape[0], dp.shape[1] // 3
+    columns = unit // hd
+    steps = order.shape[0]
+    out_specs, out_shape = chunk_outputs(steps, span, width, separate)
     return pl.pallas_call(
-        partial(input_kernel, hd),
-        grid=(steps,),
-        in_specs=[
-            pl.BlockSpec((tile, unit), lambda i: (seq * steps + i, 0)),
-            pl.BlockSpec((tile, 3 * hd), lambda i: (seq * steps + i, 0)),
-            pl.BlockSpec((width, unit), lambda i: (0, 0)),
-        ]
-        + [pl.BlockSpec((width, hd), lambda i, j=j: (0, first + j)) for j in range(3)]
-        + [pl.BlockSpec(vec.shape, lambda i: (0, 0))],
-        out_specs=pl.BlockSpec((tile, width), lambda i: (i, 0)),
-        out_shape=jax.ShapeDtypeStruct((tokens // seqs, width), bf16),
+        partial(input_kernel, len(more), hd),
+        grid_spec=pltpu.PrefetchScalarGridSpec(
+            num_scalar_prefetch=1,
+            grid=(steps,),
+            in_specs=[
+                pl.BlockSpec((span, unit), lambda i, order: (first + order[i], 0)),
+                pl.BlockSpec((span, 3 * hd), lambda i, order: (first + order[i], 0)),
+                pl.BlockSpec((width, unit), lambda i, order: (0, 0)),
+            ]
+            + [pl.BlockSpec((width, hd), lambda i, order, j=j: (0, columns + j)) for j in range(3)]
+            + [pl.BlockSpec((8, width), lambda i, order: (0, 0))]
+            + [pl.BlockSpec((1, span, width), lambda i, order: (i, 0, 0))] * len(more),
+            out_specs=out_specs,
+        ),
+        out_shape=out_shape,
         name="input_backward",
-        **params((flops, 12 * tokens // seqs * width)),
-    )(du, dp, w_qu, w_qu, w_qu, w_qu, vec)
+        **params((2 * steps * span * width * (unit + 3 * hd), 12 * steps * span * width)),
+    )(order, du, dp, w_qu, w_qu, w_qu, w_qu, vec, *more)
 
 
 def adam_kernel(pair, places, rate, c_ref, *refs):
@@ -841,66 +923,101 @@
     )(jnp.reshape(lay.c, (1,)).astype(jnp.int32), *operands)
 
 
-class LineGather:
+class SeqGather:
     def __init__(self, lay, own):
         self.lay = lay
-        self.up = self.down = own
-        self.fresh = [(own, lay.z, lambda z: True)]
-        self.todo = []
-        self.out = None
-        self.count = own.shape[0]
-
-    def step(self, k):
-        lay, n = self.lay, self.lay.nz
-        self.up = lay.hop(self.up, lambda g, c, z: (g, c, z + 1) if k - 1 <= z < n - 1 else None)
-        self.down = lay.hop(self.down, lambda g, c, z: (g, c, z - 1) if 1 <= z <= n - k else None)
-        self.fresh.append((self.up, lay.z - k, lambda z: z >= k))
-        self.fresh.append((self.down, lay.z + k, lambda z: z + k < n))
-
-    def cross(self, keep=0):
-        lay = self.lay
-        due = len(self.fresh) - keep
-        now, self.fresh = self.fresh[:due], self.fresh[due:]
-        for piece, where, valid in now:
-            ok = jnp.logical_and(where >= 0, where < lay.nz)
-            for r in range(lay.pair):
-                got = piece
-                if r:
-                    got = lay.hop(piece, lambda g, c, z: (g, c ^ r, z) if valid(z) else None)
-                for s in range(self.count):
-                    slot = (r * self.count + s) * lay.nz + where
-                    self.todo.append((got[s], jnp.where(ok, slot, -1)))
+        self.rounds, self.at = lay.nz - 1, 0
+        self.newest = own
+        self.places, self.fresh = [lay.z], [own]
+
+    def step(self):
+        self.at += 1
+        self.newest = self.lay.ring(self.newest)
+        self.fresh.append(self.newest)
+        self.places.append((self.lay.z - self.at) % self.lay.nz)
+
+    def take(self):
+        items = list(zip(self.fresh, self.places))
+        self.fresh, self.places = [], []
+        return items
 
     @property
     def state(self):
-        return (self.up, self.down, [v[0] for v in self.fresh], [v for v, _ in self.todo], self.out)
+        return (self.newest, self.fresh)
 
     @state.setter
     def state(self, state):
-        self.up, self.down, fresh, blocks, self.out = state
-        self.fresh = [(v,) + w[1:] for v, w in zip(fresh, self.fresh)]
+        self.newest, self.fresh = state
+
+
+class TokenBuffer:
+    def __init__(self, lay):
+        self.lay, self.todo, self.out = lay, [], None
+
+    def add(self, items):
+        for pieces, where in items:
+            for r, piece in enumerate(pieces):
+                for s in range(piece.shape[0]):
+                    self.todo.append((piece[s], (r * piece.shape[0] + s) * self.lay.nz + where))
+
+    def flush(self, count):
+        blocks, slots = [(v, 0) for v, _ in self.todo], [w for _, w in self.todo]
+        total = self.lay.pair * self.lay.nz * count
+        self.out = place(blocks, slots, blocks[0][0].shape[0], total, self.out)
+        self.todo = []
+        return self.out
+
+    @property
+    def state(self):
+        return ([v for v, _ in self.todo], self.out)
+
+    @state.setter
+    def state(self, state):
+        blocks, self.out = state
         self.todo = [(v, w) for v, (_, w) in zip(blocks, self.todo)]
 
-    def flush(self, keep=0):
-        due = len(self.todo) - keep
-        now, self.todo = self.todo[:due], self.todo[due:]
-        total = self.lay.pair * self.lay.nz * self.count
-        blocks, slots = [(v, 0) for v, _ in now], [w for _, w in now]
-        self.out = place(blocks, slots, blocks[0][0].shape[0], total, self.out)
-        return self.out
-
 
 class SeqScatter:
-    def __init__(self, lay, parts, count):
-        _, length, width = parts[0].shape
-        total = sum(p.astype(f32) for p in parts).astype(bf16)
-        self.state = total.reshape(count, lay.nz, length // lay.nz, width)
+    def __init__(self, lay):
+        self.lay = lay
+        self.four = lay.nz == 4
+        if self.four:
+            roles = [[3, 2, 1, 0], [0, 2, 3, 1], [3, 1, 0, 2], [0, 1, 2, 3]]
+        else:
+            roles = [list(range(lay.nz))] * lay.nz
+        self.order = jnp.array(roles, jnp.int32)[lay.z]
+
+    def load(self, chunks):
+        self.state = list(chunks)
+
+    def move(self, value, targets):
+        return self.lay.hop(value, lambda g, c, z: (g, c, targets[z]) if z in targets else None)
 
     def send(self):
-        self.state = lax.all_to_all(self.state, "seq", 1, 1, tiled=True)
+        if not self.four:
+            self.state = [lax.all_to_all(self.state[0], "seq", 0, 0, tiled=True)]
+            return
+        near, far, last, own = self.state
+        near = self.move(near, {0: 1, 3: 2, 2: 3, 1: 0})
+        across = self.move(far, {0: 2, 3: 1})
+        beside = self.move(far, {1: 2, 2: 1})
+        self.state = [near, across, beside, last, own]
+
+    def finish(self):
+        if not self.four:
+            return
+        near, across, beside, last, own = self.state
+        inner = jnp.logical_and(self.lay.z > 0, self.lay.z < 3)
+        passed = jnp.where(inner, last.astype(f32) + near.astype(f32), last.astype(f32)).astype(bf16)
+        came = self.move(passed, {1: 3, 2: 0, 0: 1, 3: 2})
+        self.state = [near, across, beside, came, own]
 
     def result(self):
-        return jnp.sum(self.state.astype(f32), axis=1)
+        if not self.four:
+            return jnp.sum(self.state[0].astype(f32), axis=0)
+        near, across, beside, came, own = (v[0].astype(f32) for v in self.state)
+        inner = jnp.logical_and(self.lay.z > 0, self.lay.z < 3)
+        return own + came + jnp.where(inner, across + beside, near)
 
 
 def body(
@@ -943,9 +1060,9 @@
         return lax.all_to_all(half, "seq", 0, 0, tiled=True).reshape(nz * rows, -1)
 
     class Whole:
-        def __init__(self, halves, size=None, first=0):
+        def __init__(self, halves, size=None, first=0, turn=0):
             self.halves, self.seen, self.state = halves, set(), None
-            self.size, self.first = size or halves[0].rows, first
+            self.size, self.first, self.turn = size or halves[0].rows, first, turn
 
         def flush(self):
             items = [
@@ -958,7 +1075,8 @@
             if items:
                 count = len(self.halves)
                 slots = [
-                    (lay.g ^ m) * count + (lay.c ^ r if count > 1 else 0) for r, m, _ in items
+                    (lay.g ^ m ^ self.turn) * count + (lay.c ^ r if count > 1 else 0)
+                    for r, m, _ in items
                 ]
                 blocks = [v for _, _, v in items]
                 self.state = place(blocks, slots, self.size, groups * count, self.state)
@@ -994,10 +1112,10 @@
     rest = [swap(qu_sources, r) for r in range(1, pair)]
     w_out = attn_params[:, 3 * width :].astype(bf16)
     dn = jnp.stack([prepare(lay, r, dn_sources) for r in range(pair)], axis=1)
-    first, rest, w_out, dn = join(first, rest, w_out, dn)
+    w_out = lax.ppermute(w_out, AXES, lay.head_owner_perm())
+    first, rest, w_out, dn, tables = join(first, rest, w_out, dn, tables)
 
     qu = [GroupGather(lay, first, False)]
-    w_out = lax.ppermute(w_out, AXES, lay.head_owner_perm())
     for r in range(1, pair):
         one = exchange(rest[r - 1])
         qu[-1].send(0)
@@ -1005,11 +1123,17 @@
         qu.append(GroupGather(lay, one, bool(r % 2)))
     dn = lax.all_to_all(dn, "seq", 0, 0, tiled=True)
     qu[-1].send(0)
-    pieces = crossed(inputs)
-    newest, dn, pieces, w_out = joined(qu, inputs, dn, pieces, w_out)
+    xs, dy, dy_buffer = SeqGather(lay, inputs), SeqGather(lay, cotangent), TokenBuffer(lay)
+
+    def crossing(items):
+        return [(crossed(v), place) for v, place in items]
+
+    (own,) = crossing(xs.take())
+    own_pieces, dn, w_out = joined(qu + [xs], own[0], dn, w_out)
+    ready = [(own_pieces, own[1])]
 
     w_qu = Whole(qu)
-    newest = lay.ring(newest)
+    xs.step()
     dn = [lay.core_hop(dn[:, r], r) if r else dn[:, r] for r in range(pair)]
     dn = [v.reshape(nz * rows, unit) for v in dn]
     dn[-1] = jnp.concatenate([dn[-1], w_out.reshape(-1, unit)])
@@ -1017,76 +1141,80 @@
     w_qu.flush()
     for v in qu:
         v.send(1)
-    newest, pieces = joined(qu + dn + [w_qu], newest, pieces)
+    (dn_stack,) = joined(qu + dn + [w_qu, xs], GroupGather.stack(dn))
     for v in qu:
         v.rest(2)
 
     w_qkvu = w_qu.result()
     vectors = last_columns(w_qkvu)
-    norm_vec = vectors[:8]
+    norm_vec = vectors
     qkv_bias = vectors[6:9].reshape(3, HEADS, hd)
     qkv_bias = lax.dynamic_index_in_dim(qkv_bias, lay.t, 1, keepdims=False).reshape(1, 3 * hd)
     up_bias = lax.dynamic_slice(vectors[9:13].reshape(-1), (lay.t * unit,), (unit,))[None]
     out_bias = vectors[4] + vectors[5]
     held = ()
 
-    def forward_piece(pieces, steps_away, held):
-        where = [(lay.z - k) % nz for k in steps_away]
+    def forward_pieces(items, held):
+        where = [place for _, place in items]
+        pieces = [v for pieces, _ in items for v in pieces]
         return piece_forward(
             lay, pieces, where, norm_vec, w_qkvu, qkv_bias, up_bias, tables, held
         )
 
-    dy = LineGather(lay, cotangent)
-    w_dn, w_wo = Whole(dn, nz * rows), Whole(dn[-1:], rows * width // unit, nz * rows)
-    for k in range(2, nz):
-        last, newest = newest, lay.ring(newest)
-        if k == 2:
-            GroupGather.send_first(dn)
-        elif k == 3:
+    w_dn, w_wo = Whole(dn, nz * rows), Whole(dn[-1:], rows * width // unit, nz * rows, lay.z)
+    tick = 0
+    while xs.at < xs.rounds:
+        taken = xs.take()
+        xs.step()
+        if tick == 0:
+            GroupGather.send_first(dn, dn_stack)
+        elif tick == 1:
+            w_dn.flush()
+            w_wo.flush()
             for v in dn:
                 v.send(1)
-            w_dn.flush()
-            w_wo.flush()
-            dy.cross()
-        next_pieces = crossed(last)
-        held = forward_piece(pieces, [k - 2], held)
-        newest, pieces, held = joined(dn + [w_dn, w_wo, dy], newest, next_pieces, held)
+        held = forward_pieces(ready, held)
+        ready = crossing(taken)
+        ready_pieces, held = joined(dn + [w_dn, w_wo, xs], [v for v, _ in ready], held)
+        ready = list(zip(ready_pieces, [place for _, place in ready]))
+        tick += 1
     for v in dn:
         v.rest(2)
 
-    dy.step(1)
-    last_pieces = crossed(newest)
-    held = forward_piece(pieces + last_pieces, [nz - 2, nz - 1], held)
+    taken = xs.take()
+    own_dy = dy.take()
+    dy.step()
+    held = forward_pieces(ready + crossing(taken), held)
+    dy_buffer.add(crossing(own_dy))
+    (held,) = joined([dy, dy_buffer, w_dn, w_wo] + dn, held)
     w_down = w_dn.result()
     w_out = w_wo.result().reshape(hd, width)
-    held, w_down, w_out = joined([dy], held, w_down, w_out)
     tile = min(512, length)
     flat = (tokens_here, width)
     x_flat, qkv, g, slope = (v.reshape(seqs, length, -1) for v in held)
     x_flat, g, slope = (v.reshape(tokens_here, -1) for v in (x_flat, g, slope))
 
-    dy.cross()
-    dy.step(2)
+    taken = dy.take()
+    dy.step()
+    dy_buffer.add(crossing(taken))
     o, lse = attn_forward(qkv, score_scale)
     o = o.reshape(tokens_here, hd)
-    out_parts = {}
-
-    def output_part(r):
-        part = output_forward(g, w_down, o, w_out, tile, r, pair)
-        return part.reshape(count, length, width)
-
+    out_sum = SeqScatter(lay)
+    parts = {}
     for r in range(1, pair):
-        out_parts[r] = output_part(r)
-    out_parts, o, lse, g = joined([dy], out_parts, o, lse, g)
-
-    for k in range(3, nz):
-        dy.step(k)
-    for r in range(1, pair):
-        out_parts[r] = lay.core_hop(out_parts[r], r)
-    dy.cross(2 * (nz - 3))
-    out_parts[0] = output_part(0)
-    out_sum = SeqScatter(lay, [out_parts[r] for r in range(pair)], count)
-    o, g = joined([dy, out_sum], o, g)
+        (parts[r],) = output_forward(g, w_down, o, w_out, span, out_sum.order, r * count * nz)
+    o, lse, g, parts, w_down, w_out = joined([dy, dy_buffer], o, lse, g, parts, w_down, w_out)
+
+    taken = dy.take()
+    while dy.at < dy.rounds:
+        dy.step()
+    dy_buffer.flush(count)
+    more = [lay.core_hop(parts[r], r) for r in range(1, pair)]
+    dy_buffer.add(crossing(taken))
+    out_sum.load(
+        output_forward(g, w_down, o, w_out, span, out_sum.order, 0, more, separate=out_sum.four)
+    )
+    o, lse, g = joined([dy, dy_buffer, out_sum], o, lse, g)
 
     def steps(*parts):
         for p in parts:
@@ -1109,95 +1237,112 @@
             steps(*parts)
 
     out_sum.send()
-    dy.cross()
-    dy_all = dy.flush().reshape(seqs, length, width)
-    dy_flat = dy_all.reshape(flat)
-    du, du_sums = hidden_backward(dy_flat, w_down, slope, tile)
-    dy_flat, du, du_sums = join(dy_flat, du, du_sums)
-
-    dp, dp_sums = attn_backward(
-        dy_flat.reshape(seqs, length, width), w_out, qkv, lse, tables, score_scale
-    )
-    dp = dp.reshape(tokens_here, 3 * hd)
-
-    def input_part(r):
-        part = input_backward(du, dp, w_qkvu, norm_vec, tile, r, pair)
-        return part.reshape(count, length, width)
-
-    z_parts = {r: input_part(r) for r in range(1, pair)}
-    z_parts, du, dp, du_sums, dp_sums = join(z_parts, du, dp, du_sums, dp_sums)
+    dy_buffer.add(crossing(dy.take()))
+    dy_all = dy_buffer.flush(count).reshape(seqs, length, width)
+    down = gradient(lay, dy_all.reshape(flat), g)
+    (dy_all,) = joined(down, dy_all)
+
+    z_sum = SeqScatter(lay)
+    dp, dp_sums, z_parts = (), {}, {}
+
+    def attention_part(r, held):
+        *held, dp_sums[r] = attn_backward(
+            dy_all, w_out, qkv, lse, tables, score_scale, r, pair, held
+        )
+        return held
+
+    def input_part(r, more=(), separate=False):
+        return input_backward(
+            du,
+            dp[0].reshape(tokens_here, 3 * hd),
+            w_qkvu,
+            norm_vec,
+            span,
+            z_sum.order,
+            r * count * nz,
+            more,
+            separate,
+        )
+
+    steps(*down)
+    du, du_sums = hidden_backward(dy_all.reshape(flat), w_down, slope, tile)
+    dy_all = after(dy_all, du)
+    for r in range(1, pair):
+        dp = attention_part(r, dp)
+    dy_all, du, du_sums, dp, dp_sums = joined([out_sum] + down, dy_all, du, du_sums, dp, dp_sums)
+
+    out_sum.finish()
+    more_rounds(down)
+    for r in range(1, pair):
+        (z_parts[r],) = input_part(r)
+    down_blocks = final_blocks(down, nz)
+    dy_all, dp, z_parts, down_blocks = joined([out_sum], dy_all, dp, z_parts, down_blocks)
 
     for r in range(1, pair):
         z_parts[r] = lay.core_hop(z_parts[r], r)
-    z_parts[0] = input_part(0)
-    up, lanes = folded_gradient(lay, x_flat, after(du, z_parts[0]), du_sums, w_qkvu, 0, 2)
-    z_sum = SeqScatter(lay, [z_parts[r] for r in range(pair)], count)
-    dy_flat, dp, du_sums, dp_sums, lanes = joined(
-        up + [out_sum, z_sum], dy_flat, dp, du_sums, dp_sums, lanes
+    down_blocks = to_owners(down_blocks)
+    dp = attention_part(0, dp)
+    z_sum.load(input_part(0, [z_parts[r] for r in range(1, pair)], z_sum.four))
+    dp = dp[0].reshape(tokens_here, 3 * hd)
+    dy_flat, du, dp, dp_sums, down_blocks = joined(
+        [z_sum], dy_all.reshape(flat), du, dp, dp_sums, down_blocks
     )
 
     z_sum.send()
+    up, lanes = folded_gradient(lay, x_flat, du, du_sums, w_qkvu, 0, 2)
+    dp, lanes = joined(up, dp, lanes)
+
+    steps(*up)
     upstream = cotangent.astype(f32)
-    upstream_sum = jnp.sum(upstream, axis=(0, 1))[:, None]
-    dp_sums = jnp.sum(dp_sums[:, 0], axis=0)
-    qkv_columns = lax.dynamic_update_slice(
-        jnp.zeros((width, 3), f32), dp_sums.reshape(3, hd).T, (lay.t * hd, 0)
-    )
-    up_columns = lax.dynamic_update_slice(jnp.zeros((ff,), f32), du_sums[0], (lay.t * unit,))
-    up_columns = up_columns.reshape(ff // width, width).T
-    others = jnp.concatenate(
-        [jnp.zeros((width, 4), f32), upstream_sum, upstream_sum, qkv_columns, up_columns], axis=1
-    )
-    others = jnp.pad(others, ((0, 0), (0, LANES - others.shape[1])))
+    flat_cotangent = cotangent.reshape(count * span, width)
+    others = plain_columns(lay, flat_cotangent, du_sums, list(dp_sums.values()), unit, hd)
+    dp_sums = sum(jnp.sum(v[:, 0], axis=0) for v in dp_sums.values())
     dp_sums = jnp.broadcast_to(dp_sums[None], (8, 3 * hd))
-
-    steps(*up)
     (dqkv,) = folded_gradient(lay, x_flat, dp, dp_sums, w_qkvu, unit, 0, (lanes, others))
-    (dy_flat,) = joined(up + dqkv, dy_flat)
-
+    dy_flat, upstream = joined(up + dqkv + [z_sum], dy_flat, upstream)
+
+    z_sum.finish()
     more_rounds(up)
     steps(*dqkv)
-    down = gradient(lay, dy_flat, g)
-    outputs = (inputs.astype(f32) + out_sum.result() + out_bias).astype(bf16)
-    dy_flat, outputs = joined(up + dqkv + down, dy_flat, outputs)
-
-    more_rounds(dqkv)
-    steps(*down)
-    up_blocks = final_blocks(up, nz)
     out_whole = dot(o, dy_flat, 0, 0)
     out_whole = out_whole.astype(bf16).reshape(groups, rows, width)
     out_whole = jnp.stack(
         [
             lax.dynamic_index_in_dim(
-                out_whole, lay.g ^ GroupScatter.member(lay, i, True), 0, keepdims=False
+                out_whole, lay.g ^ lay.z ^ GroupScatter.member(lay, i, True), 0, keepdims=False
             )
             for i in range(groups)
         ]
     )
     wo = GroupScatter(lay, out_whole[: groups // 2], out_whole[groups // 2 :], True)
-    (up_blocks,) = joined(dqkv + [wo, z_sum], up_blocks)
+    up_blocks = final_blocks(up, nz)
+    (up_blocks,) = joined([wo, z_sum, out_sum], up_blocks)
 
     mlp_state = (mlp_params, mlp_first, mlp_second)
     attn_state = (attn_params, attn_first, attn_second)
     up_blocks = to_owners(up_blocks)
-    more_rounds(down)
+    more_rounds(dqkv)
     steps(wo)
     dqkv_blocks = final_blocks(dqkv, nz)
-    normed_grad = z_sum.result()
+    outputs = (inputs.astype(f32) + out_sum.result().reshape(inputs.shape) + out_bias).astype(bf16)
+    up_blocks, dqkv_blocks, down_blocks, outputs = joined(
+        [wo], up_blocks, dqkv_blocks, down_blocks, outputs
+    )
+
+    dqkv_blocks = to_owners(dqkv_blocks)
+    more_rounds([wo])
+    mlp_result = adam_columns(
+        lay, rate_mlp, at_owner(down_blocks), 0, unit, mlp_state, ff, 1, ()
+    )
+    normed_grad = z_sum.result().reshape(inputs.shape)
     normed, scaling = normalize(inputs.astype(f32))
     grad_mean = jnp.mean(normed_grad, axis=-1, keepdims=True)
     grad_proj = jnp.mean(normed_grad * normed, axis=-1, keepdims=True)
     input_grad = upstream + scaling * (normed_grad - grad_mean - normed * grad_proj)
-    up_blocks, dqkv_blocks, input_grad = joined(down + [wo], up_blocks, dqkv_blocks, input_grad)
-
-    dqkv_blocks = to_owners(dqkv_blocks)
-    more_rounds([wo])
-    down_blocks = final_blocks(down, nz)
     up_parts = at_owner(up_blocks)
-    mlp_result = adam_columns(lay, rate_mlp, up_parts, 0, unit, mlp_state, 0, 1, ())
-    dqkv_blocks, down_blocks, mlp_result = joined([wo], dqkv_blocks, down_blocks, mlp_result)
-
-    down_blocks = to_owners(down_blocks)
+    mlp_result = adam_columns(lay, rate_mlp, up_parts, 0, unit, mlp_state, 0, 1, mlp_result)
+    dqkv_blocks, mlp_result, input_grad = joined([wo], dqkv_blocks, mlp_result, input_grad)
+
     out_grad = wo.result().astype(bf16)
     out_grad = lax.ppermute(out_grad, AXES, [(b, a) for a, b in lay.head_owner_perm()])
     dqkv_parts = at_owner(dqkv_blocks)
@@ -1210,13 +1355,6 @@
     out_grad = [out_grad[None]]
     attn_result = adam_columns(
         lay, rate_attention, out_grad, 0, width, attn_state, 3 * width, 1, attn_result
-    )
-    down_blocks, attn_result, small_result, mlp_result = join(
-        down_blocks, attn_result, small_result, mlp_result
-    )
-
-    mlp_result = adam_columns(
-        lay, rate_mlp, at_owner(down_blocks), 0, unit, mlp_state, ff, 1, mlp_result
     )
     return (outputs, input_grad, *attn_result, *mlp_result, *small_result)
 

time: 605 us -> 568 us (0.939)
  starting transfers between devices: 101 us -> 78.6 us
  Pallas kernels: 268 us -> 288 us
  other arithmetic: 41 us -> 24.8 us
  waiting for transfers between devices: 147 us -> 133 us
    ppermute x51 -> x53, waiting for transfers between devices: 79.1 us -> 105 us  [hop(): return lax.ppermute(value, AXES, self.perm(target))]
    ppermute x1, waiting for transfers between devices: 20.8 us -> 3.25 us  [body(): lax.ppermute(out_grad, AXES, [(b, a) for a, b in lay.head_owner_perm()])]
    ppermute x1, waiting for transfers between devices: 28.3 us -> 13.7 us  [body(): w_out = lax.ppermute(w_out, AXES, lay.head_owner_perm())]
    convert_element_type x2 -> x3, other arithmetic: 13 us -> 2.35 us  [the longest x1 1.57 us: body(): upstream = cotangent.astype(f32)]
    ppermute x51 -> x53, starting transfers between devices: 58 us -> 47.5 us  [hop(): return lax.ppermute(value, AXES, self.perm(target))]
    all_to_all x2 -> x0, starting transfers between devices: 10.1 us -> none  [send(): self.state = lax.all_to_all(self.state, 'seq', 1, 1, tiled=True)]
    pallas_call x4 -> x5, Pallas kernels: 46.4 us -> 55.3 us  [the longest x2 29.7 us: input_backward(): pl.pallas_call(partial(input_kernel, len(more), hd), grid_spec=pltpu.Pref...]
    all_to_all x2, waiting for transfers between devices: 9.9 us -> 1.03 us  [exchange(): return lax.all_to_all(half, 'seq', 0, 0, tiled=True).reshape(nz * rows, -1)]
  transfers between devices with their start and end apart: 61 -> 61, of which waited for: 24 -> 22; matrix products, arithmetic and copies ran while one was open for 11% -> 8% of each run, Pallas kernels for 43% -> 50%
where the time goes in v3:
time: 568 us; the launch traced here: 557 us
  Pallas kernels  288 us (51%)
  waiting for transfers between devices  133 us (23%)
  starting transfers between devices  78.6 us (14%)
  local copies, waits for them, and re-layouts  25.4 us (4%)
  other arithmetic  24.8 us (4%)
  matrix products  5.72 us (1%)
    ppermute x53, waiting for transfers between devices, hop(): return lax.ppermute(value, AXES, self.perm(target))  105 us
    pallas_call x3, Pallas kernels, gradient_call(): pl.pallas_call(partial(kernel, half), grid_spec=pltpu.PrefetchScalarGridS...  52.1 us
    ppermute x53, starting transfers between devices, hop(): return lax.ppermute(value, AXES, self.perm(target))  47.5 us
    pallas_call x3, Pallas kernels, piece_forward(): pl.pallas_call(partial(piece_kernel, pair, places, wide // 24), grid_spec...  41.4 us
    pallas_call x8, Pallas kernels, place(): pl.pallas_call(partial(place_kernel, count, tile), grid_spec=pltpu.Prefet...  32.7 us
    pallas_call x2, Pallas kernels, input_backward(): pl.pallas_call(partial(input_kernel, len(more), hd), grid_spec=pltpu.Pref...  29.7 us
    pallas_call x4, Pallas kernels, adam_columns(): pl.pallas_call(partial(adam_kernel, pair, places, rate), grid_spec=pltpu....  25.3 us
    pallas_call x2, Pallas kernels, output_forward(): pl.pallas_call(partial(output_kernel, len(more)), grid_spec=pltpu.Prefetc...  23 us
  transfers between devices with their start and end apart: 61, of which 22 were waited for; matrix products, arithmetic and copies ran while one was open for 8% of the time, Pallas kernels for 50%

profile of v3, /device:TPU:5, one launch (start us, length us, event | category | flops | bytes accessed | tf_op | source)
XLA Modules:
  0.0 557.4 jit_solution(4018304126382289958)
XLA Ops:
  31.4 13.7 %collective-permute-done.2 = bf16[64,2048]{1,0:T(8,128)(2,1)S(1)} collective-permute-done((bf16[64,2048]{1,0:T(8,128)(2,1)S(1)}, bf16[64,2048]{1,0:T(8,128)(2,1)S(1)}, u32[]{:S(2)}, u32[]{:S(2)}) %collective-permute-start.2) | collective-permute-done | bytes 262176 | tf_op jit(solution)/shard_map/ppermute | solution.py:1115
  49.8 21.6 %collective-permute-done.3.refs_1_ = bf16[256,1920]{1,0:T(8,128)(2,1)S(1)} collective-permute-done((bf16[256,1920]{1,0:T(8,128)(2,1)S(1)}, bf16[256,1920]{1,0:T(8,128)(2,1)S(1)}, u32[]{:S(2)}, u32[]{:S(2)}) %collective-permute-start.3) | collective-permute-done | bytes 983072 | tf_op jit(solution)/shard_map/ppermute | solution.py:87
  83.1 21.3 %collective-permute-done.5.refs_5_ = bf16[256,1920]{1,0:T(8,128)(2,1)S(1)} collective-permute-done((bf16[256,1920]{1,0:T(8,128)(2,1)}, bf16[256,1920]{1,0:T(8,128)(2,1)S(1)}, u32[]{:S(2)}, u32[]{:S(2)}) %collective-permute-start.5) | collective-permute-done | bytes 983072 | tf_op jit(solution)/shard_map/ppermute | solution.py:87
  110.1 5.8 %place.8.refs_2_ = bf16[8,256,1920]{2,1,0:T(8,128)(2,1)} custom-call(s32[6]{0:T(128)} %stack.172.slot_ref, bf16[256,1920]{1,0:T(8,128)(2,1)} %bitcast.133, bf16[256,1920]{1,0:T(8,128)(2,1)} %copy-done.33, bf16[256,1920]{1,0:T(8,128)(2,1)} %collective-permute-done.4.refs_2_, bf16[256,1920]{1,0:T(8,128)(2,1)} %bitcast.136, ...), custom_call_target="tpu_custom_call" | custom-call | flops 1 | bytes 11797 | tf_op jit(solution)/shard_map/place/pallas_call | solution.py:270
  118.1 11.7 %collective-permute-done.8.refs_0_ = bf16[256,1920]{1,0:T(8,128)(2,1)} collective-permute-done((bf16[256,1920]{1,0:T(8,128)(2,1)}, bf16[256,1920]{1,0:T(8,128)(2,1)}, u32[]{:S(2)}, u32[]{:S(2)}) %collective-permute-start.8) | collective-permute-done | bytes 983072 | tf_op jit(solution)/shard_map/ppermute | solution.py:87
  145.1 11.2 %piece_forward.3 = (bf16[2,1,4,256,2048]{4,3,2,1,0:T(8,128)(2,1)}, bf16[2,1,4,256,768]{4,3,2,1,0:T(8,128)(2,1)}, bf16[2,1,4,256,1024]{4,3,2,1,0:T(8,128)(2,1)}, bf16[2,1,4,256,1024]{4,3,2,1,0:T(8,128)(2,1)}) custom-call(s32[1]{0:T(128)} %bitcast.21.pos_ref, bf16[1,256,2048]{2,1,0:T(8,128)(2,1)} %refs_0_.8, bf16[1,256,2048]{2,1,0:T(8,128)(2,1)} %copy-done.31, ...), custom_call_target="tpu_custom_call" | custom-call | flops 3758097 | bytes 12583 | tf_op jit(solution)/shard_map/piece_forward/pallas_call | solution.py:612
  175.8 11.3 %piece_forward.4 = (bf16[2,1,4,256,2048]{4,3,2,1,0:T(8,128)(2,1)}, bf16[2,1,4,256,768]{4,3,2,1,0:T(8,128)(2,1)}, bf16[2,1,4,256,1024]{4,3,2,1,0:T(8,128)(2,1)}, bf16[2,1,4,256,1024]{4,3,2,1,0:T(8,128)(2,1)}) custom-call(s32[1]{0:T(128)} %bitcast.27.pos_ref, ...), custom_call_target="tpu_custom_call", output_to_operand_aliasing={{0}: (8, {}), {1}: (9, {}), {2}: (10, {}), {3}: (11, {})} | custom-call | flops 3758097 | bytes 12583 | tf_op jit(solution)/shard_map/piece_forward/pallas_call | solution.py:612
  195.9 18.8 %piece_forward.5 = (bf16[2,1,4,256,2048]{4,3,2,1,0:T(8,128)(2,1)}, bf16[2,1,4,256,768]{4,3,2,1,0:T(8,128)(2,1)}, bf16[2,1,4,256,1024]{4,3,2,1,0:T(8,128)(2,1)}, bf16[2,1,4,256,1024]{4,3,2,1,0:T(8,128)(2,1)}) custom-call(s32[2]{0:T(128)} %pad_add_fusion.1.pos_ref, ...), custom_call_target="tpu_custom_call", output_to_operand_aliasing={{0}: (10, {}), {1}: (11, {}), {2}: (12, {}), {3}: (13, {})} | custom-call | flops 7516193 | bytes 25166 | tf_op jit(solution)/shard_map/piece_forward/pallas_call | solution.py:612
  227.4 6.3 %attn_forward.1 = (bf16[2,1024,256]{2,1,0:T(8,128)(2,1)}, f32[2,1024,128]{2,1,0:T(8,128)}) custom-call(bf16[2,1024,768]{2,1,0:T(8,128)(2,1)} %bitcast.116), custom_call_target="tpu_custom_call" | custom-call | flops 2147484 | bytes 12583 | tf_op jit(solution)/shard_map/attn_forward/pallas_call | solution.py:656
  233.7 10.6 %output_forward.2 = bf16[4,256,2048]{2,1,0:T(8,128)(2,1)} custom-call(s32[4]{0:T(128)} %fusion.18.order_ref, bf16[2048,1024]{1,0:T(8,128)(2,1)} %bitcast.113, bf16[2048,1024]{1,0:T(8,128)(2,1)} %bitcast.110, bf16[2048,256]{1,0:T(8,128)(2,1)} %bitcast.123, bf16[256,2048]{1,0:T(8,128)(2,1)} %reshape_reshape.16.wo_ref), custom_call_target="tpu_custom_call" | custom-call | flops 5368710 | bytes 16778 | tf_op jit(solution)/shard_map/output_forward/pallas_call | solution.py:787
  255.5 12.4 %output_forward.3 = (bf16[1,256,2048]{2,1,0:T(8,128)(2,1)}, bf16[1,256,2048]{2,1,0:T(8,128)(2,1)}, bf16[1,256,2048]{2,1,0:T(8,128)(2,1)}, bf16[1,256,2048]{2,1,0:T(8,128)(2,1)}) custom-call(s32[4]{0:T(128)} %fusion.18.order_ref, bf16[2048,1024]{1,0:T(8,128)(2,1)} %bitcast.114, bf16[2048,1024]{1,0:T(8,128)(2,1)} %bitcast.111, bf16[2048,256]{1,0:T(8,128)(2,1)} %bitcast.124, ...), custom_call_target="tpu_custom_call" | custom-call | flops 5368710 | bytes 16778 | tf_op jit(solution)/shard_map/output_forward/pallas_call | solution.py:787
  283.3 15.9 %gradient.3 = (bf16[2,256,1024]{2,1,0:T(8,128)(2,1)}, bf16[2,256,1024]{2,1,0:T(8,128)(2,1)}, bf16[2,256,1024]{2,1,0:T(8,128)(2,1)}, bf16[2,256,1024]{2,1,0:T(8,128)(2,1)}) custom-call(s32[8]{0:T(128)} %stack.187.block_ref.refs_0_, bf16[2048,2048]{1,0:T(8,128)(2,1)} %bitcast.103, bf16[2048,1024]{1,0:T(8,128)(2,1)} %bitcast.115), custom_call_target="tpu_custom_call" | custom-call | flops 8589935 | bytes 16778 | tf_op jit(solution)/shard_map/gradient/pallas_call | solution.py:407
  300.1 13.8 %hidden_backward.1 = (bf16[2048,1024]{1,0:T(8,128)(2,1)}, f32[8,1024]{1,0:T(8,128)}) custom-call(bf16[2048,2048]{1,0:T(8,128)(2,1)} %bitcast.104, bf16[2048,1024]{1,0:T(8,128)(2,1)} %bitcast.112, bf16[2048,1024]{1,0:T(8,128)(2,1)} %bitcast.122), custom_call_target="tpu_custom_call" | custom-call | flops 8589935 | bytes 25166 | tf_op jit(solution)/shard_map/hidden_backward/pallas_call | solution.py:825
  313.9 10.7 %attn_backward.2 = (bf16[2,1024,768]{2,1,0:T(8,128)(2,1)}, f32[1,8,768]{2,1,0:T(8,128)}) custom-call(bf16[2,1024,2048]{2,1,0:T(8,128)(2,1)} %bitcast.105, bf16[256,2048]{1,0:T(8,128)(2,1)} %reshape_reshape.16.wo_ref, bf16[2,1024,768]{2,1,0:T(8,128)(2,1)} %bitcast.117, f32[2,1024,128]{2,1,0:T(8,128)} %get-tuple-element.369.lse_ref, ...), custom_call_target="tpu_custom_call" | custom-call | flops 3758097 | bytes 16778 | tf_op jit(solution)/shard_map/attn_backward/pallas_call | solution.py:726
  333.1 13.6 %input_backward.2 = bf16[4,256,2048]{2,1,0:T(8,128)(2,1)} custom-call(s32[4]{0:T(128)} %fusion.18.order_ref, bf16[2048,1024]{1,0:T(8,128)(2,1)} %get-tuple-element.410.du_ref.refs_2_, bf16[2048,768]{1,0:T(8,128)(2,1)} %bitcast.119, bf16[2048,1920]{1,0:T(8,128)(2,1)} %bitcast.91, bf16[2048,1920]{1,0:T(8,128)(2,1)} %bitcast.92, bf16[2048,1920]{1,0:T(8,128)(2,1)} %bitcast.93, ...), custom_call_target="tpu_custom_call" | custom-call | flops 7516193 | bytes 25166 | tf_op jit(solution)/shard_map/input_backward/pallas_call | solution.py:861
  357.1 10.6 %attn_backward.3 = (bf16[2,1024,768]{2,1,0:T(8,128)(2,1)}, f32[1,8,768]{2,1,0:T(8,128)}) custom-call(bf16[2,1024,2048]{2,1,0:T(8,128)(2,1)} %bitcast.106, bf16[256,2048]{1,0:T(8,128)(2,1)} %reshape_reshape.16.wo_ref, bf16[2,1024,768]{2,1,0:T(8,128)(2,1)} %bitcast.118, f32[2,1024,128]{2,1,0:T(8,128)} %get-tuple-element.369.lse_ref, ...), custom_call_target="tpu_custom_call", output_to_operand_aliasing={{0}: (5, {})} | custom-call | flops 3758097 | bytes 16778 | tf_op jit(solution)/shard_map/attn_backward/pallas_call | solution.py:726
  367.8 16.0 %input_backward.3 = (bf16[1,256,2048]{2,1,0:T(8,128)(2,1)}, bf16[1,256,2048]{2,1,0:T(8,128)(2,1)}, bf16[1,256,2048]{2,1,0:T(8,128)(2,1)}, bf16[1,256,2048]{2,1,0:T(8,128)(2,1)}) custom-call(s32[4]{0:T(128)} %fusion.18.order_ref, bf16[2048,1024]{1,0:T(8,128)(2,1)} %get-tuple-element.410.du_ref.refs_2_, bf16[2048,768]{1,0:T(8,128)(2,1)} %bitcast.120, ...), custom_call_target="tpu_custom_call" | custom-call | flops 7516193 | bytes 25166 | tf_op jit(solution)/shard_map/input_backward/pallas_call | solution.py:861
  390.7 19.1 %gradient.4 = (bf16[2,256,1024]{2,1,0:T(8,128)(2,1)}, bf16[2,256,1024]{2,1,0:T(8,128)(2,1)}, bf16[2,256,1024]{2,1,0:T(8,128)(2,1)}, bf16[2,256,1024]{2,1,0:T(8,128)(2,1)}, f32[2048,128]{1,0:T(8,128)}) custom-call(s32[8]{0:T(128)} %stack.187.block_ref.refs_0_, bf16[2048,2048]{1,0:T(8,128)(2,1)} %bitcast.108, ...), custom_call_target="tpu_custom_call" | custom-call | flops 8589935 | bytes 16778 | tf_op jit(solution)/shard_map/gradient/pallas_call | solution.py:407
  418.0 17.1 %gradient.5 = (bf16[2,256,896]{2,1,0:T(8,128)(2,1)}, bf16[2,256,896]{2,1,0:T(8,128)(2,1)}, bf16[2,256,896]{2,1,0:T(8,128)(2,1)}, bf16[2,256,896]{2,1,0:T(8,128)(2,1)}) custom-call(s32[8]{0:T(128)} %stack.187.block_ref.refs_0_, bf16[2048,2048]{1,0:T(8,128)(2,1)} %bitcast.109, bf16[2048,768]{1,0:T(8,128)(2,1)} %bitcast.121, ...), custom_call_target="tpu_custom_call" | custom-call | flops 7516193 | bytes 15729 | tf_op jit(solution)/shard_map/gradient/pallas_call | solution.py:407
  458.9 15.1 %collective-permute-done.45.refs_2_ = bf16[2,256,896]{2,1,0:T(8,128)(2,1)S(1)} collective-permute-done((bf16[2,256,896]{2,1,0:T(8,128)(2,1)}, bf16[2,256,896]{2,1,0:T(8,128)(2,1)S(1)}, u32[]{:S(2)}, u32[]{:S(2)}) %collective-permute-start.45) | collective-permute-done | bytes 917536 | tf_op jit(solution)/shard_map/ppermute | solution.py:87
  499.8 9.8 %all-to-all-done.4 = bf16[4,2,64,1024]{3,2,1,0:T(8,128)(2,1)S(1)} async-done(((bf16[4,2,64,1024]{3,2,1,0:T(8,128)(2,1)}), bf16[4,2,64,1024]{3,2,1,0:T(8,128)(2,1)S(1)}, u32[]{:S(2)}, u32[]{:S(2)}) %all-to-all-start.4) | async-done | bytes 1048608 | tf_op jit(solution)/shard_map/all_to_all | solution.py:1224
  519.7 7.6 %adam_columns.4 = (f32[64,16384]{1,0:T(8,128)}, f32[64,16384]{1,0:T(8,128)}, f32[64,16384]{1,0:T(8,128)}, f32[64,16384]{1,0:T(8,128)}) custom-call(s32[1]{0:T(128)} %bitcast.4.c_ref, bf16[4,64,1024]{2,1,0:T(8,128)(2,1)} %get-tuple-element.530.refs_0_, bf16[4,64,1024]{2,1,0:T(8,128)(2,1)} %copy-done.42, f32[64,16384]{1,0:T(8,128)} %refs_2_.9, ...), custom_call_target="tpu_custom_call" | custom-call | flops 15729 | bytes 15729 | tf_op jit(solution)/shard_map/adam_columns/pallas_call | solution.py:909
  528.1 7.6 %adam_columns.5 = (f32[64,16384]{1,0:T(8,128)}, f32[64,16384]{1,0:T(8,128)}, f32[64,16384]{1,0:T(8,128)}, f32[64,16384]{1,0:T(8,128)}) custom-call(s32[1]{0:T(128)} %bitcast.4.c_ref, bf16[4,64,1024]{2,1,0:T(8,128)(2,1)} %get-tuple-element.532.refs_0_, ...), custom_call_target="tpu_custom_call", output_to_operand_aliasing={{0}: (6, {}), {1}: (7, {}), {2}: (8, {}), {3}: (9, {})} | custom-call | flops 15729 | bytes 15729 | tf_op jit(solution)/shard_map/adam_columns/pallas_call | solution.py:909
  542.3 7.0 %adam_columns.6 = (f32[64,8192]{1,0:T(8,128)}, f32[64,8192]{1,0:T(8,128)}, f32[64,8192]{1,0:T(8,128)}, f32[64,8192]{1,0:T(8,128)}) custom-call(s32[1]{0:T(128)} %bitcast.4.c_ref, bf16[4,64,896]{2,1,0:T(8,128)(2,1)} %copy-done.17, bf16[4,64,896]{2,1,0:T(8,128)(2,1)} %copy-done.36, f32[64,8192]{1,0:T(8,128)} %refs_1_.5, f32[64,8192]{1,0:T(8,128)} %refs_2_.11, ...), custom_call_target="tpu_custom_call" | custom-call | flops 11797 | bytes 11797 | tf_op jit(solution)/shard_map/adam_columns/pallas_call | solution.py:909
  (297 shorter events, 246.8 us)
Async XLA Ops:
  5.5 39.6 %all-to-all-start = ((bf16[4,64,1920]{2,1,0:T(8,128)(2,1)}), bf16[4,64,1920]{2,1,0:T(8,128)(2,1)S(1)}, u32[]{:S(2)}, u32[]{:S(2)}) async-start(bf16[4,64,1920]{2,1,0:T(8,128)(2,1)} %prepare.4), calls=%async_computation | async-start | bytes 1966080 | tf_op jit(solution)/shard_map/all_to_all | solution.py:1060
  13.6 31.5 %collective-permute-start.1 = (bf16[4,64,1920]{2,1,0:T(8,128)(2,1)}, bf16[4,64,1920]{2,1,0:T(8,128)(2,1)S(1)}, u32[]{:S(2)}, u32[]{:S(2)}) collective-permute-start(bf16[4,64,1920]{2,1,0:T(8,128)(2,1)} %prepare.5), channel_id=1, source_target_pairs={{0,4},{1,5},{2,6},{3,7},{4,0},{5,1},{6,2},{7,3},{8,12},{9,13},{10,... | collective-permute-start | bytes 2949128 | tf_op jit(solution)/shard_map/ppermute | solution.py:87
  15.6 29.5 %collective-permute-start.2 = (bf16[64,2048]{1,0:T(8,128)(2,1)S(1)}, bf16[64,2048]{1,0:T(8,128)(2,1)S(1)}, u32[]{:S(2)}, u32[]{:S(2)}) collective-permute-start(bf16[64,2048]{1,0:T(8,128)(2,1)S(1)} %slice.122), channel_id=1, source_target_pairs={{0,0},{1,8},{2,16},{3,24},{4,4},{5,12},{6,20},{7,28},{8,9},{9,1},{... | collective-permute-start | bytes 786440 | tf_op jit(solution)/shard_map/ppermute | solution.py:1115
  46.1 27.3 %all-to-all-start.1 = ((bf16[4,64,1920]{2,1,0:T(8,128)(2,1)}), bf16[4,64,1920]{2,1,0:T(8,128)(2,1)S(1)}, u32[]{:S(2)}, u32[]{:S(2)}) async-start(bf16[4,64,1920]{2,1,0:T(8,128)(2,1)} %copy-done.32), calls=%async_computation.1 | async-start | bytes 1966080 | tf_op jit(solution)/shard_map/all_to_all | solution.py:1060
  74.7 30.7 %all-to-all-start.2 = ((bf16[4,2,64,1024]{3,2,1,0:T(8,128)(2,1)}), bf16[4,2,64,1024]{3,2,1,0:T(8,128)(2,1)S(1)}, u32[]{:S(2)}, u32[]{:S(2)}) async-start(bf16[4,2,64,1024]{3,2,1,0:T(8,128)(2,1)} %copy.76), calls=%async_computation.2 | async-start | bytes 2097152 | tf_op jit(solution)/shard_map/all_to_all | solution.py:1124
  105.4 26.6 %collective-permute-start.10 = (bf16[1,256,2048]{2,1,0:T(8,128)(2,1)S(1)}, bf16[1,256,2048]{2,1,0:T(8,128)(2,1)}, u32[]{:S(2)}, u32[]{:S(2)}) collective-permute-start(bf16[1,256,2048]{2,1,0:T(8,128)(2,1)S(1)} %copy-done), channel_id=1, source_target_pairs={{0,1},{1,2},{2,3},{3,0},{4,5},{5,6},{6,7},{7,4},{8,9},{9,10},{10,1... | collective-permute-start | bytes 3145736 | tf_op jit(solution)/shard_map/ppermute | solution.py:87
  132.0 29.4 %collective-permute-start.12 = (bf16[640,1024]{1,0:T(8,128)(2,1)}, bf16[640,1024]{1,0:T(8,128)(2,1)S(1)}, u32[]{:S(2)}, u32[]{:S(2)}) collective-permute-start(bf16[640,1024]{1,0:T(8,128)(2,1)} %pad_maximum_fusion.1), channel_id=1, source_target_pairs={{0,8},{1,9},{2,10},{3,11},{4,12},{5,13},{6,14},{7,15},{8,0},{9,1},... | collective-permute-start | bytes 3932168 | tf_op jit(solution)/shard_map/ppermute | solution.py:87
  132.6 29.1 %collective-permute-start.13 = (bf16[640,1024]{1,0:T(8,128)(2,1)}, bf16[640,1024]{1,0:T(8,128)(2,1)S(1)}, u32[]{:S(2)}, u32[]{:S(2)}) collective-permute-start(bf16[640,1024]{1,0:T(8,128)(2,1)} %pad_maximum_fusion.1), channel_id=1, source_target_pairs={{0,16},{1,17},{2,18},{3,19},{4,20},{5,21},{6,22},{7,23},{8,24},{9,... | collective-permute-start | bytes 3932168 | tf_op jit(solution)/shard_map/ppermute | solution.py:87
  134.4 26.9 %collective-permute-start.14 = (bf16[1,256,2048]{2,1,0:T(8,128)(2,1)}, bf16[1,256,2048]{2,1,0:T(8,128)(2,1)}, u32[]{:S(2)}, u32[]{:S(2)}) collective-permute-start(bf16[1,256,2048]{2,1,0:T(8,128)(2,1)} %collective-permute-done.10.refs_0_), channel_id=1, source_target_pairs={{0,1},{1,2},{2,3},{3,0},{4,5},{5,6},{6,7},{7,4},{8,9},{9,10},{10,1... | collective-permute-start | bytes 3145736 | tf_op jit(solution)/shard_map/ppermute | solution.py:87
  164.0 27.1 %collective-permute-start.18 = (bf16[1,256,2048]{2,1,0:T(8,128)(2,1)}, bf16[1,256,2048]{2,1,0:T(8,128)(2,1)}, u32[]{:S(2)}, u32[]{:S(2)}) collective-permute-start(bf16[1,256,2048]{2,1,0:T(8,128)(2,1)} %collective-permute-done.14.refs_0_), channel_id=1, source_target_pairs={{0,1},{1,2},{2,3},{3,0},{4,5},{5,6},{6,7},{7,4},{8,9},{9,10},{10,1... | collective-permute-start | bytes 3145736 | tf_op jit(solution)/shard_map/ppermute | solution.py:87
  191.9 26.1 %collective-permute-start.20 = (bf16[1,256,2048]{2,1,0:T(8,128)(2,1)S(1)}, bf16[1,256,2048]{2,1,0:T(8,128)(2,1)}, u32[]{:S(2)}, u32[]{:S(2)}) collective-permute-start(bf16[1,256,2048]{2,1,0:T(8,128)(2,1)S(1)} %copy-done.5), channel_id=1, source_target_pairs={{0,1},{1,2},{2,3},{3,0},{4,5},{5,6},{6,7},{7,4},{8,9},{9,10},{10,1... | collective-permute-start | bytes 3145736 | tf_op jit(solution)/shard_map/ppermute | solution.py:87
  218.0 26.3 %collective-permute-start.23 = (bf16[1,256,2048]{2,1,0:T(8,128)(2,1)}, bf16[1,256,2048]{2,1,0:T(8,128)(2,1)}, u32[]{:S(2)}, u32[]{:S(2)}) collective-permute-start(bf16[1,256,2048]{2,1,0:T(8,128)(2,1)} %collective-permute-done.20), channel_id=1, source_target_pairs={{0,4},{1,5},{2,6},{3,7},{4,0},{5,1},{6,2},{7,3},{8,12},{9,13},{10,... | collective-permute-start | bytes 3145736 | tf_op jit(solution)/shard_map/ppermute | solution.py:87
  219.3 26.8 %collective-permute-start.22 = (bf16[1,256,2048]{2,1,0:T(8,128)(2,1)}, bf16[1,256,2048]{2,1,0:T(8,128)(2,1)S(1)}, u32[]{:S(2)}, u32[]{:S(2)}) collective-permute-start(bf16[1,256,2048]{2,1,0:T(8,128)(2,1)} %collective-permute-done.20), channel_id=1, source_target_pairs={{0,1},{1,2},{2,3},{3,0},{4,5},{5,6},{6,7},{7,4},{8,9},{9,10},{10,1... | collective-permute-start | bytes 3145736 | tf_op jit(solution)/shard_map/ppermute | solution.py:87
  275.7 48.9 %collective-permute-start.29 = (bf16[1,256,2048]{2,1,0:T(8,128)(2,1)}, bf16[1,256,2048]{2,1,0:T(8,128)(2,1)S(1)}, u32[]{:S(2)}, u32[]{:S(2)}) collective-permute-start(bf16[1,256,2048]{2,1,0:T(8,128)(2,1)} %get-tuple-element.373), channel_id=1, source_target_pairs={{0,2},{3,1},{4,6},{7,5},{8,10},{11,9},{12,14},{15,13},{16,18},{19,... | collective-permute-start | bytes 3145736 | tf_op jit(solution)/shard_map/ppermute | solution.py:87
  277.1 47.6 %collective-permute-start.30 = (bf16[1,256,2048]{2,1,0:T(8,128)(2,1)}, bf16[1,256,2048]{2,1,0:T(8,128)(2,1)S(1)}, u32[]{:S(2)}, u32[]{:S(2)}) collective-permute-start(bf16[1,256,2048]{2,1,0:T(8,128)(2,1)} %get-tuple-element.373), channel_id=1, source_target_pairs={{1,2},{2,1},{5,6},{6,5},{9,10},{10,9},{13,14},{14,13},{17,18},{18,... | collective-permute-start | bytes 3145736 | tf_op jit(solution)/shard_map/ppermute | solution.py:87
  278.2 46.4 %collective-permute-start.28 = (bf16[1,256,2048]{2,1,0:T(8,128)(2,1)}, bf16[1,256,2048]{2,1,0:T(8,128)(2,1)S(1)}, u32[]{:S(2)}, u32[]{:S(2)}) collective-permute-start(bf16[1,256,2048]{2,1,0:T(8,128)(2,1)} %get-tuple-element.372), channel_id=1, source_target_pairs={{0,1},{1,0},{2,3},{3,2},{4,5},{5,4},{6,7},{7,6},{8,9},{9,8},{10,11... | collective-permute-start | bytes 3145736 | tf_op jit(solution)/shard_map/ppermute | solution.py:87
  325.3 26.2 %collective-permute-start.35 = (bf16[1,256,2048]{2,1,0:T(8,128)(2,1)S(1)}, bf16[1,256,2048]{2,1,0:T(8,128)(2,1)}, u32[]{:S(2)}, u32[]{:S(2)}) collective-permute-start(bf16[1,256,2048]{2,1,0:T(8,128)(2,1)S(1)} %fusion.9), channel_id=1, source_target_pairs={{0,1},{1,3},{2,0},{3,2},{4,5},{5,7},{6,4},{7,6},{8,9},{9,11},{10,8... | collective-permute-start | bytes 3145736 | tf_op jit(solution)/shard_map/ppermute | solution.py:87
  353.2 30.6 %all-to-all-start.3 = ((bf16[4,2,64,1024]{3,2,1,0:T(8,128)(2,1)}), bf16[4,2,64,1024]{3,2,1,0:T(8,128)(2,1)S(1)}, u32[]{:S(2)}, u32[]{:S(2)}) async-start(bf16[4,2,64,1024]{3,2,1,0:T(8,128)(2,1)} %final_blocks.3), calls=%async_computation.3 | async-start | bytes 2097152 | tf_op jit(solution)/shard_map/all_to_all | solution.py:1224
  383.8 51.3 %collective-permute-start.40 = (bf16[1,256,2048]{2,1,0:T(8,128)(2,1)}, bf16[1,256,2048]{2,1,0:T(8,128)(2,1)}, u32[]{:S(2)}, u32[]{:S(2)}) collective-permute-start(bf16[1,256,2048]{2,1,0:T(8,128)(2,1)} %get-tuple-element.430), channel_id=1, source_target_pairs={{0,2},{3,1},{4,6},{7,5},{8,10},{11,9},{12,14},{15,13},{16,18},{19,... | collective-permute-start | bytes 3145736 | tf_op jit(solution)/shard_map/ppermute | solution.py:87
  389.1 46.1 %collective-permute-start.41 = (bf16[1,256,2048]{2,1,0:T(8,128)(2,1)}, bf16[1,256,2048]{2,1,0:T(8,128)(2,1)}, u32[]{:S(2)}, u32[]{:S(2)}) collective-permute-start(bf16[1,256,2048]{2,1,0:T(8,128)(2,1)} %get-tuple-element.430), channel_id=1, source_target_pairs={{1,2},{2,1},{5,6},{6,5},{9,10},{10,9},{13,14},{14,13},{17,18},{18,... | collective-permute-start | bytes 3145736 | tf_op jit(solution)/shard_map/ppermute | solution.py:87
  435.6 44.6 %collective-permute-start.44 = (bf16[1,256,2048]{2,1,0:T(8,128)(2,1)S(1)}, bf16[1,256,2048]{2,1,0:T(8,128)(2,1)}, u32[]{:S(2)}, u32[]{:S(2)}) collective-permute-start(bf16[1,256,2048]{2,1,0:T(8,128)(2,1)S(1)} %fusion.10), channel_id=1, source_target_pairs={{0,1},{1,3},{2,0},{3,2},{4,5},{5,7},{6,4},{7,6},{8,9},{9,11},{10,8... | collective-permute-start | bytes 3145736 | tf_op jit(solution)/shard_map/ppermute | solution.py:87
  443.3 30.6 %collective-permute-start.45 = (bf16[2,256,896]{2,1,0:T(8,128)(2,1)}, bf16[2,256,896]{2,1,0:T(8,128)(2,1)S(1)}, u32[]{:S(2)}, u32[]{:S(2)}) collective-permute-start(bf16[2,256,896]{2,1,0:T(8,128)(2,1)} %get-tuple-element.456), channel_id=1, source_target_pairs={{0,8},{1,9},{2,10},{3,11},{4,12},{5,13},{6,14},{7,15},{8,0},{9,1},... | collective-permute-start | bytes 2752520 | tf_op jit(solution)/shard_map/ppermute | solution.py:87
  444.2 29.8 %collective-permute-start.46 = (bf16[2,256,896]{2,1,0:T(8,128)(2,1)}, bf16[2,256,896]{2,1,0:T(8,128)(2,1)}, u32[]{:S(2)}, u32[]{:S(2)}) collective-permute-start(bf16[2,256,896]{2,1,0:T(8,128)(2,1)} %get-tuple-element.457), channel_id=1, source_target_pairs={{0,16},{1,17},{2,18},{3,19},{4,20},{5,21},{6,22},{7,23},{8,24},{9,... | collective-permute-start | bytes 2752520 | tf_op jit(solution)/shard_map/ppermute | solution.py:87
  481.3 28.3 %all-to-all-start.4 = ((bf16[4,2,64,1024]{3,2,1,0:T(8,128)(2,1)}), bf16[4,2,64,1024]{3,2,1,0:T(8,128)(2,1)S(1)}, u32[]{:S(2)}, u32[]{:S(2)}) async-start(bf16[4,2,64,1024]{3,2,1,0:T(8,128)(2,1)} %final_blocks.4), calls=%async_computation.4 | async-start | bytes 2097152 | tf_op jit(solution)/shard_map/all_to_all | solution.py:1224
  (85 other events, 983.3 us)

commit v4 on v3

--- a/solution.py
+++ b/solution.py
@@ -264,7 +264,7 @@
 def place(blocks, slots, rows, total, held=None):
     count = len(blocks)
     width = blocks[0][0].shape[1]
-    tile = max(min(64, rows), rows // 2)
+    tile = rows if count * rows * width <= 2**21 else max(min(64, rows), rows // 2)
     operands = [v for v, _ in blocks] + ([] if held is None else [held])
     any_spec = pl.BlockSpec(memory_space=pl.ANY)
     return pl.pallas_call(
@@ -454,7 +454,7 @@
 def fold(parts):
     held, rows, n = parts[0].keep.shape
     half = held // 2
-    tile = min(64, rows)
+    tile = min(128, rows)
     full = pl.BlockSpec((held, tile, n), lambda i: (0, i, 0))
     part = pl.BlockSpec((half, tile, n), lambda i: (0, i, 0))
     count = len(parts)
@@ -474,18 +474,23 @@
 
 def blocks_kernel(count, *refs):
     out_ref = refs[-1]
+    places, _, rows, _ = out_ref.shape
     for p in range(count):
-        out_ref[0, p] = (refs[p][0].astype(f32) + refs[count + p][0].astype(f32)).astype(bf16)
+        total = (refs[p][0].astype(f32) + refs[count + p][0].astype(f32)).astype(bf16)
+        for z in range(places):
+            out_ref[z, p] = total[z * rows : (z + 1) * rows]
 
 
 def final_blocks(parts, nz):
     _, total, n = parts[0].keep.shape
     rows, count = total // nz, len(parts)
+    steps = nz // 2 if nz % 2 == 0 else nz
+    places = nz // steps
     return pl.pallas_call(
         partial(blocks_kernel, count),
-        grid=(nz,),
-        in_specs=[pl.BlockSpec((1, rows, n), lambda i: (0, i, 0))] * (2 * count),
-        out_specs=pl.BlockSpec((1, count, rows, n), lambda i: (i, 0, 0, 0)),
+        grid=(steps,),
+        in_specs=[pl.BlockSpec((1, places * rows, n), lambda i: (0, i, 0))] * (2 * count),
+        out_specs=pl.BlockSpec((places, count, rows, n), lambda i: (i, 0, 0, 0)),
         out_shape=jax.ShapeDtypeStruct((nz, count, rows, n), bf16),
         name="final_blocks",
         **params((count * total * n, 8 * count * total * n)),
@@ -654,7 +659,7 @@
     seqs, length, wide = qkv.shape
     hd = wide // 3
     return pl.pallas_call(
-        partial(attn_fwd_kernel, scale, min(256, length)),
+        partial(attn_fwd_kernel, scale, min(512, length)),
         grid=(seqs,),
         in_specs=[pl.BlockSpec((1, length, wide), lambda s: (s, 0, 0))],
         out_specs=[
@@ -724,7 +729,7 @@
         return (first + s, 0, 0)
 
     return pl.pallas_call(
-        partial(attn_bwd_kernel, hd // 8, scale, min(256, length)),
+        partial(attn_bwd_kernel, hd // 8, scale, min(512, length)),
         grid=(share,),
         in_specs=[
             pl.BlockSpec((1, length, width), row_map),

time: 568 us -> 564 us (level)
  Pallas kernels: 288 us -> 279 us
  waiting for transfers between devices: 133 us -> 139 us
  transfers between devices with their start and end apart: 61 -> 61, of which waited for: 22 -> 25; matrix products, arithmetic and copies ran while one was open for 8% -> 8% of each run, Pallas kernels for 50% -> 49%
where the time goes in v4:
time: 564 us; the launch traced here: 554 us
  Pallas kernels  279 us (49%)
  waiting for transfers between devices  139 us (25%)
  starting transfers between devices  78.6 us (14%)
  local copies, waits for them, and re-layouts  25.4 us (5%)
  other arithmetic  24.8 us (4%)
  matrix products  5.72 us (1%)
    ppermute x53, waiting for transfers between devices, hop(): return lax.ppermute(value, AXES, self.perm(target))  111 us
    pallas_call x3, Pallas kernels, gradient_call(): pl.pallas_call(partial(kernel, half), grid_spec=pltpu.PrefetchScalarGridS...  52.1 us
    ppermute x53, starting transfers between devices, hop(): return lax.ppermute(value, AXES, self.perm(target))  47.5 us
    pallas_call x3, Pallas kernels, piece_forward(): pl.pallas_call(partial(piece_kernel, pair, places, wide // 24), grid_spec...  41.4 us
    pallas_call x8, Pallas kernels, place(): pl.pallas_call(partial(place_kernel, count, tile), grid_spec=pltpu.Prefet...  30.5 us
    pallas_call x2, Pallas kernels, input_backward(): pl.pallas_call(partial(input_kernel, len(more), hd), grid_spec=pltpu.Pref...  29.7 us
    pallas_call x4, Pallas kernels, adam_columns(): pl.pallas_call(partial(adam_kernel, pair, places, rate), grid_spec=pltpu....  25.3 us
    pallas_call x2, Pallas kernels, output_forward(): pl.pallas_call(partial(output_kernel, len(more)), grid_spec=pltpu.Prefetc...  23 us
  transfers between devices with their start and end apart: 61, of which 25 were waited for; matrix products, arithmetic and copies ran while one was open for 8% of the time, Pallas kernels for 49%

profile of v4, /device:TPU:5, one launch (start us, length us, event | category | flops | bytes accessed | tf_op | source)
XLA Modules:
  0.0 554.2 jit_solution(896412138924651932)
XLA Ops:
  31.4 13.7 %collective-permute-done.2 = bf16[64,2048]{1,0:T(8,128)(2,1)S(1)} collective-permute-done((bf16[64,2048]{1,0:T(8,128)(2,1)S(1)}, bf16[64,2048]{1,0:T(8,128)(2,1)S(1)}, u32[]{:S(2)}, u32[]{:S(2)}) %collective-permute-start.2) | collective-permute-done | bytes 262176 | tf_op jit(solution)/shard_map/ppermute | solution.py:1120
  49.8 21.6 %collective-permute-done.3.refs_1_ = bf16[256,1920]{1,0:T(8,128)(2,1)S(1)} collective-permute-done((bf16[256,1920]{1,0:T(8,128)(2,1)S(1)}, bf16[256,1920]{1,0:T(8,128)(2,1)S(1)}, u32[]{:S(2)}, u32[]{:S(2)}) %collective-permute-start.3) | collective-permute-done | bytes 983072 | tf_op jit(solution)/shard_map/ppermute | solution.py:87
  83.1 21.3 %collective-permute-done.5.refs_5_ = bf16[256,1920]{1,0:T(8,128)(2,1)S(1)} collective-permute-done((bf16[256,1920]{1,0:T(8,128)(2,1)}, bf16[256,1920]{1,0:T(8,128)(2,1)S(1)}, u32[]{:S(2)}, u32[]{:S(2)}) %collective-permute-start.5) | collective-permute-done | bytes 983072 | tf_op jit(solution)/shard_map/ppermute | solution.py:87
  110.1 5.8 %place.8.refs_2_ = bf16[8,256,1920]{2,1,0:T(8,128)(2,1)} custom-call(s32[6]{0:T(128)} %stack.172.slot_ref, bf16[256,1920]{1,0:T(8,128)(2,1)} %bitcast.133, bf16[256,1920]{1,0:T(8,128)(2,1)} %copy-done.33, bf16[256,1920]{1,0:T(8,128)(2,1)} %collective-permute-done.4.refs_2_, bf16[256,1920]{1,0:T(8,128)(2,1)} %bitcast.136, ...), custom_call_target="tpu_custom_call" | custom-call | flops 1 | bytes 11797 | tf_op jit(solution)/shard_map/place/pallas_call | solution.py:270
  118.1 11.7 %collective-permute-done.8.refs_0_ = bf16[256,1920]{1,0:T(8,128)(2,1)} collective-permute-done((bf16[256,1920]{1,0:T(8,128)(2,1)}, bf16[256,1920]{1,0:T(8,128)(2,1)}, u32[]{:S(2)}, u32[]{:S(2)}) %collective-permute-start.8) | collective-permute-done | bytes 983072 | tf_op jit(solution)/shard_map/ppermute | solution.py:87
  144.8 11.2 %piece_forward.3 = (bf16[2,1,4,256,2048]{4,3,2,1,0:T(8,128)(2,1)}, bf16[2,1,4,256,768]{4,3,2,1,0:T(8,128)(2,1)}, bf16[2,1,4,256,1024]{4,3,2,1,0:T(8,128)(2,1)}, bf16[2,1,4,256,1024]{4,3,2,1,0:T(8,128)(2,1)}) custom-call(s32[1]{0:T(128)} %bitcast.21.pos_ref, bf16[1,256,2048]{2,1,0:T(8,128)(2,1)} %refs_0_.8, bf16[1,256,2048]{2,1,0:T(8,128)(2,1)} %copy-done.31, ...), custom_call_target="tpu_custom_call" | custom-call | flops 3758097 | bytes 12583 | tf_op jit(solution)/shard_map/piece_forward/pallas_call | solution.py:617
  175.1 11.3 %piece_forward.4 = (bf16[2,1,4,256,2048]{4,3,2,1,0:T(8,128)(2,1)}, bf16[2,1,4,256,768]{4,3,2,1,0:T(8,128)(2,1)}, bf16[2,1,4,256,1024]{4,3,2,1,0:T(8,128)(2,1)}, bf16[2,1,4,256,1024]{4,3,2,1,0:T(8,128)(2,1)}) custom-call(s32[1]{0:T(128)} %bitcast.27.pos_ref, ...), custom_call_target="tpu_custom_call", output_to_operand_aliasing={{0}: (8, {}), {1}: (9, {}), {2}: (10, {}), {3}: (11, {})} | custom-call | flops 3758097 | bytes 12583 | tf_op jit(solution)/shard_map/piece_forward/pallas_call | solution.py:617
  195.9 18.8 %piece_forward.5 = (bf16[2,1,4,256,2048]{4,3,2,1,0:T(8,128)(2,1)}, bf16[2,1,4,256,768]{4,3,2,1,0:T(8,128)(2,1)}, bf16[2,1,4,256,1024]{4,3,2,1,0:T(8,128)(2,1)}, bf16[2,1,4,256,1024]{4,3,2,1,0:T(8,128)(2,1)}) custom-call(s32[2]{0:T(128)} %pad_add_fusion.1.pos_ref, ...), custom_call_target="tpu_custom_call", output_to_operand_aliasing={{0}: (10, {}), {1}: (11, {}), {2}: (12, {}), {3}: (13, {})} | custom-call | flops 7516193 | bytes 25166 | tf_op jit(solution)/shard_map/piece_forward/pallas_call | solution.py:617
  226.4 6.2 %attn_forward.1 = (bf16[2,1024,256]{2,1,0:T(8,128)(2,1)}, f32[2,1024,128]{2,1,0:T(8,128)}) custom-call(bf16[2,1024,768]{2,1,0:T(8,128)(2,1)} %bitcast.116), custom_call_target="tpu_custom_call" | custom-call | flops 2147484 | bytes 12583 | tf_op jit(solution)/shard_map/attn_forward/pallas_call | solution.py:661
  232.6 10.6 %output_forward.2 = bf16[4,256,2048]{2,1,0:T(8,128)(2,1)} custom-call(s32[4]{0:T(128)} %fusion.18.order_ref, bf16[2048,1024]{1,0:T(8,128)(2,1)} %bitcast.113, bf16[2048,1024]{1,0:T(8,128)(2,1)} %bitcast.110, bf16[2048,256]{1,0:T(8,128)(2,1)} %bitcast.123, bf16[256,2048]{1,0:T(8,128)(2,1)} %reshape_reshape.16.wo_ref), custom_call_target="tpu_custom_call" | custom-call | flops 5368710 | bytes 16778 | tf_op jit(solution)/shard_map/output_forward/pallas_call | solution.py:792
  255.5 12.4 %output_forward.3 = (bf16[1,256,2048]{2,1,0:T(8,128)(2,1)}, bf16[1,256,2048]{2,1,0:T(8,128)(2,1)}, bf16[1,256,2048]{2,1,0:T(8,128)(2,1)}, bf16[1,256,2048]{2,1,0:T(8,128)(2,1)}) custom-call(s32[4]{0:T(128)} %fusion.18.order_ref, bf16[2048,1024]{1,0:T(8,128)(2,1)} %bitcast.114, bf16[2048,1024]{1,0:T(8,128)(2,1)} %bitcast.111, bf16[2048,256]{1,0:T(8,128)(2,1)} %bitcast.124, ...), custom_call_target="tpu_custom_call" | custom-call | flops 5368710 | bytes 16778 | tf_op jit(solution)/shard_map/output_forward/pallas_call | solution.py:792
  283.3 15.9 %gradient.3 = (bf16[2,256,1024]{2,1,0:T(8,128)(2,1)}, bf16[2,256,1024]{2,1,0:T(8,128)(2,1)}, bf16[2,256,1024]{2,1,0:T(8,128)(2,1)}, bf16[2,256,1024]{2,1,0:T(8,128)(2,1)}) custom-call(s32[8]{0:T(128)} %stack.187.block_ref.refs_0_, bf16[2048,2048]{1,0:T(8,128)(2,1)} %bitcast.103, bf16[2048,1024]{1,0:T(8,128)(2,1)} %bitcast.115), custom_call_target="tpu_custom_call" | custom-call | flops 8589935 | bytes 16778 | tf_op jit(solution)/shard_map/gradient/pallas_call | solution.py:407
  300.0 13.8 %hidden_backward.1 = (bf16[2048,1024]{1,0:T(8,128)(2,1)}, f32[8,1024]{1,0:T(8,128)}) custom-call(bf16[2048,2048]{1,0:T(8,128)(2,1)} %bitcast.104, bf16[2048,1024]{1,0:T(8,128)(2,1)} %bitcast.112, bf16[2048,1024]{1,0:T(8,128)(2,1)} %bitcast.122), custom_call_target="tpu_custom_call" | custom-call | flops 8589935 | bytes 25166 | tf_op jit(solution)/shard_map/hidden_backward/pallas_call | solution.py:830
  313.8 10.2 %attn_backward.2 = (bf16[2,1024,768]{2,1,0:T(8,128)(2,1)}, f32[1,8,768]{2,1,0:T(8,128)}) custom-call(bf16[2,1024,2048]{2,1,0:T(8,128)(2,1)} %bitcast.105, bf16[256,2048]{1,0:T(8,128)(2,1)} %reshape_reshape.16.wo_ref, bf16[2,1024,768]{2,1,0:T(8,128)(2,1)} %bitcast.117, f32[2,1024,128]{2,1,0:T(8,128)} %get-tuple-element.369.lse_ref, ...), custom_call_target="tpu_custom_call" | custom-call | flops 3758097 | bytes 16778 | tf_op jit(solution)/shard_map/attn_backward/pallas_call | solution.py:731
  331.7 13.6 %input_backward.2 = bf16[4,256,2048]{2,1,0:T(8,128)(2,1)} custom-call(s32[4]{0:T(128)} %fusion.18.order_ref, bf16[2048,1024]{1,0:T(8,128)(2,1)} %get-tuple-element.410.du_ref.refs_2_, bf16[2048,768]{1,0:T(8,128)(2,1)} %bitcast.119, bf16[2048,1920]{1,0:T(8,128)(2,1)} %bitcast.91, bf16[2048,1920]{1,0:T(8,128)(2,1)} %bitcast.92, bf16[2048,1920]{1,0:T(8,128)(2,1)} %bitcast.93, ...), custom_call_target="tpu_custom_call" | custom-call | flops 7516193 | bytes 25166 | tf_op jit(solution)/shard_map/input_backward/pallas_call | solution.py:866
  355.7 10.2 %attn_backward.3 = (bf16[2,1024,768]{2,1,0:T(8,128)(2,1)}, f32[1,8,768]{2,1,0:T(8,128)}) custom-call(bf16[2,1024,2048]{2,1,0:T(8,128)(2,1)} %bitcast.106, bf16[256,2048]{1,0:T(8,128)(2,1)} %reshape_reshape.16.wo_ref, bf16[2,1024,768]{2,1,0:T(8,128)(2,1)} %bitcast.118, f32[2,1024,128]{2,1,0:T(8,128)} %get-tuple-element.369.lse_ref, ...), custom_call_target="tpu_custom_call", output_to_operand_aliasing={{0}: (5, {})} | custom-call | flops 3758097 | bytes 16778 | tf_op jit(solution)/shard_map/attn_backward/pallas_call | solution.py:731
  365.9 16.1 %input_backward.3 = (bf16[1,256,2048]{2,1,0:T(8,128)(2,1)}, bf16[1,256,2048]{2,1,0:T(8,128)(2,1)}, bf16[1,256,2048]{2,1,0:T(8,128)(2,1)}, bf16[1,256,2048]{2,1,0:T(8,128)(2,1)}) custom-call(s32[4]{0:T(128)} %fusion.18.order_ref, bf16[2048,1024]{1,0:T(8,128)(2,1)} %get-tuple-element.410.du_ref.refs_2_, bf16[2048,768]{1,0:T(8,128)(2,1)} %bitcast.120, ...), custom_call_target="tpu_custom_call" | custom-call | flops 7516193 | bytes 25166 | tf_op jit(solution)/shard_map/input_backward/pallas_call | solution.py:866
  388.8 19.1 %gradient.4 = (bf16[2,256,1024]{2,1,0:T(8,128)(2,1)}, bf16[2,256,1024]{2,1,0:T(8,128)(2,1)}, bf16[2,256,1024]{2,1,0:T(8,128)(2,1)}, bf16[2,256,1024]{2,1,0:T(8,128)(2,1)}, f32[2048,128]{1,0:T(8,128)}) custom-call(s32[8]{0:T(128)} %stack.187.block_ref.refs_0_, bf16[2048,2048]{1,0:T(8,128)(2,1)} %bitcast.108, ...), custom_call_target="tpu_custom_call" | custom-call | flops 8589935 | bytes 16778 | tf_op jit(solution)/shard_map/gradient/pallas_call | solution.py:407
  416.2 17.1 %gradient.5 = (bf16[2,256,896]{2,1,0:T(8,128)(2,1)}, bf16[2,256,896]{2,1,0:T(8,128)(2,1)}, bf16[2,256,896]{2,1,0:T(8,128)(2,1)}, bf16[2,256,896]{2,1,0:T(8,128)(2,1)}) custom-call(s32[8]{0:T(128)} %stack.187.block_ref.refs_0_, bf16[2048,2048]{1,0:T(8,128)(2,1)} %bitcast.109, bf16[2048,768]{1,0:T(8,128)(2,1)} %bitcast.121, ...), custom_call_target="tpu_custom_call" | custom-call | flops 7516193 | bytes 15729 | tf_op jit(solution)/shard_map/gradient/pallas_call | solution.py:407
  455.0 16.2 %collective-permute-done.45.refs_2_ = bf16[2,256,896]{2,1,0:T(8,128)(2,1)S(1)} collective-permute-done((bf16[2,256,896]{2,1,0:T(8,128)(2,1)}, bf16[2,256,896]{2,1,0:T(8,128)(2,1)S(1)}, u32[]{:S(2)}, u32[]{:S(2)}) %collective-permute-start.45) | collective-permute-done | bytes 917536 | tf_op jit(solution)/shard_map/ppermute | solution.py:87
  496.1 10.0 %all-to-all-done.4 = bf16[4,2,64,1024]{3,2,1,0:T(8,128)(2,1)S(1)} async-done(((bf16[4,2,64,1024]{3,2,1,0:T(8,128)(2,1)}), bf16[4,2,64,1024]{3,2,1,0:T(8,128)(2,1)S(1)}, u32[]{:S(2)}, u32[]{:S(2)}) %all-to-all-start.4) | async-done | bytes 1048608 | tf_op jit(solution)/shard_map/all_to_all | solution.py:1229
  515.9 7.6 %adam_columns.4 = (f32[64,16384]{1,0:T(8,128)}, f32[64,16384]{1,0:T(8,128)}, f32[64,16384]{1,0:T(8,128)}, f32[64,16384]{1,0:T(8,128)}) custom-call(s32[1]{0:T(128)} %bitcast.4.c_ref, bf16[4,64,1024]{2,1,0:T(8,128)(2,1)} %get-tuple-element.530.refs_0_, bf16[4,64,1024]{2,1,0:T(8,128)(2,1)} %copy-done.42, f32[64,16384]{1,0:T(8,128)} %refs_2_.9, ...), custom_call_target="tpu_custom_call" | custom-call | flops 15729 | bytes 15729 | tf_op jit(solution)/shard_map/adam_columns/pallas_call | solution.py:914
  524.2 7.6 %adam_columns.5 = (f32[64,16384]{1,0:T(8,128)}, f32[64,16384]{1,0:T(8,128)}, f32[64,16384]{1,0:T(8,128)}, f32[64,16384]{1,0:T(8,128)}) custom-call(s32[1]{0:T(128)} %bitcast.4.c_ref, bf16[4,64,1024]{2,1,0:T(8,128)(2,1)} %get-tuple-element.532.refs_0_, ...), custom_call_target="tpu_custom_call", output_to_operand_aliasing={{0}: (6, {}), {1}: (7, {}), {2}: (8, {}), {3}: (9, {})} | custom-call | flops 15729 | bytes 15729 | tf_op jit(solution)/shard_map/adam_columns/pallas_call | solution.py:914
  538.8 7.0 %adam_columns.6 = (f32[64,8192]{1,0:T(8,128)}, f32[64,8192]{1,0:T(8,128)}, f32[64,8192]{1,0:T(8,128)}, f32[64,8192]{1,0:T(8,128)}) custom-call(s32[1]{0:T(128)} %bitcast.4.c_ref, bf16[4,64,896]{2,1,0:T(8,128)(2,1)} %copy-done.17, bf16[4,64,896]{2,1,0:T(8,128)(2,1)} %copy-done.36, f32[64,8192]{1,0:T(8,128)} %refs_1_.5, f32[64,8192]{1,0:T(8,128)} %refs_2_.11, ...), custom_call_target="tpu_custom_call" | custom-call | flops 11797 | bytes 11797 | tf_op jit(solution)/shard_map/adam_columns/pallas_call | solution.py:914
  (297 shorter events, 243.5 us)
Async XLA Ops:
  5.5 39.6 %all-to-all-start = ((bf16[4,64,1920]{2,1,0:T(8,128)(2,1)}), bf16[4,64,1920]{2,1,0:T(8,128)(2,1)S(1)}, u32[]{:S(2)}, u32[]{:S(2)}) async-start(bf16[4,64,1920]{2,1,0:T(8,128)(2,1)} %prepare.4), calls=%async_computation | async-start | bytes 1966080 | tf_op jit(solution)/shard_map/all_to_all | solution.py:1065
  13.6 31.5 %collective-permute-start.1 = (bf16[4,64,1920]{2,1,0:T(8,128)(2,1)}, bf16[4,64,1920]{2,1,0:T(8,128)(2,1)S(1)}, u32[]{:S(2)}, u32[]{:S(2)}) collective-permute-start(bf16[4,64,1920]{2,1,0:T(8,128)(2,1)} %prepare.5), channel_id=1, source_target_pairs={{0,4},{1,5},{2,6},{3,7},{4,0},{5,1},{6,2},{7,3},{8,12},{9,13},{10,... | collective-permute-start | bytes 2949128 | tf_op jit(solution)/shard_map/ppermute | solution.py:87
  15.6 29.5 %collective-permute-start.2 = (bf16[64,2048]{1,0:T(8,128)(2,1)S(1)}, bf16[64,2048]{1,0:T(8,128)(2,1)S(1)}, u32[]{:S(2)}, u32[]{:S(2)}) collective-permute-start(bf16[64,2048]{1,0:T(8,128)(2,1)S(1)} %slice.122), channel_id=1, source_target_pairs={{0,0},{1,8},{2,16},{3,24},{4,4},{5,12},{6,20},{7,28},{8,9},{9,1},{... | collective-permute-start | bytes 786440 | tf_op jit(solution)/shard_map/ppermute | solution.py:1120
  46.1 27.3 %all-to-all-start.1 = ((bf16[4,64,1920]{2,1,0:T(8,128)(2,1)}), bf16[4,64,1920]{2,1,0:T(8,128)(2,1)S(1)}, u32[]{:S(2)}, u32[]{:S(2)}) async-start(bf16[4,64,1920]{2,1,0:T(8,128)(2,1)} %copy-done.32), calls=%async_computation.1 | async-start | bytes 1966080 | tf_op jit(solution)/shard_map/all_to_all | solution.py:1065
  74.7 30.7 %all-to-all-start.2 = ((bf16[4,2,64,1024]{3,2,1,0:T(8,128)(2,1)}), bf16[4,2,64,1024]{3,2,1,0:T(8,128)(2,1)S(1)}, u32[]{:S(2)}, u32[]{:S(2)}) async-start(bf16[4,2,64,1024]{3,2,1,0:T(8,128)(2,1)} %copy.76), calls=%async_computation.2 | async-start | bytes 2097152 | tf_op jit(solution)/shard_map/all_to_all | solution.py:1129
  105.4 26.6 %collective-permute-start.10 = (bf16[1,256,2048]{2,1,0:T(8,128)(2,1)S(1)}, bf16[1,256,2048]{2,1,0:T(8,128)(2,1)}, u32[]{:S(2)}, u32[]{:S(2)}) collective-permute-start(bf16[1,256,2048]{2,1,0:T(8,128)(2,1)S(1)} %copy-done), channel_id=1, source_target_pairs={{0,1},{1,2},{2,3},{3,0},{4,5},{5,6},{6,7},{7,4},{8,9},{9,10},{10,1... | collective-permute-start | bytes 3145736 | tf_op jit(solution)/shard_map/ppermute | solution.py:87
  132.0 29.4 %collective-permute-start.12 = (bf16[640,1024]{1,0:T(8,128)(2,1)}, bf16[640,1024]{1,0:T(8,128)(2,1)S(1)}, u32[]{:S(2)}, u32[]{:S(2)}) collective-permute-start(bf16[640,1024]{1,0:T(8,128)(2,1)} %pad_maximum_fusion.1), channel_id=1, source_target_pairs={{0,8},{1,9},{2,10},{3,11},{4,12},{5,13},{6,14},{7,15},{8,0},{9,1},... | collective-permute-start | bytes 3932168 | tf_op jit(solution)/shard_map/ppermute | solution.py:87
  132.6 29.1 %collective-permute-start.13 = (bf16[640,1024]{1,0:T(8,128)(2,1)}, bf16[640,1024]{1,0:T(8,128)(2,1)S(1)}, u32[]{:S(2)}, u32[]{:S(2)}) collective-permute-start(bf16[640,1024]{1,0:T(8,128)(2,1)} %pad_maximum_fusion.1), channel_id=1, source_target_pairs={{0,16},{1,17},{2,18},{3,19},{4,20},{5,21},{6,22},{7,23},{8,24},{9,... | collective-permute-start | bytes 3932168 | tf_op jit(solution)/shard_map/ppermute | solution.py:87
  134.4 26.9 %collective-permute-start.14 = (bf16[1,256,2048]{2,1,0:T(8,128)(2,1)}, bf16[1,256,2048]{2,1,0:T(8,128)(2,1)}, u32[]{:S(2)}, u32[]{:S(2)}) collective-permute-start(bf16[1,256,2048]{2,1,0:T(8,128)(2,1)} %collective-permute-done.10.refs_0_), channel_id=1, source_target_pairs={{0,1},{1,2},{2,3},{3,0},{4,5},{5,6},{6,7},{7,4},{8,9},{9,10},{10,1... | collective-permute-start | bytes 3145736 | tf_op jit(solution)/shard_map/ppermute | solution.py:87
  164.0 27.1 %collective-permute-start.18 = (bf16[1,256,2048]{2,1,0:T(8,128)(2,1)}, bf16[1,256,2048]{2,1,0:T(8,128)(2,1)}, u32[]{:S(2)}, u32[]{:S(2)}) collective-permute-start(bf16[1,256,2048]{2,1,0:T(8,128)(2,1)} %collective-permute-done.14.refs_0_), channel_id=1, source_target_pairs={{0,1},{1,2},{2,3},{3,0},{4,5},{5,6},{6,7},{7,4},{8,9},{9,10},{10,1... | collective-permute-start | bytes 3145736 | tf_op jit(solution)/shard_map/ppermute | solution.py:87
  191.9 26.1 %collective-permute-start.20 = (bf16[1,256,2048]{2,1,0:T(8,128)(2,1)S(1)}, bf16[1,256,2048]{2,1,0:T(8,128)(2,1)}, u32[]{:S(2)}, u32[]{:S(2)}) collective-permute-start(bf16[1,256,2048]{2,1,0:T(8,128)(2,1)S(1)} %copy-done.5), channel_id=1, source_target_pairs={{0,1},{1,2},{2,3},{3,0},{4,5},{5,6},{6,7},{7,4},{8,9},{9,10},{10,1... | collective-permute-start | bytes 3145736 | tf_op jit(solution)/shard_map/ppermute | solution.py:87
  219.3 26.8 %collective-permute-start.22 = (bf16[1,256,2048]{2,1,0:T(8,128)(2,1)}, bf16[1,256,2048]{2,1,0:T(8,128)(2,1)S(1)}, u32[]{:S(2)}, u32[]{:S(2)}) collective-permute-start(bf16[1,256,2048]{2,1,0:T(8,128)(2,1)} %collective-permute-done.20), channel_id=1, source_target_pairs={{0,1},{1,2},{2,3},{3,0},{4,5},{5,6},{6,7},{7,4},{8,9},{9,10},{10,1... | collective-permute-start | bytes 3145736 | tf_op jit(solution)/shard_map/ppermute | solution.py:87
  246.9 26.1 %collective-permute-start.24 = (bf16[1,256,2048]{2,1,0:T(8,128)(2,1)S(1)}, bf16[1,256,2048]{2,1,0:T(8,128)(2,1)}, u32[]{:S(2)}, u32[]{:S(2)}) collective-permute-start(bf16[1,256,2048]{2,1,0:T(8,128)(2,1)S(1)} %collective-permute-done.22), channel_id=1, source_target_pairs={{0,1},{1,2},{2,3},{3,0},{4,5},{5,6},{6,7},{7,4},{8,9},{9,10},{10,1... | collective-permute-start | bytes 3145736 | tf_op jit(solution)/shard_map/ppermute | solution.py:87
  275.7 48.3 %collective-permute-start.29 = (bf16[1,256,2048]{2,1,0:T(8,128)(2,1)}, bf16[1,256,2048]{2,1,0:T(8,128)(2,1)S(1)}, u32[]{:S(2)}, u32[]{:S(2)}) collective-permute-start(bf16[1,256,2048]{2,1,0:T(8,128)(2,1)} %get-tuple-element.373), channel_id=1, source_target_pairs={{0,2},{3,1},{4,6},{7,5},{8,10},{11,9},{12,14},{15,13},{16,18},{19,... | collective-permute-start | bytes 3145736 | tf_op jit(solution)/shard_map/ppermute | solution.py:87
  277.1 47.0 %collective-permute-start.30 = (bf16[1,256,2048]{2,1,0:T(8,128)(2,1)}, bf16[1,256,2048]{2,1,0:T(8,128)(2,1)S(1)}, u32[]{:S(2)}, u32[]{:S(2)}) collective-permute-start(bf16[1,256,2048]{2,1,0:T(8,128)(2,1)} %get-tuple-element.373), channel_id=1, source_target_pairs={{1,2},{2,1},{5,6},{6,5},{9,10},{10,9},{13,14},{14,13},{17,18},{18,... | collective-permute-start | bytes 3145736 | tf_op jit(solution)/shard_map/ppermute | solution.py:87
  278.2 45.8 %collective-permute-start.28 = (bf16[1,256,2048]{2,1,0:T(8,128)(2,1)}, bf16[1,256,2048]{2,1,0:T(8,128)(2,1)S(1)}, u32[]{:S(2)}, u32[]{:S(2)}) collective-permute-start(bf16[1,256,2048]{2,1,0:T(8,128)(2,1)} %get-tuple-element.372), channel_id=1, source_target_pairs={{0,1},{1,0},{2,3},{3,2},{4,5},{5,4},{6,7},{7,6},{8,9},{9,8},{10,11... | collective-permute-start | bytes 3145736 | tf_op jit(solution)/shard_map/ppermute | solution.py:87
  351.8 30.2 %all-to-all-start.3 = ((bf16[4,2,64,1024]{3,2,1,0:T(8,128)(2,1)}), bf16[4,2,64,1024]{3,2,1,0:T(8,128)(2,1)S(1)}, u32[]{:S(2)}, u32[]{:S(2)}) async-start(bf16[4,2,64,1024]{3,2,1,0:T(8,128)(2,1)} %final_blocks.3), calls=%async_computation.3 | async-start | bytes 2097152 | tf_op jit(solution)/shard_map/all_to_all | solution.py:1229
  382.0 51.4 %collective-permute-start.40 = (bf16[1,256,2048]{2,1,0:T(8,128)(2,1)}, bf16[1,256,2048]{2,1,0:T(8,128)(2,1)}, u32[]{:S(2)}, u32[]{:S(2)}) collective-permute-start(bf16[1,256,2048]{2,1,0:T(8,128)(2,1)} %get-tuple-element.430), channel_id=1, source_target_pairs={{0,2},{3,1},{4,6},{7,5},{8,10},{11,9},{12,14},{15,13},{16,18},{19,... | collective-permute-start | bytes 3145736 | tf_op jit(solution)/shard_map/ppermute | solution.py:87
  387.2 46.2 %collective-permute-start.41 = (bf16[1,256,2048]{2,1,0:T(8,128)(2,1)}, bf16[1,256,2048]{2,1,0:T(8,128)(2,1)}, u32[]{:S(2)}, u32[]{:S(2)}) collective-permute-start(bf16[1,256,2048]{2,1,0:T(8,128)(2,1)} %get-tuple-element.430), channel_id=1, source_target_pairs={{1,2},{2,1},{5,6},{6,5},{9,10},{10,9},{13,14},{14,13},{17,18},{18,... | collective-permute-start | bytes 3145736 | tf_op jit(solution)/shard_map/ppermute | solution.py:87
  433.8 43.1 %collective-permute-start.44 = (bf16[1,256,2048]{2,1,0:T(8,128)(2,1)S(1)}, bf16[1,256,2048]{2,1,0:T(8,128)(2,1)}, u32[]{:S(2)}, u32[]{:S(2)}) collective-permute-start(bf16[1,256,2048]{2,1,0:T(8,128)(2,1)S(1)} %fusion.10), channel_id=1, source_target_pairs={{0,1},{1,3},{2,0},{3,2},{4,5},{5,7},{6,4},{7,6},{8,9},{9,11},{10,8... | collective-permute-start | bytes 3145736 | tf_op jit(solution)/shard_map/ppermute | solution.py:87
  440.6 30.6 %collective-permute-start.45 = (bf16[2,256,896]{2,1,0:T(8,128)(2,1)}, bf16[2,256,896]{2,1,0:T(8,128)(2,1)S(1)}, u32[]{:S(2)}, u32[]{:S(2)}) collective-permute-start(bf16[2,256,896]{2,1,0:T(8,128)(2,1)} %get-tuple-element.456), channel_id=1, source_target_pairs={{0,8},{1,9},{2,10},{3,11},{4,12},{5,13},{6,14},{7,15},{8,0},{9,1},... | collective-permute-start | bytes 2752520 | tf_op jit(solution)/shard_map/ppermute | solution.py:87
  441.2 30.0 %collective-permute-start.46 = (bf16[2,256,896]{2,1,0:T(8,128)(2,1)}, bf16[2,256,896]{2,1,0:T(8,128)(2,1)}, u32[]{:S(2)}, u32[]{:S(2)}) collective-permute-start(bf16[2,256,896]{2,1,0:T(8,128)(2,1)} %get-tuple-element.457), channel_id=1, source_target_pairs={{0,16},{1,17},{2,18},{3,19},{4,20},{5,21},{6,22},{7,23},{8,24},{9,... | collective-permute-start | bytes 2752520 | tf_op jit(solution)/shard_map/ppermute | solution.py:87
  477.6 28.4 %all-to-all-start.4 = ((bf16[4,2,64,1024]{3,2,1,0:T(8,128)(2,1)}), bf16[4,2,64,1024]{3,2,1,0:T(8,128)(2,1)S(1)}, u32[]{:S(2)}, u32[]{:S(2)}) async-start(bf16[4,2,64,1024]{3,2,1,0:T(8,128)(2,1)} %final_blocks.4), calls=%async_computation.4 | async-start | bytes 2097152 | tf_op jit(solution)/shard_map/all_to_all | solution.py:1229
  506.1 25.9 %all-to-all-start.5 = ((bf16[4,2,64,896]{3,2,1,0:T(8,128)(2,1)}), bf16[4,2,64,896]{3,2,1,0:T(8,128)(2,1)S(1)}, u32[]{:S(2)}, u32[]{:S(2)}) async-start(bf16[4,2,64,896]{3,2,1,0:T(8,128)(2,1)} %final_blocks.5), calls=%async_computation.5 | async-start | bytes 1835008 | tf_op jit(solution)/shard_map/all_to_all | solution.py:1229
  (85 other events, 976.4 us)

commit v5 on v4

--- a/solution.py
+++ b/solution.py
@@ -214,8 +214,11 @@
     out_ref = refs[-1]
     at = 0
     for ref in refs[:-1]:
-        out_ref[0, :, at : at + ref.shape[1]] = ref[...].astype(bf16)
-        at += ref.shape[1]
+        value = ref[...].astype(bf16)
+        if value.shape[1] < LANES:
+            value = jnp.pad(value, ((0, 0), (0, LANES - value.shape[1])))
+        out_ref[0, :, at : at + value.shape[1]] = value
+        at += value.shape[1]
 
 
 def prepare(lay, r, sources):
@@ -226,7 +229,7 @@
             return pl.BlockSpec((rows, width), lambda z, c: (0, 0))
         return pl.BlockSpec((rows, width), lambda z, c: (0, first + z * pair + (c[0] ^ r)))
 
-    total = sum(width for _, _, width in sources)
+    total = sum(max(width, LANES) for _, _, width in sources)
     return pl.pallas_call(
         cast_kernel,
         grid_spec=pltpu.PrefetchScalarGridSpec(
@@ -903,7 +906,7 @@
     nz, rows, _ = parts[0].shape
     pair = len(parts)
     total = state[0].shape[1]
-    places = max(1, min(nz, 2048 // (pair * piece)))
+    places = max(1, min(nz, 1024 // (pair * piece)))
     wide = places * pair * piece
     steps = nz // places
     first = start // wide
@@ -1051,10 +1054,9 @@
     seqs, length = count * pair, span * nz
     tokens_here = seqs * length
 
-    wide_small = jnp.pad(small, ((0, 0), (0, LANES - small.shape[1])))
     qu_sources = [(mlp_params, 0, unit)]
     qu_sources += [(attn_params, j * HEADS, hd) for j in range(3)]
-    qu_sources += [(wide_small, None, LANES)]
+    qu_sources += [(small, None, small.shape[1])]
     dn_sources = [(mlp_params, HEADS, unit)]
 
     def swap(sources, r):

time: 564 us -> 564 us (level)
  no operation moved by 1% of the time
where the time goes in v5:
time: 564 us; the launch traced here: 554 us
  Pallas kernels  279 us (49%)
  waiting for transfers between devices  139 us (25%)
  starting transfers between devices  78.6 us (14%)
  local copies, waits for them, and re-layouts  25.4 us (5%)
  other arithmetic  24.8 us (4%)
  matrix products  5.72 us (1%)
    ppermute x53, waiting for transfers between devices, hop(): return lax.ppermute(value, AXES, self.perm(target))  111 us
    pallas_call x3, Pallas kernels, gradient_call(): pl.pallas_call(partial(kernel, half), grid_spec=pltpu.PrefetchScalarGridS...  52.1 us
    ppermute x53, starting transfers between devices, hop(): return lax.ppermute(value, AXES, self.perm(target))  47.5 us
    pallas_call x3, Pallas kernels, piece_forward(): pl.pallas_call(partial(piece_kernel, pair, places, wide // 24), grid_spec...  41.4 us
    pallas_call x8, Pallas kernels, place(): pl.pallas_call(partial(place_kernel, count, tile), grid_spec=pltpu.Prefet...  30.5 us
    pallas_call x2, Pallas kernels, input_backward(): pl.pallas_call(partial(input_kernel, len(more), hd), grid_spec=pltpu.Pref...  29.7 us
    pallas_call x4, Pallas kernels, adam_columns(): pl.pallas_call(partial(adam_kernel, pair, places, rate), grid_spec=pltpu....  25.5 us
    pallas_call x2, Pallas kernels, output_forward(): pl.pallas_call(partial(output_kernel, len(more)), grid_spec=pltpu.Prefetc...  23 us
  transfers between devices with their start and end apart: 61, of which 25 were waited for; matrix products, arithmetic and copies ran while one was open for 8% of the time, Pallas kernels for 49%

profile of v5, /device:TPU:5, one launch (start us, length us, event | category | flops | bytes accessed | tf_op | source)
XLA Modules:
  0.0 554.2 jit_solution(2890295348488723507)
XLA Ops:
  31.4 13.7 %collective-permute-done.2 = bf16[64,2048]{1,0:T(8,128)(2,1)S(1)} collective-permute-done((bf16[64,2048]{1,0:T(8,128)(2,1)S(1)}, bf16[64,2048]{1,0:T(8,128)(2,1)S(1)}, u32[]{:S(2)}, u32[]{:S(2)}) %collective-permute-start.2) | collective-permute-done | bytes 262176 | tf_op jit(solution)/shard_map/ppermute | solution.py:1122
  49.7 21.6 %collective-permute-done.3.refs_1_ = bf16[256,1920]{1,0:T(8,128)(2,1)S(1)} collective-permute-done((bf16[256,1920]{1,0:T(8,128)(2,1)S(1)}, bf16[256,1920]{1,0:T(8,128)(2,1)S(1)}, u32[]{:S(2)}, u32[]{:S(2)}) %collective-permute-start.3) | collective-permute-done | bytes 983072 | tf_op jit(solution)/shard_map/ppermute | solution.py:87
  83.1 21.3 %collective-permute-done.5.refs_5_ = bf16[256,1920]{1,0:T(8,128)(2,1)S(1)} collective-permute-done((bf16[256,1920]{1,0:T(8,128)(2,1)}, bf16[256,1920]{1,0:T(8,128)(2,1)S(1)}, u32[]{:S(2)}, u32[]{:S(2)}) %collective-permute-start.5) | collective-permute-done | bytes 983072 | tf_op jit(solution)/shard_map/ppermute | solution.py:87
  110.1 5.8 %place.8.refs_2_ = bf16[8,256,1920]{2,1,0:T(8,128)(2,1)} custom-call(s32[6]{0:T(128)} %stack.172.slot_ref, bf16[256,1920]{1,0:T(8,128)(2,1)} %bitcast.133, bf16[256,1920]{1,0:T(8,128)(2,1)} %copy-done.33, bf16[256,1920]{1,0:T(8,128)(2,1)} %collective-permute-done.4.refs_2_, bf16[256,1920]{1,0:T(8,128)(2,1)} %bitcast.136, ...), custom_call_target="tpu_custom_call" | custom-call | flops 1 | bytes 11797 | tf_op jit(solution)/shard_map/place/pallas_call | solution.py:273
  118.1 11.7 %collective-permute-done.8.refs_0_ = bf16[256,1920]{1,0:T(8,128)(2,1)} collective-permute-done((bf16[256,1920]{1,0:T(8,128)(2,1)}, bf16[256,1920]{1,0:T(8,128)(2,1)}, u32[]{:S(2)}, u32[]{:S(2)}) %collective-permute-start.8) | collective-permute-done | bytes 983072 | tf_op jit(solution)/shard_map/ppermute | solution.py:87
  144.8 11.2 %piece_forward.3 = (bf16[2,1,4,256,2048]{4,3,2,1,0:T(8,128)(2,1)}, bf16[2,1,4,256,768]{4,3,2,1,0:T(8,128)(2,1)}, bf16[2,1,4,256,1024]{4,3,2,1,0:T(8,128)(2,1)}, bf16[2,1,4,256,1024]{4,3,2,1,0:T(8,128)(2,1)}) custom-call(s32[1]{0:T(128)} %bitcast.21.pos_ref, bf16[1,256,2048]{2,1,0:T(8,128)(2,1)} %refs_0_.8, bf16[1,256,2048]{2,1,0:T(8,128)(2,1)} %copy-done.31, ...), custom_call_target="tpu_custom_call" | custom-call | flops 3758097 | bytes 12583 | tf_op jit(solution)/shard_map/piece_forward/pallas_call | solution.py:620
  175.1 11.4 %piece_forward.4 = (bf16[2,1,4,256,2048]{4,3,2,1,0:T(8,128)(2,1)}, bf16[2,1,4,256,768]{4,3,2,1,0:T(8,128)(2,1)}, bf16[2,1,4,256,1024]{4,3,2,1,0:T(8,128)(2,1)}, bf16[2,1,4,256,1024]{4,3,2,1,0:T(8,128)(2,1)}) custom-call(s32[1]{0:T(128)} %bitcast.27.pos_ref, ...), custom_call_target="tpu_custom_call", output_to_operand_aliasing={{0}: (8, {}), {1}: (9, {}), {2}: (10, {}), {3}: (11, {})} | custom-call | flops 3758097 | bytes 12583 | tf_op jit(solution)/shard_map/piece_forward/pallas_call | solution.py:620
  195.9 18.8 %piece_forward.5 = (bf16[2,1,4,256,2048]{4,3,2,1,0:T(8,128)(2,1)}, bf16[2,1,4,256,768]{4,3,2,1,0:T(8,128)(2,1)}, bf16[2,1,4,256,1024]{4,3,2,1,0:T(8,128)(2,1)}, bf16[2,1,4,256,1024]{4,3,2,1,0:T(8,128)(2,1)}) custom-call(s32[2]{0:T(128)} %pad_add_fusion.1.pos_ref, ...), custom_call_target="tpu_custom_call", output_to_operand_aliasing={{0}: (10, {}), {1}: (11, {}), {2}: (12, {}), {3}: (13, {})} | custom-call | flops 7516193 | bytes 25166 | tf_op jit(solution)/shard_map/piece_forward/pallas_call | solution.py:620
  226.4 6.2 %attn_forward.1 = (bf16[2,1024,256]{2,1,0:T(8,128)(2,1)}, f32[2,1024,128]{2,1,0:T(8,128)}) custom-call(bf16[2,1024,768]{2,1,0:T(8,128)(2,1)} %bitcast.116), custom_call_target="tpu_custom_call" | custom-call | flops 2147484 | bytes 12583 | tf_op jit(solution)/shard_map/attn_forward/pallas_call | solution.py:664
  232.6 10.6 %output_forward.2 = bf16[4,256,2048]{2,1,0:T(8,128)(2,1)} custom-call(s32[4]{0:T(128)} %fusion.18.order_ref, bf16[2048,1024]{1,0:T(8,128)(2,1)} %bitcast.113, bf16[2048,1024]{1,0:T(8,128)(2,1)} %bitcast.110, bf16[2048,256]{1,0:T(8,128)(2,1)} %bitcast.123, bf16[256,2048]{1,0:T(8,128)(2,1)} %reshape_reshape.16.wo_ref), custom_call_target="tpu_custom_call" | custom-call | flops 5368710 | bytes 16778 | tf_op jit(solution)/shard_map/output_forward/pallas_call | solution.py:795
  255.5 12.4 %output_forward.3 = (bf16[1,256,2048]{2,1,0:T(8,128)(2,1)}, bf16[1,256,2048]{2,1,0:T(8,128)(2,1)}, bf16[1,256,2048]{2,1,0:T(8,128)(2,1)}, bf16[1,256,2048]{2,1,0:T(8,128)(2,1)}) custom-call(s32[4]{0:T(128)} %fusion.18.order_ref, bf16[2048,1024]{1,0:T(8,128)(2,1)} %bitcast.114, bf16[2048,1024]{1,0:T(8,128)(2,1)} %bitcast.111, bf16[2048,256]{1,0:T(8,128)(2,1)} %bitcast.124, ...), custom_call_target="tpu_custom_call" | custom-call | flops 5368710 | bytes 16778 | tf_op jit(solution)/shard_map/output_forward/pallas_call | solution.py:795
  283.3 15.9 %gradient.3 = (bf16[2,256,1024]{2,1,0:T(8,128)(2,1)}, bf16[2,256,1024]{2,1,0:T(8,128)(2,1)}, bf16[2,256,1024]{2,1,0:T(8,128)(2,1)}, bf16[2,256,1024]{2,1,0:T(8,128)(2,1)}) custom-call(s32[8]{0:T(128)} %stack.187.block_ref.refs_0_, bf16[2048,2048]{1,0:T(8,128)(2,1)} %bitcast.103, bf16[2048,1024]{1,0:T(8,128)(2,1)} %bitcast.115), custom_call_target="tpu_custom_call" | custom-call | flops 8589935 | bytes 16778 | tf_op jit(solution)/shard_map/gradient/pallas_call | solution.py:410
  300.0 13.8 %hidden_backward.1 = (bf16[2048,1024]{1,0:T(8,128)(2,1)}, f32[8,1024]{1,0:T(8,128)}) custom-call(bf16[2048,2048]{1,0:T(8,128)(2,1)} %bitcast.104, bf16[2048,1024]{1,0:T(8,128)(2,1)} %bitcast.112, bf16[2048,1024]{1,0:T(8,128)(2,1)} %bitcast.122), custom_call_target="tpu_custom_call" | custom-call | flops 8589935 | bytes 25166 | tf_op jit(solution)/shard_map/hidden_backward/pallas_call | solution.py:833
  313.8 10.2 %attn_backward.2 = (bf16[2,1024,768]{2,1,0:T(8,128)(2,1)}, f32[1,8,768]{2,1,0:T(8,128)}) custom-call(bf16[2,1024,2048]{2,1,0:T(8,128)(2,1)} %bitcast.105, bf16[256,2048]{1,0:T(8,128)(2,1)} %reshape_reshape.16.wo_ref, bf16[2,1024,768]{2,1,0:T(8,128)(2,1)} %bitcast.117, f32[2,1024,128]{2,1,0:T(8,128)} %get-tuple-element.369.lse_ref, ...), custom_call_target="tpu_custom_call" | custom-call | flops 3758097 | bytes 16778 | tf_op jit(solution)/shard_map/attn_backward/pallas_call | solution.py:734
  331.7 13.6 %input_backward.2 = bf16[4,256,2048]{2,1,0:T(8,128)(2,1)} custom-call(s32[4]{0:T(128)} %fusion.18.order_ref, bf16[2048,1024]{1,0:T(8,128)(2,1)} %get-tuple-element.410.du_ref.refs_2_, bf16[2048,768]{1,0:T(8,128)(2,1)} %bitcast.119, bf16[2048,1920]{1,0:T(8,128)(2,1)} %bitcast.91, bf16[2048,1920]{1,0:T(8,128)(2,1)} %bitcast.92, bf16[2048,1920]{1,0:T(8,128)(2,1)} %bitcast.93, ...), custom_call_target="tpu_custom_call" | custom-call | flops 7516193 | bytes 25166 | tf_op jit(solution)/shard_map/input_backward/pallas_call | solution.py:869
  355.7 10.2 %attn_backward.3 = (bf16[2,1024,768]{2,1,0:T(8,128)(2,1)}, f32[1,8,768]{2,1,0:T(8,128)}) custom-call(bf16[2,1024,2048]{2,1,0:T(8,128)(2,1)} %bitcast.106, bf16[256,2048]{1,0:T(8,128)(2,1)} %reshape_reshape.16.wo_ref, bf16[2,1024,768]{2,1,0:T(8,128)(2,1)} %bitcast.118, f32[2,1024,128]{2,1,0:T(8,128)} %get-tuple-element.369.lse_ref, ...), custom_call_target="tpu_custom_call", output_to_operand_aliasing={{0}: (5, {})} | custom-call | flops 3758097 | bytes 16778 | tf_op jit(solution)/shard_map/attn_backward/pallas_call | solution.py:734
  365.9 16.1 %input_backward.3 = (bf16[1,256,2048]{2,1,0:T(8,128)(2,1)}, bf16[1,256,2048]{2,1,0:T(8,128)(2,1)}, bf16[1,256,2048]{2,1,0:T(8,128)(2,1)}, bf16[1,256,2048]{2,1,0:T(8,128)(2,1)}) custom-call(s32[4]{0:T(128)} %fusion.18.order_ref, bf16[2048,1024]{1,0:T(8,128)(2,1)} %get-tuple-element.410.du_ref.refs_2_, bf16[2048,768]{1,0:T(8,128)(2,1)} %bitcast.120, ...), custom_call_target="tpu_custom_call" | custom-call | flops 7516193 | bytes 25166 | tf_op jit(solution)/shard_map/input_backward/pallas_call | solution.py:869
  388.8 19.1 %gradient.4 = (bf16[2,256,1024]{2,1,0:T(8,128)(2,1)}, bf16[2,256,1024]{2,1,0:T(8,128)(2,1)}, bf16[2,256,1024]{2,1,0:T(8,128)(2,1)}, bf16[2,256,1024]{2,1,0:T(8,128)(2,1)}, f32[2048,128]{1,0:T(8,128)}) custom-call(s32[8]{0:T(128)} %stack.187.block_ref.refs_0_, bf16[2048,2048]{1,0:T(8,128)(2,1)} %bitcast.108, ...), custom_call_target="tpu_custom_call" | custom-call | flops 8589935 | bytes 16778 | tf_op jit(solution)/shard_map/gradient/pallas_call | solution.py:410
  416.2 17.1 %gradient.5 = (bf16[2,256,896]{2,1,0:T(8,128)(2,1)}, bf16[2,256,896]{2,1,0:T(8,128)(2,1)}, bf16[2,256,896]{2,1,0:T(8,128)(2,1)}, bf16[2,256,896]{2,1,0:T(8,128)(2,1)}) custom-call(s32[8]{0:T(128)} %stack.187.block_ref.refs_0_, bf16[2048,2048]{1,0:T(8,128)(2,1)} %bitcast.109, bf16[2048,768]{1,0:T(8,128)(2,1)} %bitcast.121, ...), custom_call_target="tpu_custom_call" | custom-call | flops 7516193 | bytes 15729 | tf_op jit(solution)/shard_map/gradient/pallas_call | solution.py:410
  455.1 16.2 %collective-permute-done.45.refs_2_ = bf16[2,256,896]{2,1,0:T(8,128)(2,1)S(1)} collective-permute-done((bf16[2,256,896]{2,1,0:T(8,128)(2,1)}, bf16[2,256,896]{2,1,0:T(8,128)(2,1)S(1)}, u32[]{:S(2)}, u32[]{:S(2)}) %collective-permute-start.45) | collective-permute-done | bytes 917536 | tf_op jit(solution)/shard_map/ppermute | solution.py:87
  496.1 10.0 %all-to-all-done.4 = bf16[4,2,64,1024]{3,2,1,0:T(8,128)(2,1)S(1)} async-done(((bf16[4,2,64,1024]{3,2,1,0:T(8,128)(2,1)}), bf16[4,2,64,1024]{3,2,1,0:T(8,128)(2,1)S(1)}, u32[]{:S(2)}, u32[]{:S(2)}) %all-to-all-start.4) | async-done | bytes 1048608 | tf_op jit(solution)/shard_map/all_to_all | solution.py:1231
  515.9 7.6 %adam_columns.4 = (f32[64,16384]{1,0:T(8,128)}, f32[64,16384]{1,0:T(8,128)}, f32[64,16384]{1,0:T(8,128)}, f32[64,16384]{1,0:T(8,128)}) custom-call(s32[1]{0:T(128)} %bitcast.4.c_ref, bf16[4,64,1024]{2,1,0:T(8,128)(2,1)} %get-tuple-element.530.refs_0_, bf16[4,64,1024]{2,1,0:T(8,128)(2,1)} %copy-done.42, f32[64,16384]{1,0:T(8,128)} %refs_2_.9, ...), custom_call_target="tpu_custom_call" | custom-call | flops 15729 | bytes 15729 | tf_op jit(solution)/shard_map/adam_columns/pallas_call | solution.py:917
  524.3 7.6 %adam_columns.5 = (f32[64,16384]{1,0:T(8,128)}, f32[64,16384]{1,0:T(8,128)}, f32[64,16384]{1,0:T(8,128)}, f32[64,16384]{1,0:T(8,128)}) custom-call(s32[1]{0:T(128)} %bitcast.4.c_ref, bf16[4,64,1024]{2,1,0:T(8,128)(2,1)} %get-tuple-element.532.refs_0_, ...), custom_call_target="tpu_custom_call", output_to_operand_aliasing={{0}: (6, {}), {1}: (7, {}), {2}: (8, {}), {3}: (9, {})} | custom-call | flops 15729 | bytes 15729 | tf_op jit(solution)/shard_map/adam_columns/pallas_call | solution.py:917
  538.8 7.2 %adam_columns.6 = (f32[64,8192]{1,0:T(8,128)}, f32[64,8192]{1,0:T(8,128)}, f32[64,8192]{1,0:T(8,128)}, f32[64,8192]{1,0:T(8,128)}) custom-call(s32[1]{0:T(128)} %bitcast.4.c_ref, bf16[4,64,896]{2,1,0:T(8,128)(2,1)} %copy-done.17, bf16[4,64,896]{2,1,0:T(8,128)(2,1)} %copy-done.36, f32[64,8192]{1,0:T(8,128)} %refs_1_.5, f32[64,8192]{1,0:T(8,128)} %refs_2_.11, ...), custom_call_target="tpu_custom_call" | custom-call | flops 11797 | bytes 11797 | tf_op jit(solution)/shard_map/adam_columns/pallas_call | solution.py:917
  (296 shorter events, 243.3 us)
Async XLA Ops:
  5.5 39.6 %all-to-all-start = ((bf16[4,64,1920]{2,1,0:T(8,128)(2,1)}), bf16[4,64,1920]{2,1,0:T(8,128)(2,1)S(1)}, u32[]{:S(2)}, u32[]{:S(2)}) async-start(bf16[4,64,1920]{2,1,0:T(8,128)(2,1)} %prepare.4), calls=%async_computation | async-start | bytes 1966080 | tf_op jit(solution)/shard_map/all_to_all | solution.py:1067
  13.6 31.5 %collective-permute-start.1 = (bf16[4,64,1920]{2,1,0:T(8,128)(2,1)}, bf16[4,64,1920]{2,1,0:T(8,128)(2,1)S(1)}, u32[]{:S(2)}, u32[]{:S(2)}) collective-permute-start(bf16[4,64,1920]{2,1,0:T(8,128)(2,1)} %prepare.5), channel_id=1, source_target_pairs={{0,4},{1,5},{2,6},{3,7},{4,0},{5,1},{6,2},{7,3},{8,12},{9,13},{10,... | collective-permute-start | bytes 2949128 | tf_op jit(solution)/shard_map/ppermute | solution.py:87
  15.6 29.5 %collective-permute-start.2 = (bf16[64,2048]{1,0:T(8,128)(2,1)S(1)}, bf16[64,2048]{1,0:T(8,128)(2,1)S(1)}, u32[]{:S(2)}, u32[]{:S(2)}) collective-permute-start(bf16[64,2048]{1,0:T(8,128)(2,1)S(1)} %slice.122), channel_id=1, source_target_pairs={{0,0},{1,8},{2,16},{3,24},{4,4},{5,12},{6,20},{7,28},{8,9},{9,1},{... | collective-permute-start | bytes 786440 | tf_op jit(solution)/shard_map/ppermute | solution.py:1122
  46.1 27.3 %all-to-all-start.1 = ((bf16[4,64,1920]{2,1,0:T(8,128)(2,1)}), bf16[4,64,1920]{2,1,0:T(8,128)(2,1)S(1)}, u32[]{:S(2)}, u32[]{:S(2)}) async-start(bf16[4,64,1920]{2,1,0:T(8,128)(2,1)} %copy-done.32), calls=%async_computation.1 | async-start | bytes 1966080 | tf_op jit(solution)/shard_map/all_to_all | solution.py:1067
  74.7 30.7 %all-to-all-start.2 = ((bf16[4,2,64,1024]{3,2,1,0:T(8,128)(2,1)}), bf16[4,2,64,1024]{3,2,1,0:T(8,128)(2,1)S(1)}, u32[]{:S(2)}, u32[]{:S(2)}) async-start(bf16[4,2,64,1024]{3,2,1,0:T(8,128)(2,1)} %copy.80), calls=%async_computation.2 | async-start | bytes 2097152 | tf_op jit(solution)/shard_map/all_to_all | solution.py:1131
  105.4 26.6 %collective-permute-start.10 = (bf16[1,256,2048]{2,1,0:T(8,128)(2,1)S(1)}, bf16[1,256,2048]{2,1,0:T(8,128)(2,1)}, u32[]{:S(2)}, u32[]{:S(2)}) collective-permute-start(bf16[1,256,2048]{2,1,0:T(8,128)(2,1)S(1)} %copy-done), channel_id=1, source_target_pairs={{0,1},{1,2},{2,3},{3,0},{4,5},{5,6},{6,7},{7,4},{8,9},{9,10},{10,1... | collective-permute-start | bytes 3145736 | tf_op jit(solution)/shard_map/ppermute | solution.py:87
  132.0 29.4 %collective-permute-start.12 = (bf16[640,1024]{1,0:T(8,128)(2,1)}, bf16[640,1024]{1,0:T(8,128)(2,1)S(1)}, u32[]{:S(2)}, u32[]{:S(2)}) collective-permute-start(bf16[640,1024]{1,0:T(8,128)(2,1)} %pad_maximum_fusion.1), channel_id=1, source_target_pairs={{0,8},{1,9},{2,10},{3,11},{4,12},{5,13},{6,14},{7,15},{8,0},{9,1},... | collective-permute-start | bytes 3932168 | tf_op jit(solution)/shard_map/ppermute | solution.py:87
  132.6 29.1 %collective-permute-start.13 = (bf16[640,1024]{1,0:T(8,128)(2,1)}, bf16[640,1024]{1,0:T(8,128)(2,1)S(1)}, u32[]{:S(2)}, u32[]{:S(2)}) collective-permute-start(bf16[640,1024]{1,0:T(8,128)(2,1)} %pad_maximum_fusion.1), channel_id=1, source_target_pairs={{0,16},{1,17},{2,18},{3,19},{4,20},{5,21},{6,22},{7,23},{8,24},{9,... | collective-permute-start | bytes 3932168 | tf_op jit(solution)/shard_map/ppermute | solution.py:87
  134.4 26.9 %collective-permute-start.14 = (bf16[1,256,2048]{2,1,0:T(8,128)(2,1)}, bf16[1,256,2048]{2,1,0:T(8,128)(2,1)}, u32[]{:S(2)}, u32[]{:S(2)}) collective-permute-start(bf16[1,256,2048]{2,1,0:T(8,128)(2,1)} %collective-permute-done.10.refs_0_), channel_id=1, source_target_pairs={{0,1},{1,2},{2,3},{3,0},{4,5},{5,6},{6,7},{7,4},{8,9},{9,10},{10,1... | collective-permute-start | bytes 3145736 | tf_op jit(solution)/shard_map/ppermute | solution.py:87
  164.0 27.1 %collective-permute-start.18 = (bf16[1,256,2048]{2,1,0:T(8,128)(2,1)}, bf16[1,256,2048]{2,1,0:T(8,128)(2,1)}, u32[]{:S(2)}, u32[]{:S(2)}) collective-permute-start(bf16[1,256,2048]{2,1,0:T(8,128)(2,1)} %collective-permute-done.14.refs_0_), channel_id=1, source_target_pairs={{0,1},{1,2},{2,3},{3,0},{4,5},{5,6},{6,7},{7,4},{8,9},{9,10},{10,1... | collective-permute-start | bytes 3145736 | tf_op jit(solution)/shard_map/ppermute | solution.py:87
  191.9 26.1 %collective-permute-start.20 = (bf16[1,256,2048]{2,1,0:T(8,128)(2,1)S(1)}, bf16[1,256,2048]{2,1,0:T(8,128)(2,1)}, u32[]{:S(2)}, u32[]{:S(2)}) collective-permute-start(bf16[1,256,2048]{2,1,0:T(8,128)(2,1)S(1)} %copy-done.5), channel_id=1, source_target_pairs={{0,1},{1,2},{2,3},{3,0},{4,5},{5,6},{6,7},{7,4},{8,9},{9,10},{10,1... | collective-permute-start | bytes 3145736 | tf_op jit(solution)/shard_map/ppermute | solution.py:87
  219.3 26.8 %collective-permute-start.22 = (bf16[1,256,2048]{2,1,0:T(8,128)(2,1)}, bf16[1,256,2048]{2,1,0:T(8,128)(2,1)S(1)}, u32[]{:S(2)}, u32[]{:S(2)}) collective-permute-start(bf16[1,256,2048]{2,1,0:T(8,128)(2,1)} %collective-permute-done.20), channel_id=1, source_target_pairs={{0,1},{1,2},{2,3},{3,0},{4,5},{5,6},{6,7},{7,4},{8,9},{9,10},{10,1... | collective-permute-start | bytes 3145736 | tf_op jit(solution)/shard_map/ppermute | solution.py:87
  246.9 26.1 %collective-permute-start.24 = (bf16[1,256,2048]{2,1,0:T(8,128)(2,1)S(1)}, bf16[1,256,2048]{2,1,0:T(8,128)(2,1)}, u32[]{:S(2)}, u32[]{:S(2)}) collective-permute-start(bf16[1,256,2048]{2,1,0:T(8,128)(2,1)S(1)} %collective-permute-done.22), channel_id=1, source_target_pairs={{0,1},{1,2},{2,3},{3,0},{4,5},{5,6},{6,7},{7,4},{8,9},{9,10},{10,1... | collective-permute-start | bytes 3145736 | tf_op jit(solution)/shard_map/ppermute | solution.py:87
  275.7 48.3 %collective-permute-start.29 = (bf16[1,256,2048]{2,1,0:T(8,128)(2,1)}, bf16[1,256,2048]{2,1,0:T(8,128)(2,1)S(1)}, u32[]{:S(2)}, u32[]{:S(2)}) collective-permute-start(bf16[1,256,2048]{2,1,0:T(8,128)(2,1)} %get-tuple-element.373), channel_id=1, source_target_pairs={{0,2},{3,1},{4,6},{7,5},{8,10},{11,9},{12,14},{15,13},{16,18},{19,... | collective-permute-start | bytes 3145736 | tf_op jit(solution)/shard_map/ppermute | solution.py:87
  277.1 47.0 %collective-permute-start.30 = (bf16[1,256,2048]{2,1,0:T(8,128)(2,1)}, bf16[1,256,2048]{2,1,0:T(8,128)(2,1)S(1)}, u32[]{:S(2)}, u32[]{:S(2)}) collective-permute-start(bf16[1,256,2048]{2,1,0:T(8,128)(2,1)} %get-tuple-element.373), channel_id=1, source_target_pairs={{1,2},{2,1},{5,6},{6,5},{9,10},{10,9},{13,14},{14,13},{17,18},{18,... | collective-permute-start | bytes 3145736 | tf_op jit(solution)/shard_map/ppermute | solution.py:87
  278.2 45.8 %collective-permute-start.28 = (bf16[1,256,2048]{2,1,0:T(8,128)(2,1)}, bf16[1,256,2048]{2,1,0:T(8,128)(2,1)S(1)}, u32[]{:S(2)}, u32[]{:S(2)}) collective-permute-start(bf16[1,256,2048]{2,1,0:T(8,128)(2,1)} %get-tuple-element.372), channel_id=1, source_target_pairs={{0,1},{1,0},{2,3},{3,2},{4,5},{5,4},{6,7},{7,6},{8,9},{9,8},{10,11... | collective-permute-start | bytes 3145736 | tf_op jit(solution)/shard_map/ppermute | solution.py:87
  351.8 30.2 %all-to-all-start.3 = ((bf16[4,2,64,1024]{3,2,1,0:T(8,128)(2,1)}), bf16[4,2,64,1024]{3,2,1,0:T(8,128)(2,1)S(1)}, u32[]{:S(2)}, u32[]{:S(2)}) async-start(bf16[4,2,64,1024]{3,2,1,0:T(8,128)(2,1)} %final_blocks.3), calls=%async_computation.3 | async-start | bytes 2097152 | tf_op jit(solution)/shard_map/all_to_all | solution.py:1231
  382.0 51.4 %collective-permute-start.40 = (bf16[1,256,2048]{2,1,0:T(8,128)(2,1)}, bf16[1,256,2048]{2,1,0:T(8,128)(2,1)}, u32[]{:S(2)}, u32[]{:S(2)}) collective-permute-start(bf16[1,256,2048]{2,1,0:T(8,128)(2,1)} %get-tuple-element.430), channel_id=1, source_target_pairs={{0,2},{3,1},{4,6},{7,5},{8,10},{11,9},{12,14},{15,13},{16,18},{19,... | collective-permute-start | bytes 3145736 | tf_op jit(solution)/shard_map/ppermute | solution.py:87
  387.2 46.2 %collective-permute-start.41 = (bf16[1,256,2048]{2,1,0:T(8,128)(2,1)}, bf16[1,256,2048]{2,1,0:T(8,128)(2,1)}, u32[]{:S(2)}, u32[]{:S(2)}) collective-permute-start(bf16[1,256,2048]{2,1,0:T(8,128)(2,1)} %get-tuple-element.430), channel_id=1, source_target_pairs={{1,2},{2,1},{5,6},{6,5},{9,10},{10,9},{13,14},{14,13},{17,18},{18,... | collective-permute-start | bytes 3145736 | tf_op jit(solution)/shard_map/ppermute | solution.py:87
  433.8 43.1 %collective-permute-start.44 = (bf16[1,256,2048]{2,1,0:T(8,128)(2,1)S(1)}, bf16[1,256,2048]{2,1,0:T(8,128)(2,1)}, u32[]{:S(2)}, u32[]{:S(2)}) collective-permute-start(bf16[1,256,2048]{2,1,0:T(8,128)(2,1)S(1)} %fusion.10), channel_id=1, source_target_pairs={{0,1},{1,3},{2,0},{3,2},{4,5},{5,7},{6,4},{7,6},{8,9},{9,11},{10,8... | collective-permute-start | bytes 3145736 | tf_op jit(solution)/shard_map/ppermute | solution.py:87
  440.6 30.6 %collective-permute-start.45 = (bf16[2,256,896]{2,1,0:T(8,128)(2,1)}, bf16[2,256,896]{2,1,0:T(8,128)(2,1)S(1)}, u32[]{:S(2)}, u32[]{:S(2)}) collective-permute-start(bf16[2,256,896]{2,1,0:T(8,128)(2,1)} %get-tuple-element.456), channel_id=1, source_target_pairs={{0,8},{1,9},{2,10},{3,11},{4,12},{5,13},{6,14},{7,15},{8,0},{9,1},... | collective-permute-start | bytes 2752520 | tf_op jit(solution)/shard_map/ppermute | solution.py:87
  441.2 30.0 %collective-permute-start.46 = (bf16[2,256,896]{2,1,0:T(8,128)(2,1)}, bf16[2,256,896]{2,1,0:T(8,128)(2,1)}, u32[]{:S(2)}, u32[]{:S(2)}) collective-permute-start(bf16[2,256,896]{2,1,0:T(8,128)(2,1)} %get-tuple-element.457), channel_id=1, source_target_pairs={{0,16},{1,17},{2,18},{3,19},{4,20},{5,21},{6,22},{7,23},{8,24},{9,... | collective-permute-start | bytes 2752520 | tf_op jit(solution)/shard_map/ppermute | solution.py:87
  477.6 28.4 %all-to-all-start.4 = ((bf16[4,2,64,1024]{3,2,1,0:T(8,128)(2,1)}), bf16[4,2,64,1024]{3,2,1,0:T(8,128)(2,1)S(1)}, u32[]{:S(2)}, u32[]{:S(2)}) async-start(bf16[4,2,64,1024]{3,2,1,0:T(8,128)(2,1)} %final_blocks.4), calls=%async_computation.4 | async-start | bytes 2097152 | tf_op jit(solution)/shard_map/all_to_all | solution.py:1231
  506.1 25.9 %all-to-all-start.5 = ((bf16[4,2,64,896]{3,2,1,0:T(8,128)(2,1)}), bf16[4,2,64,896]{3,2,1,0:T(8,128)(2,1)S(1)}, u32[]{:S(2)}, u32[]{:S(2)}) async-start(bf16[4,2,64,896]{3,2,1,0:T(8,128)(2,1)} %final_blocks.5), calls=%async_computation.5 | async-start | bytes 1835008 | tf_op jit(solution)/shard_map/all_to_all | solution.py:1231
  (85 other events, 977.0 us)
